TPU v7x, 512 devices: a whole 4x4x16 slice. The times are simulated.
512 devices in a mesh: rep: 8 (over x, z_hi), fsdp: 64 (over y, z_lo, core).
Axes of the slice: x: 4, y: 4, z: 16 (z_hi: 2, z_lo: 8; z = z_hi * 8 + z_lo), core: 2. Of those that a mesh axis runs over, the one named last changes fastest.
Arguments:
- tokens: bfloat16 [65536, 4096], P(('rep', 'fsdp')), may hold values from -6 to 6
- kv_weight: bfloat16 [8, 4096, 1024], P('rep', 'fsdp'), may hold values from -0.09375 to 0.09375
- kv_cotangent: bfloat16 [65536, 1024], P(('rep', 'fsdp')), may hold values from -6 to 6
- fragment_index: int32 [1], replicated, may hold values from 0 to 7
- anchor: float32 [8, 262144], P(None, 'fsdp'), may hold values from -6 to 6
- momentum: float32 [8, 262144], P(None, 'fsdp'), may hold values from -6 to 6
- replica_frag: bfloat16 [8, 8, 262144], P('rep', None, 'fsdp'), may hold values from -6 to 6
Outputs:
- key_value: bfloat16 [65536, 1024], P(('rep', 'fsdp'))
- input_grad: bfloat16 [65536, 4096], P(('rep', 'fsdp'))
- anchor_new: float32 [262144], P('fsdp')
- momentum_new: float32 [262144], P('fsdp')
All inputs are finite; a program needn't handle non-finite values.
Results may differ from a plain program's by a relative error of at most 0.0049.
Values may be sent and summed in bfloat16 or wider, within the bound.
No kernel may reach another device: no remote copies, remote signals or barrier semaphores. Data moves between devices by JAX's collectives and lax.ppermute only.
A program may use at most 64 MiB of HBM per device.

v0:
```python
import jax
import jax.numpy as jnp
from jax import lax
from jax.sharding import PartitionSpec as P

norm_eps = 1e-05
outer_momentum = 0.9
outer_rate = 0.7


def local(tokens, kv_weight, kv_cotangent, fragment_index, anchor, momentum, replica_frag):
    weight = kv_weight[0]
    rows_in = tokens.astype(jnp.float32)
    inv_rms = lax.rsqrt(jnp.mean(rows_in * rows_in, axis=1, keepdims=True) + norm_eps)
    normed = rows_in * inv_rms
    normed_bf = normed.astype(jnp.bfloat16)
    full_rows = lax.all_gather(weight, "fsdp", axis=0, tiled=True)
    key_value = jnp.dot(normed_bf, full_rows, preferred_element_type=jnp.float32)
    normed_grad = lax.dot_general(
        kv_cotangent, full_rows, (((1,), (1,)), ((), ())), preferred_element_type=jnp.float32
    )
    inner = jnp.mean(normed_grad * normed, axis=1, keepdims=True)
    input_grad = (inv_rms * (normed_grad - normed * inner)).astype(jnp.bfloat16)
    frag_pick = fragment_index[0]
    anchor_now = lax.dynamic_index_in_dim(anchor, frag_pick, 0, keepdims=False)
    moment_now = lax.dynamic_index_in_dim(momentum, frag_pick, 0, keepdims=False)
    replica_now = lax.dynamic_index_in_dim(replica_frag[0], frag_pick, 0, keepdims=False).astype(
        jnp.float32
    )
    replica_drift = anchor_now - replica_now
    replicas = lax.axis_size("rep")
    outer_grad = lax.psum(replica_drift, "rep") / replicas
    momentum_new = outer_momentum * moment_now + outer_grad
    anchor_new = anchor_now - outer_rate * (outer_grad + outer_momentum * momentum_new)
    return (key_value.astype(jnp.bfloat16), input_grad, anchor_new, momentum_new)


def solution(mesh):
    return jax.shard_map(
        local,
        mesh=mesh,
        in_specs=(
            P(("rep", "fsdp"), None),
            P("rep", "fsdp", None),
            P(("rep", "fsdp"), None),
            P(),
            P(None, "fsdp"),
            P(None, "fsdp"),
            P("rep", None, "fsdp"),
        ),
        out_specs=(P(("rep", "fsdp"), None), P(("rep", "fsdp"), None), P("fsdp"), P("fsdp")),
        check_vma=False,
    )
```

profile of v0, /device:TPU:1, one launch (start us, length us, event | category | flops | bytes accessed | tf_op | source)
XLA Modules:
  0.0 160.2 jit_solution(11142468776428612123)
XLA Ops:
  7.2 0.0 copy-start
  7.2 0.0 copy-start.2
  7.2 0.0 all-gather.3.cloned.1.call-start
  7.2 0.7 all-gather.3.cloned.1.call-update
  8.6 0.9 constant_dynamic-slice_fusion
  9.5 0.9 dynamic-slice_convert_fusion
  10.4 75.7 %psum.7 = f32[4096]{0:T(1024)S(1)} all-reduce(f32[4096]{0:T(1024)S(1)} %sub.10), channel_id=1, replica_groups=mesh['rep'=8,'fsdp'=64] {'rep'}, use_global_device_ids=true, to_apply=%region_2.3 | all-reduce | flops 4096 | bytes 32768 | tf_op jit(solution)/shard_map/psum | solution.py:32
  86.1 1.5 fusion.11
  87.6 0.9 dynamic-slice_multiply_fusion
  88.6 0.6 multiply_subtract_fusion
  89.2 54.2 %all-gather.3.cloned.1.call-done = bf16[1,4096,1024]{2,1,0:T(8,128)(2,1)} async-done(((bf16[1,64,1024]{2,1,0:T(8,128)(2,1)}), bf16[1,4096,1024]{2,1,0:T(8,128)(2,1)}) %all-gather.3.cloned.1.call-update) | async-done | bytes 8388624 | tf_op jit(solution)/shard_map/all_gather | solution.py:17
  143.4 0.0 copy-done
  143.4 0.0 copy-done.2
  143.4 0.0 copy-start.1
  143.4 6.5 %fusion.7 = (f32[128]{0:T(128)S(1)}, f32[128,4096]{1,0:T(8,128)S(1)}) fusion(bf16[128,4096]{1,0:T(8,128)(2,1)S(1)} %copy-done.2, f32[128]{0:T(128)S(1)} %add_rsqrt_fusion, bf16[128,1024]{1,0:T(8,128)(2,1)S(1)} %copy-done, bf16[1,4096,1024]{2,1,0:T(8,128)(2,1)} %all-gather.3.cloned.1.call-done), kind=kOutput, calls=%fused_computation.9 | convolution fusion | flops 1075838848 | bytes 11797504 | tf_op jit(solution)/shard_map/dot_general | solution.py:19
  149.9 1.5 fusion.10
  151.4 0.0 copy-done.1
  151.4 2.0 %fusion.12 = bf16[128,1024]{1,0:T(8,128)(2,1)} fusion(bf16[1,4096,1024]{2,1,0:T(8,128)(2,1)S(1)} %copy-done.1, bf16[128,4096]{1,0:T(8,128)(2,1)S(1)} %copy-done.2, f32[128]{0:T(128)S(1)} %add_rsqrt_fusion), kind=kOutput, calls=%fused_computation.14 | convolution fusion | flops 1075445760 | bytes 9699840 | tf_op jit(solution)/shard_map/dot_general | solution.py:18
  (3 shorter events, 0.0 us)
Async XLA Ops:
  7.2 136.2 %copy-start = (bf16[128,1024]{1,0:T(8,128)(2,1)S(1)}, bf16[128,1024]{1,0:T(8,128)(2,1)}, u32[]{:S(2)}) copy-start(bf16[128,1024]{1,0:T(8,128)(2,1)} %param.9) | copy-start | bytes 786436
  7.2 136.2 %copy-start.2 = (bf16[128,4096]{1,0:T(8,128)(2,1)S(1)}, bf16[128,4096]{1,0:T(8,128)(2,1)}, u32[]{:S(2)}) copy-start(bf16[128,4096]{1,0:T(8,128)(2,1)} %param.7) | copy-start | bytes 3145732
  7.2 136.2 %all-gather.3.cloned.1.call-start = ((), (), s32[]{:S(2)}) async-start(), calls=%async_computation | async-start | bytes 8519680 | tf_op jit(solution)/shard_map/all_gather | solution.py:17
  143.4 8.0 %copy-start.1 = (bf16[1,4096,1024]{2,1,0:T(8,128)(2,1)S(1)}, bf16[1,4096,1024]{2,1,0:T(8,128)(2,1)}, u32[]{:S(2)}) copy-start(bf16[1,4096,1024]{2,1,0:T(8,128)(2,1)} %all-gather.3.cloned.1.call-done) | copy-start | bytes 25165828
Sparse Core Ops, SparseCore 0:
  10.2 133.1 all-gather.2
where the time goes:
time: 160 us
  blocking collectives  75.7 us (47%)
  waiting for transfers between devices  54.9 us (34%)
  between operations  14.7 us (9%)
  matrix products  8.5 us (5%)
  other arithmetic  5.44 us (3%)
    psum x1, blocking collectives, local(): outer_grad = lax.psum(replica_drift, 'rep') / replicas  75.7 us
    all_gather x1, waiting for transfers between devices, local(): full_rows = lax.all_gather(weight, 'fsdp', axis=0, tiled=True)  54.2 us
    dot_general x1, matrix products, local(): lax.dot_general(kv_cotangent, full_rows, (((1,), (1,)), ((), ())), prefer...  6.49 us
  transfers between devices with their start and end apart: 1, of which 1 were waited for; matrix products, arithmetic and copies ran while one was open for 3% of the time, Pallas kernels for 0%

commit v1 on v0

v1 whole, which is shorter than its diff:
```python
import jax
import jax.numpy as jnp
from jax import lax
from jax.experimental import pallas as pl
from jax.experimental.pallas import tpu as pltpu
from jax.sharding import PartitionSpec as P

norm_eps = 1e-05
outer_momentum = 0.9
outer_rate = 0.7

NY, NZ, NC = 4, 8, 2
FIRST, SECOND = (0, 4, 2, 6), (1, 5, 3, 7)
MIB = 1 << 20


def device_pairs(move):
    pairs = []
    for y in range(NY):
        for z in range(NZ):
            for c in range(NC):
                to_y, to_z, to_c = move(y, z, c)
                pairs.append(((y * NZ + z) * NC + c, ((to_y % NY) * NZ + to_z) * NC + to_c))
    return pairs


def to_z(bit):
    return device_pairs(lambda y, z, c: (y, z ^ bit, c))


def to_y(step):
    return device_pairs(lambda y, z, c: (y + step, z, c))


to_core = device_pairs(lambda y, z, c: (y, z, 1 - c))


def send(x, pairs):
    return lax.ppermute(x, "fsdp", pairs)


def place():
    me = lax.axis_index("fsdp")
    return me // (NZ * NC), lax.rem(me // NC, NZ), lax.rem(me, NC)


def chip_columns(y, z, dy, dz):
    chip = lax.rem(y + (dy + NY), NY) * NZ + jnp.bitwise_xor(z, dz)
    return pl.ds(pl.multiple_of(chip * 128, 128), 128)


def project_kernel(tok_ref, cot_ref, tok_sib_ref, cot_sib_ref, *refs):
    pieces, (out_ref, sib_ref, inv_ref, kv_ref) = refs[:10], refs[10:]
    y, z, c = place()
    rows = tok_ref.shape[0]
    half = lax.broadcasted_iota(jnp.int32, (rows, 128), 1) < 64
    invs = []
    for ref in (tok_ref, tok_sib_ref):
        x = ref[...].astype(jnp.float32)
        invs.append(lax.rsqrt(jnp.mean(x * x, axis=1, keepdims=True) + norm_eps))
    inv_ref[...] = invs[0]
    cot = jnp.concatenate([cot_ref[...], cot_sib_ref[...]], axis=0)
    low = c == 0
    plan = []
    for g in range(2):
        own, left, right, f, s = pieces[5 * g : 5 * g + 5]
        order = (FIRST, SECOND)[g]
        plan += [(0, order, (own,)), (-1, order, (left,)), (1, order, (right,)), (2, order, (f, s))]
    for n, (dy, order, group) in enumerate(plan):
        weight = group[0][...] if len(group) == 1 else jnp.concatenate([group[0][...], group[1][...]], axis=0)
        lhs = []
        for ref, inv in zip((tok_ref, tok_sib_ref), invs):
            cols = []
            for i in (0, 2):
                p = ref[:, chip_columns(y, z, dy, order[i])].astype(jnp.float32) * inv
                q = ref[:, chip_columns(y, z, dy, order[i + 1])].astype(jnp.float32) * inv
                lo = jnp.where(half, p, pltpu.roll(q, 64, 1))
                hi = jnp.where(half, pltpu.roll(p, 64, 1), q)
                cols.append(jnp.where(low, lo, hi).astype(jnp.bfloat16))
            lhs.append(jnp.concatenate(cols, axis=1))
        part = jnp.dot(jnp.concatenate(lhs, axis=0), weight, preferred_element_type=jnp.float32)
        if n == 0:
            kv_ref[...] = part
        else:
            kv_ref[...] += part
        grad = lax.dot_general(cot, weight, (((1,), (1,)), ((), ())), preferred_element_type=jnp.float32)
        out_ref[:, 1024 + 256 * n : 1024 + 256 * (n + 1)] = grad[:rows]
        sib_ref[:, 1024 + 256 * n : 1024 + 256 * (n + 1)] = grad[rows:].astype(jnp.bfloat16)
    out_ref[:, :1024] = kv_ref[:rows]
    sib_ref[:, :1024] = kv_ref[rows:].astype(jnp.bfloat16)


def finish_kernel(tok_ref, inv_ref, own_ref, got_ref, kv_ref, grad_ref, full_ref):
    y, z, c = place()
    rows = tok_ref.shape[0]
    half = lax.broadcasted_iota(jnp.int32, (rows, 128), 1) < 64
    low = c == 0
    inv = inv_ref[...]
    kv_ref[...] = (own_ref[:, :1024] + got_ref[:, :1024].astype(jnp.float32)).astype(jnp.bfloat16)
    total = jnp.zeros((rows, 128), jnp.float32)
    n = 0
    for order in (FIRST, SECOND):
        for dy in (0, -1, 1, 2):
            for i in (0, 2):
                at = 1024 + 256 * n + 64 * i
                mine = own_ref[:, at : at + 128]
                other = got_ref[:, at : at + 128].astype(jnp.float32)
                zero = jnp.where(low, mine, other)
                one = jnp.where(low, other, mine)
                for k, whole in (
                    (0, jnp.where(half, zero, pltpu.roll(one, 64, 1))),
                    (1, jnp.where(half, pltpu.roll(zero, 64, 1), one)),
                ):
                    cols = chip_columns(y, z, dy, order[i + k])
                    full_ref[:, cols] = whole
                    total += whole * (tok_ref[:, cols].astype(jnp.float32) * inv)
            n += 1
    inner = jnp.sum(total, axis=1, keepdims=True) / tok_ref.shape[1]
    normed = tok_ref[...].astype(jnp.float32) * inv
    grad_ref[...] = (inv * (full_ref[...] - normed * inner)).astype(jnp.bfloat16)


def gather_pieces(shard):
    pair = jnp.concatenate([shard, send(shard, to_z(4))], axis=0)
    first = jnp.concatenate([pair, send(pair, to_z(2))], axis=0)
    second = send(first, to_z(1))
    pieces = []
    for own in (first, second):
        h = own.shape[0] // 2
        left = send(own, to_y(1))
        right = send(own, to_y(-1))
        pieces += [own, left, right, send(left[:h], to_y(1)), send(right[h:], to_y(-1))]
    return pieces


def local(tokens, kv_weight, kv_cotangent, fragment_index, anchor, momentum, replica_frag):
    rows, width = tokens.shape
    tok_sib = send(tokens, to_core)
    cot_sib = send(kv_cotangent, to_core)
    pieces = gather_pieces(kv_weight[0])
    params = pltpu.CompilerParams(vmem_limit_bytes=40 * MIB)
    own, for_sib, inv = pl.pallas_call(
        project_kernel,
        out_shape=(
            jax.ShapeDtypeStruct((rows, 1024 + width // 2), jnp.float32),
            jax.ShapeDtypeStruct((rows, 1024 + width // 2), jnp.bfloat16),
            jax.ShapeDtypeStruct((rows, 1), jnp.float32),
        ),
        scratch_shapes=[pltpu.VMEM((2 * rows, 1024), jnp.float32)],
        compiler_params=params,
        cost_estimate=pl.CostEstimate(flops=2**31, bytes_accessed=8 * MIB, transcendentals=256),
        name="project",
    )(tokens, kv_cotangent, tok_sib, cot_sib, *pieces)
    got = send(for_sib, to_core)
    key_value, input_grad = pl.pallas_call(
        finish_kernel,
        out_shape=(
            jax.ShapeDtypeStruct((rows, 1024), jnp.bfloat16),
            jax.ShapeDtypeStruct((rows, width), jnp.bfloat16),
        ),
        scratch_shapes=[pltpu.VMEM((rows, width), jnp.float32)],
        compiler_params=params,
        cost_estimate=pl.CostEstimate(flops=2**22, bytes_accessed=5 * MIB, transcendentals=0),
        name="finish",
    )(tokens, inv, own, got)

    frag_pick = fragment_index[0]
    anchor_now = lax.dynamic_index_in_dim(anchor, frag_pick, 0, keepdims=False)
    moment_now = lax.dynamic_index_in_dim(momentum, frag_pick, 0, keepdims=False)
    replica_now = lax.dynamic_index_in_dim(replica_frag[0], frag_pick, 0, keepdims=False).astype(
        jnp.float32
    )
    replicas = lax.axis_size("rep")
    drift = anchor_now - replica_now
    for bit in (1, 2, 4):
        drift = drift + lax.ppermute(drift, "rep", [(r, r ^ bit) for r in range(replicas)])
    outer_grad = drift / replicas
    momentum_new = outer_momentum * moment_now + outer_grad
    anchor_new = anchor_now - outer_rate * (outer_grad + outer_momentum * momentum_new)
    return key_value, input_grad, anchor_new, momentum_new


def solution(mesh):
    return jax.shard_map(
        local,
        mesh=mesh,
        in_specs=(
            P(("rep", "fsdp"), None),
            P("rep", "fsdp", None),
            P(("rep", "fsdp"), None),
            P(),
            P(None, "fsdp"),
            P(None, "fsdp"),
            P("rep", None, "fsdp"),
        ),
        out_specs=(P(("rep", "fsdp"), None), P(("rep", "fsdp"), None), P("fsdp"), P("fsdp")),
        check_vma=False,
    )
```

time: 160 us -> 128 us (0.80)
  the two profiles are of different devices: /device:TPU:1 before, /device:TPU:30 now
where the time goes in v1:
time: 128 us; the launch traced here: 127 us
  starting transfers between devices  61.7 us (48%)
  waiting for transfers between devices  51.2 us (40%)
  Pallas kernels  7.23 us (6%)
  other arithmetic  4.28 us (3%)
  between operations  1.57 us (1%)
    ppermute x14, waiting for transfers between devices, send(): return lax.ppermute(x, 'fsdp', pairs)  43.7 us
    ppermute x14, starting transfers between devices, send(): return lax.ppermute(x, 'fsdp', pairs)  42 us
    ppermute x3, starting transfers between devices, local(): lax.ppermute(drift, 'rep', [(r, r ^ bit) for r in range(replicas)])  19.7 us
    ppermute x3, waiting for transfers between devices, local(): lax.ppermute(drift, 'rep', [(r, r ^ bit) for r in range(replicas)])  7.48 us
    pallas_call x1, Pallas kernels, local(): pl.pallas_call(project_kernel, out_shape=(jax.ShapeDtypeStruct((rows, 102...  4.69 us
  transfers between devices with their start and end apart: 17, of which 11 were waited for; matrix products, arithmetic and copies ran while one was open for 3% of the time, Pallas kernels for 0%

profile of v1, /device:TPU:30, one launch (start us, length us, event | category | flops | bytes accessed | tf_op | source)
XLA Modules:
  0.0 127.1 jit_solution(13045494171875661911)
XLA Ops:
  0.6 0.0 copy-start
  0.6 0.0 copy-start.1
  0.7 0.0 copy-start.2
  0.7 9.2 %collective-permute-start.2 = (bf16[64,1024]{1,0:T(8,128)(2,1)}, bf16[64,1024]{1,0:T(8,128)(2,1)S(1)}, u32[]{:S(2)}, u32[]{:S(2)}) collective-permute-start(bf16[64,1024]{1,0:T(8,128)(2,1)} %bitcast.8), channel_id=1, source_target_pairs={{0,8},{1,9},{2,10},{3,11},{4,12},{5,13},{6,14},{7,15},{8,0},{9,1},... | collective-permute-start | bytes 393224 | tf_op jit(solution)/shard_map/ppermute | solution.py:39
  9.9 12.1 %collective-permute-done.2 = bf16[64,1024]{1,0:T(8,128)(2,1)S(1)} collective-permute-done((bf16[64,1024]{1,0:T(8,128)(2,1)}, bf16[64,1024]{1,0:T(8,128)(2,1)S(1)}, u32[]{:S(2)}, u32[]{:S(2)}) %collective-permute-start.2) | collective-permute-done | bytes 131104 | tf_op jit(solution)/shard_map/ppermute | solution.py:39
  22.0 0.9 pad_maximum_fusion.1
  22.9 1.9 %collective-permute-start.3 = (bf16[128,1024]{1,0:T(8,128)(2,1)S(1)}, bf16[128,1024]{1,0:T(8,128)(2,1)S(1)}, u32[]{:S(2)}, u32[]{:S(2)}) collective-permute-start(bf16[128,1024]{1,0:T(8,128)(2,1)S(1)} %pad_maximum_fusion.1), channel_id=1, source_target_pairs={{0,4},{1,5},{2,6},{3,7},{4,0},{5,1},{6,2},{7,3},{8,12},{9,13},{10,... | collective-permute-start | bytes 786440 | tf_op jit(solution)/shard_map/ppermute | solution.py:39
  24.9 14.0 %collective-permute-done.3 = bf16[128,1024]{1,0:T(8,128)(2,1)S(1)} collective-permute-done((bf16[128,1024]{1,0:T(8,128)(2,1)S(1)}, bf16[128,1024]{1,0:T(8,128)(2,1)S(1)}, u32[]{:S(2)}, u32[]{:S(2)}) %collective-permute-start.3) | collective-permute-done | bytes 262176 | tf_op jit(solution)/shard_map/ppermute | solution.py:39
  38.9 0.9 pad_maximum_fusion.refs_0_
  39.8 1.9 %collective-permute-start.8 = (bf16[256,1024]{1,0:T(8,128)(2,1)S(1)}, bf16[256,1024]{1,0:T(8,128)(2,1)}, u32[]{:S(2)}, u32[]{:S(2)}) collective-permute-start(bf16[256,1024]{1,0:T(8,128)(2,1)S(1)} %pad_maximum_fusion.refs_0_), channel_id=1, source_target_pairs={{0,2},{1,3},{2,0},{3,1},{4,6},{5,7},{6,4},{7,5},{8,10},{9,11},{10,... | collective-permute-start | bytes 1572872 | tf_op jit(solution)/shard_map/ppermute | solution.py:39
  41.7 2.1 %collective-permute-start.4 = (bf16[256,1024]{1,0:T(8,128)(2,1)S(1)}, bf16[256,1024]{1,0:T(8,128)(2,1)S(1)}, u32[]{:S(2)}, u32[]{:S(2)}) collective-permute-start(bf16[256,1024]{1,0:T(8,128)(2,1)S(1)} %pad_maximum_fusion.refs_0_), channel_id=1, source_target_pairs={{0,16},{1,17},{2,18},{3,19},{4,20},{5,21},{6,22},{7,23},{8,24},{9,... | collective-permute-start | bytes 1572872 | tf_op jit(solution)/shard_map/ppermute | solution.py:39
  43.9 0.0 copy-done.1
  43.9 1.9 %collective-permute-start = (bf16[128,4096]{1,0:T(8,128)(2,1)S(1)}, bf16[128,4096]{1,0:T(8,128)(2,1)}, u32[]{:S(2)}, u32[]{:S(2)}) collective-permute-start(bf16[128,4096]{1,0:T(8,128)(2,1)S(1)} %copy-done.1), channel_id=1, source_target_pairs={{0,1},{1,0},{2,3},{3,2},{4,5},{5,4},{6,7},{7,6},{8,9},{9,8},{10,11... | collective-permute-start | bytes 3145736 | tf_op jit(solution)/shard_map/ppermute | solution.py:39
  45.8 3.7 %collective-permute-start.5 = (bf16[256,1024]{1,0:T(8,128)(2,1)S(1)}, bf16[256,1024]{1,0:T(8,128)(2,1)S(1)}, u32[]{:S(2)}, u32[]{:S(2)}) collective-permute-start(bf16[256,1024]{1,0:T(8,128)(2,1)S(1)} %pad_maximum_fusion.refs_0_), channel_id=1, source_target_pairs={{0,48},{1,49},{2,50},{3,51},{4,52},{5,53},{6,54},{7,55},{8,56},{9,... | collective-permute-start | bytes 1572872 | tf_op jit(solution)/shard_map/ppermute | solution.py:39
  49.5 5.3 %collective-permute-done.8.refs_5_ = bf16[256,1024]{1,0:T(8,128)(2,1)} collective-permute-done((bf16[256,1024]{1,0:T(8,128)(2,1)S(1)}, bf16[256,1024]{1,0:T(8,128)(2,1)}, u32[]{:S(2)}, u32[]{:S(2)}) %collective-permute-start.8) | collective-permute-done | bytes 524320 | tf_op jit(solution)/shard_map/ppermute | solution.py:39
  54.8 2.1 %collective-permute-start.9 = (bf16[256,1024]{1,0:T(8,128)(2,1)}, bf16[256,1024]{1,0:T(8,128)(2,1)S(1)}, u32[]{:S(2)}, u32[]{:S(2)}) collective-permute-start(bf16[256,1024]{1,0:T(8,128)(2,1)} %collective-permute-done.8.refs_5_), channel_id=1, source_target_pairs={{0,16},{1,17},{2,18},{3,19},{4,20},{5,21},{6,22},{7,23},{8,24},{9,... | collective-permute-start | bytes 1572872 | tf_op jit(solution)/shard_map/ppermute | solution.py:39
  57.0 3.7 %collective-permute-start.10 = (bf16[256,1024]{1,0:T(8,128)(2,1)}, bf16[256,1024]{1,0:T(8,128)(2,1)}, u32[]{:S(2)}, u32[]{:S(2)}) collective-permute-start(bf16[256,1024]{1,0:T(8,128)(2,1)} %collective-permute-done.8.refs_5_), channel_id=1, source_target_pairs={{0,48},{1,49},{2,50},{3,51},{4,52},{5,53},{6,54},{7,55},{8,56},{9,... | collective-permute-start | bytes 1572872 | tf_op jit(solution)/shard_map/ppermute | solution.py:39
  60.7 0.0 collective-permute-done.4.refs_1_
  60.7 0.0 copy-done.2
  60.7 1.9 %collective-permute-start.1 = (bf16[128,1024]{1,0:T(8,128)(2,1)S(1)}, bf16[128,1024]{1,0:T(8,128)(2,1)}, u32[]{:S(2)}, u32[]{:S(2)}) collective-permute-start(bf16[128,1024]{1,0:T(8,128)(2,1)S(1)} %copy-done.2), channel_id=1, source_target_pairs={{0,1},{1,0},{2,3},{3,2},{4,5},{5,4},{6,7},{7,6},{8,9},{9,8},{10,11... | collective-permute-start | bytes 786440 | tf_op jit(solution)/shard_map/ppermute | solution.py:39
  63.3 0.3 collective-permute-done.5.refs_2_
  63.6 3.0 %collective-permute-start.6 = (bf16[128,1024]{1,0:T(8,128)(2,1)S(1)}, bf16[128,1024]{1,0:T(8,128)(2,1)S(1)}, u32[]{:S(2)}, u32[]{:S(2)}) collective-permute-start(bf16[128,1024]{1,0:T(8,128)(2,1)S(1)} %slice.16), channel_id=1, source_target_pairs={{0,16},{1,17},{2,18},{3,19},{4,20},{5,21},{6,22},{7,23},{8,24},{9,... | collective-permute-start | bytes 786440 | tf_op jit(solution)/shard_map/ppermute | solution.py:39
  66.7 3.0 %collective-permute-done.9.refs_6_ = bf16[256,1024]{1,0:T(8,128)(2,1)S(1)} collective-permute-done((bf16[256,1024]{1,0:T(8,128)(2,1)}, bf16[256,1024]{1,0:T(8,128)(2,1)S(1)}, u32[]{:S(2)}, u32[]{:S(2)}) %collective-permute-start.9) | collective-permute-done | bytes 524320 | tf_op jit(solution)/shard_map/ppermute | solution.py:39
  69.8 2.6 %collective-permute-start.7 = (bf16[128,1024]{1,0:T(8,128)(2,1)S(1)}, bf16[128,1024]{1,0:T(8,128)(2,1)S(1)}, u32[]{:S(2)}, u32[]{:S(2)}) collective-permute-start(bf16[128,1024]{1,0:T(8,128)(2,1)S(1)} %slice.17), channel_id=1, source_target_pairs={{0,48},{1,49},{2,50},{3,51},{4,52},{5,53},{6,54},{7,55},{8,56},{9,... | collective-permute-start | bytes 786440 | tf_op jit(solution)/shard_map/ppermute | solution.py:39
  72.4 2.8 %collective-permute-done.10.refs_7_ = bf16[256,1024]{1,0:T(8,128)(2,1)} collective-permute-done((bf16[256,1024]{1,0:T(8,128)(2,1)}, bf16[256,1024]{1,0:T(8,128)(2,1)}, u32[]{:S(2)}, u32[]{:S(2)}) %collective-permute-start.10) | collective-permute-done | bytes 524320 | tf_op jit(solution)/shard_map/ppermute | solution.py:39
  75.3 2.3 %collective-permute-start.11 = (bf16[128,1024]{1,0:T(8,128)(2,1)S(1)}, bf16[128,1024]{1,0:T(8,128)(2,1)S(1)}, u32[]{:S(2)}, u32[]{:S(2)}) collective-permute-start(bf16[128,1024]{1,0:T(8,128)(2,1)S(1)} %slice.18), channel_id=1, source_target_pairs={{0,16},{1,17},{2,18},{3,19},{4,20},{5,21},{6,22},{7,23},{8,24},{9,... | collective-permute-start | bytes 786440 | tf_op jit(solution)/shard_map/ppermute | solution.py:39
  77.5 1.0 slice.19
  78.5 0.0 collective-permute-done.1.cot_sib_ref
  78.5 3.6 %collective-permute-start.12 = (bf16[128,1024]{1,0:T(8,128)(2,1)S(1)}, bf16[128,1024]{1,0:T(8,128)(2,1)S(1)}, u32[]{:S(2)}, u32[]{:S(2)}) collective-permute-start(bf16[128,1024]{1,0:T(8,128)(2,1)S(1)} %slice.19), channel_id=1, source_target_pairs={{0,48},{1,49},{2,50},{3,51},{4,52},{5,53},{6,54},{7,55},{8,56},{9,... | collective-permute-start | bytes 786440 | tf_op jit(solution)/shard_map/ppermute | solution.py:39
  82.1 0.0 copy-done
  82.1 0.0 collective-permute-done.tok_sib_ref
  82.1 0.0 collective-permute-done.6.refs_3_
  82.1 0.0 collective-permute-done.7.refs_4_
  82.2 1.9 %collective-permute-done.11.refs_8_ = bf16[128,1024]{1,0:T(8,128)(2,1)S(1)} collective-permute-done((bf16[128,1024]{1,0:T(8,128)(2,1)S(1)}, bf16[128,1024]{1,0:T(8,128)(2,1)S(1)}, u32[]{:S(2)}, u32[]{:S(2)}) %collective-permute-start.11) | collective-permute-done | bytes 262176 | tf_op jit(solution)/shard_map/ppermute | solution.py:39
  84.1 4.2 %collective-permute-done.12.refs_9_ = bf16[128,1024]{1,0:T(8,128)(2,1)S(1)} collective-permute-done((bf16[128,1024]{1,0:T(8,128)(2,1)S(1)}, bf16[128,1024]{1,0:T(8,128)(2,1)S(1)}, u32[]{:S(2)}, u32[]{:S(2)}) %collective-permute-start.12) | collective-permute-done | bytes 262176 | tf_op jit(solution)/shard_map/ppermute | solution.py:39
  88.3 4.7 %project.1 = (f32[128,3072]{1,0:T(8,128)S(1)}, bf16[128,3072]{1,0:T(8,128)(2,1)S(1)}, f32[128,1]{1,0:T(8,128)S(1)}) custom-call(bf16[128,4096]{1,0:T(8,128)(2,1)S(1)} %copy-done.1, bf16[128,1024]{1,0:T(8,128)(2,1)S(1)} %copy-done.2, bf16[128,4096]{1,0:T(8,128)(2,1)} %collective-permute-done.tok_sib_ref, ...), custom_call_target="tpu_custom_call" | custom-call | flops 2147483648 | bytes 8388608 | tf_op jit(solution)/shard_map/project/pallas_call | solution.py:142
  93.0 1.9 %collective-permute-start.13 = (bf16[128,3072]{1,0:T(8,128)(2,1)S(1)}, bf16[128,3072]{1,0:T(8,128)(2,1)S(1)}, u32[]{:S(2)}, u32[]{:S(2)}) collective-permute-start(bf16[128,3072]{1,0:T(8,128)(2,1)S(1)} %get-tuple-element.11), channel_id=1, source_target_pairs={{0,1},{1,0},{2,3},{3,2},{4,5},{5,4},{6,7},{7,6},{8,9},{9,8},{10,11... | collective-permute-start | bytes 2359304 | tf_op jit(solution)/shard_map/ppermute | solution.py:39
  94.9 0.9 dynamic-slice_convert_fusion
  95.8 13.7 %collective-permute-start.14 = (f32[4096]{0:T(1024)S(1)}, f32[4096]{0:T(1024)S(1)}, u32[]{:S(2)}, u32[]{:S(2)}) collective-permute-start(f32[4096]{0:T(1024)S(1)} %sub.6), channel_id=1, source_target_pairs={{0,64},{64,0},{128,192},{192,128},{256,320},{320,256},{384,448},{4... | collective-permute-start | bytes 49160 | tf_op jit(solution)/shard_map/ppermute | solution.py:176
  109.5 1.7 %collective-permute-done.14 = f32[4096]{0:T(1024)S(1)} collective-permute-done((f32[4096]{0:T(1024)S(1)}, f32[4096]{0:T(1024)S(1)}, u32[]{:S(2)}, u32[]{:S(2)}) %collective-permute-start.14) | collective-permute-done | bytes 16416 | tf_op jit(solution)/shard_map/ppermute | solution.py:176
  111.2 2.7 %collective-permute-start.15 = (f32[4096]{0:T(1024)S(1)}, f32[4096]{0:T(1024)S(1)}, u32[]{:S(2)}, u32[]{:S(2)}) collective-permute-start(f32[4096]{0:T(1024)S(1)} %add.23), channel_id=1, source_target_pairs={{0,128},{64,192},{128,0},{192,64},{256,384},{320,448},{384,256},{4... | collective-permute-start | bytes 49160 | tf_op jit(solution)/shard_map/ppermute | solution.py:176
  113.9 2.9 %collective-permute-done.15 = f32[4096]{0:T(1024)S(1)} collective-permute-done((f32[4096]{0:T(1024)S(1)}, f32[4096]{0:T(1024)S(1)}, u32[]{:S(2)}, u32[]{:S(2)}) %collective-permute-start.15) | collective-permute-done | bytes 16416 | tf_op jit(solution)/shard_map/ppermute | solution.py:176
  116.8 3.3 %collective-permute-start.16 = (f32[4096]{0:T(1024)S(1)}, f32[4096]{0:T(1024)S(1)}, u32[]{:S(2)}, u32[]{:S(2)}) collective-permute-start(f32[4096]{0:T(1024)S(1)} %add.24), channel_id=1, source_target_pairs={{0,256},{64,320},{128,384},{192,448},{256,0},{320,64},{384,128},{4... | collective-permute-start | bytes 49160 | tf_op jit(solution)/shard_map/ppermute | solution.py:176
  120.1 0.9 dynamic-slice_multiply_fusion
  121.0 2.9 %collective-permute-done.16 = f32[4096]{0:T(1024)S(1)} collective-permute-done((f32[4096]{0:T(1024)S(1)}, f32[4096]{0:T(1024)S(1)}, u32[]{:S(2)}, u32[]{:S(2)}) %collective-permute-start.16) | collective-permute-done | bytes 16416 | tf_op jit(solution)/shard_map/ppermute | solution.py:176
  123.9 0.6 multiply_subtract_fusion
  124.6 0.0 collective-permute-done.13.got_ref
  124.6 2.5 %finish.1 = (bf16[128,1024]{1,0:T(8,128)(2,1)}, bf16[128,4096]{1,0:T(8,128)(2,1)}) custom-call(bf16[128,4096]{1,0:T(8,128)(2,1)S(1)} %copy-done.1, f32[128,1]{1,0:T(8,128)S(1)} %get-tuple-element.9.inv_ref, f32[128,3072]{1,0:T(8,128)S(1)} %get-tuple-element.10.own_ref, bf16[128,3072]{1,0:T(8,128)(2,1)S(1)} %collective-permute-done.13.got_ref), custom_call_target="tpu_custom_call" | custom-call | flops 4194304 | bytes 5242880 | tf_op jit(solution)/shard_map/finish/pallas_call | solution.py:155
  (7 shorter events, 0.1 us)
Async XLA Ops:
  0.6 81.5 %copy-start = (f32[8,4096]{1,0:T(8,128)S(1)}, f32[8,4096]{1,0:T(8,128)}, u32[]{:S(2)}) copy-start(f32[8,4096]{1,0:T(8,128)} %param.11) | copy-start | bytes 393220
  0.6 43.2 %copy-start.1 = (bf16[128,4096]{1,0:T(8,128)(2,1)S(1)}, bf16[128,4096]{1,0:T(8,128)(2,1)}, u32[]{:S(2)}) copy-start(bf16[128,4096]{1,0:T(8,128)(2,1)} %tok_ref.3) | copy-start | bytes 3145732
  0.7 60.1 %copy-start.2 = (bf16[128,1024]{1,0:T(8,128)(2,1)S(1)}, bf16[128,1024]{1,0:T(8,128)(2,1)}, u32[]{:S(2)}) copy-start(bf16[128,1024]{1,0:T(8,128)(2,1)} %cot_ref.1) | copy-start | bytes 786436
  0.7 21.4 %collective-permute-start.2 = (bf16[64,1024]{1,0:T(8,128)(2,1)}, bf16[64,1024]{1,0:T(8,128)(2,1)S(1)}, u32[]{:S(2)}, u32[]{:S(2)}) collective-permute-start(bf16[64,1024]{1,0:T(8,128)(2,1)} %bitcast.8), channel_id=1, source_target_pairs={{0,8},{1,9},{2,10},{3,11},{4,12},{5,13},{6,14},{7,15},{8,0},{9,1},... | collective-permute-start | bytes 393224 | tf_op jit(solution)/shard_map/ppermute | solution.py:39
  22.9 15.9 %collective-permute-start.3 = (bf16[128,1024]{1,0:T(8,128)(2,1)S(1)}, bf16[128,1024]{1,0:T(8,128)(2,1)S(1)}, u32[]{:S(2)}, u32[]{:S(2)}) collective-permute-start(bf16[128,1024]{1,0:T(8,128)(2,1)S(1)} %pad_maximum_fusion.1), channel_id=1, source_target_pairs={{0,4},{1,5},{2,6},{3,7},{4,0},{5,1},{6,2},{7,3},{8,12},{9,13},{10,... | collective-permute-start | bytes 786440 | tf_op jit(solution)/shard_map/ppermute | solution.py:39
  39.8 15.1 %collective-permute-start.8 = (bf16[256,1024]{1,0:T(8,128)(2,1)S(1)}, bf16[256,1024]{1,0:T(8,128)(2,1)}, u32[]{:S(2)}, u32[]{:S(2)}) collective-permute-start(bf16[256,1024]{1,0:T(8,128)(2,1)S(1)} %pad_maximum_fusion.refs_0_), channel_id=1, source_target_pairs={{0,2},{1,3},{2,0},{3,1},{4,6},{5,7},{6,4},{7,5},{8,10},{9,11},{10,... | collective-permute-start | bytes 1572872 | tf_op jit(solution)/shard_map/ppermute | solution.py:39
  41.7 19.0 %collective-permute-start.4 = (bf16[256,1024]{1,0:T(8,128)(2,1)S(1)}, bf16[256,1024]{1,0:T(8,128)(2,1)S(1)}, u32[]{:S(2)}, u32[]{:S(2)}) collective-permute-start(bf16[256,1024]{1,0:T(8,128)(2,1)S(1)} %pad_maximum_fusion.refs_0_), channel_id=1, source_target_pairs={{0,16},{1,17},{2,18},{3,19},{4,20},{5,21},{6,22},{7,23},{8,24},{9,... | collective-permute-start | bytes 1572872 | tf_op jit(solution)/shard_map/ppermute | solution.py:39
  43.9 38.3 %collective-permute-start = (bf16[128,4096]{1,0:T(8,128)(2,1)S(1)}, bf16[128,4096]{1,0:T(8,128)(2,1)}, u32[]{:S(2)}, u32[]{:S(2)}) collective-permute-start(bf16[128,4096]{1,0:T(8,128)(2,1)S(1)} %copy-done.1), channel_id=1, source_target_pairs={{0,1},{1,0},{2,3},{3,2},{4,5},{5,4},{6,7},{7,6},{8,9},{9,8},{10,11... | collective-permute-start | bytes 3145736 | tf_op jit(solution)/shard_map/ppermute | solution.py:39
  45.8 17.8 %collective-permute-start.5 = (bf16[256,1024]{1,0:T(8,128)(2,1)S(1)}, bf16[256,1024]{1,0:T(8,128)(2,1)S(1)}, u32[]{:S(2)}, u32[]{:S(2)}) collective-permute-start(bf16[256,1024]{1,0:T(8,128)(2,1)S(1)} %pad_maximum_fusion.refs_0_), channel_id=1, source_target_pairs={{0,48},{1,49},{2,50},{3,51},{4,52},{5,53},{6,54},{7,55},{8,56},{9,... | collective-permute-start | bytes 1572872 | tf_op jit(solution)/shard_map/ppermute | solution.py:39
  54.8 14.9 %collective-permute-start.9 = (bf16[256,1024]{1,0:T(8,128)(2,1)}, bf16[256,1024]{1,0:T(8,128)(2,1)S(1)}, u32[]{:S(2)}, u32[]{:S(2)}) collective-permute-start(bf16[256,1024]{1,0:T(8,128)(2,1)} %collective-permute-done.8.refs_5_), channel_id=1, source_target_pairs={{0,16},{1,17},{2,18},{3,19},{4,20},{5,21},{6,22},{7,23},{8,24},{9,... | collective-permute-start | bytes 1572872 | tf_op jit(solution)/shard_map/ppermute | solution.py:39
  57.0 18.3 %collective-permute-start.10 = (bf16[256,1024]{1,0:T(8,128)(2,1)}, bf16[256,1024]{1,0:T(8,128)(2,1)}, u32[]{:S(2)}, u32[]{:S(2)}) collective-permute-start(bf16[256,1024]{1,0:T(8,128)(2,1)} %collective-permute-done.8.refs_5_), channel_id=1, source_target_pairs={{0,48},{1,49},{2,50},{3,51},{4,52},{5,53},{6,54},{7,55},{8,56},{9,... | collective-permute-start | bytes 1572872 | tf_op jit(solution)/shard_map/ppermute | solution.py:39
  60.7 17.8 %collective-permute-start.1 = (bf16[128,1024]{1,0:T(8,128)(2,1)S(1)}, bf16[128,1024]{1,0:T(8,128)(2,1)}, u32[]{:S(2)}, u32[]{:S(2)}) collective-permute-start(bf16[128,1024]{1,0:T(8,128)(2,1)S(1)} %copy-done.2), channel_id=1, source_target_pairs={{0,1},{1,0},{2,3},{3,2},{4,5},{5,4},{6,7},{7,6},{8,9},{9,8},{10,11... | collective-permute-start | bytes 786440 | tf_op jit(solution)/shard_map/ppermute | solution.py:39
  63.6 18.5 %collective-permute-start.6 = (bf16[128,1024]{1,0:T(8,128)(2,1)S(1)}, bf16[128,1024]{1,0:T(8,128)(2,1)S(1)}, u32[]{:S(2)}, u32[]{:S(2)}) collective-permute-start(bf16[128,1024]{1,0:T(8,128)(2,1)S(1)} %slice.16), channel_id=1, source_target_pairs={{0,16},{1,17},{2,18},{3,19},{4,20},{5,21},{6,22},{7,23},{8,24},{9,... | collective-permute-start | bytes 786440 | tf_op jit(solution)/shard_map/ppermute | solution.py:39
  69.8 12.4 %collective-permute-start.7 = (bf16[128,1024]{1,0:T(8,128)(2,1)S(1)}, bf16[128,1024]{1,0:T(8,128)(2,1)S(1)}, u32[]{:S(2)}, u32[]{:S(2)}) collective-permute-start(bf16[128,1024]{1,0:T(8,128)(2,1)S(1)} %slice.17), channel_id=1, source_target_pairs={{0,48},{1,49},{2,50},{3,51},{4,52},{5,53},{6,54},{7,55},{8,56},{9,... | collective-permute-start | bytes 786440 | tf_op jit(solution)/shard_map/ppermute | solution.py:39
  75.3 8.8 %collective-permute-start.11 = (bf16[128,1024]{1,0:T(8,128)(2,1)S(1)}, bf16[128,1024]{1,0:T(8,128)(2,1)S(1)}, u32[]{:S(2)}, u32[]{:S(2)}) collective-permute-start(bf16[128,1024]{1,0:T(8,128)(2,1)S(1)} %slice.18), channel_id=1, source_target_pairs={{0,16},{1,17},{2,18},{3,19},{4,20},{5,21},{6,22},{7,23},{8,24},{9,... | collective-permute-start | bytes 786440 | tf_op jit(solution)/shard_map/ppermute | solution.py:39
  78.5 9.8 %collective-permute-start.12 = (bf16[128,1024]{1,0:T(8,128)(2,1)S(1)}, bf16[128,1024]{1,0:T(8,128)(2,1)S(1)}, u32[]{:S(2)}, u32[]{:S(2)}) collective-permute-start(bf16[128,1024]{1,0:T(8,128)(2,1)S(1)} %slice.19), channel_id=1, source_target_pairs={{0,48},{1,49},{2,50},{3,51},{4,52},{5,53},{6,54},{7,55},{8,56},{9,... | collective-permute-start | bytes 786440 | tf_op jit(solution)/shard_map/ppermute | solution.py:39
  93.0 31.6 %collective-permute-start.13 = (bf16[128,3072]{1,0:T(8,128)(2,1)S(1)}, bf16[128,3072]{1,0:T(8,128)(2,1)S(1)}, u32[]{:S(2)}, u32[]{:S(2)}) collective-permute-start(bf16[128,3072]{1,0:T(8,128)(2,1)S(1)} %get-tuple-element.11), channel_id=1, source_target_pairs={{0,1},{1,0},{2,3},{3,2},{4,5},{5,4},{6,7},{7,6},{8,9},{9,8},{10,11... | collective-permute-start | bytes 2359304 | tf_op jit(solution)/shard_map/ppermute | solution.py:39
  95.8 15.4 %collective-permute-start.14 = (f32[4096]{0:T(1024)S(1)}, f32[4096]{0:T(1024)S(1)}, u32[]{:S(2)}, u32[]{:S(2)}) collective-permute-start(f32[4096]{0:T(1024)S(1)} %sub.6), channel_id=1, source_target_pairs={{0,64},{64,0},{128,192},{192,128},{256,320},{320,256},{384,448},{4... | collective-permute-start | bytes 49160 | tf_op jit(solution)/shard_map/ppermute | solution.py:176
  111.2 5.6 %collective-permute-start.15 = (f32[4096]{0:T(1024)S(1)}, f32[4096]{0:T(1024)S(1)}, u32[]{:S(2)}, u32[]{:S(2)}) collective-permute-start(f32[4096]{0:T(1024)S(1)} %add.23), channel_id=1, source_target_pairs={{0,128},{64,192},{128,0},{192,64},{256,384},{320,448},{384,256},{4... | collective-permute-start | bytes 49160 | tf_op jit(solution)/shard_map/ppermute | solution.py:176
  116.8 7.1 %collective-permute-start.16 = (f32[4096]{0:T(1024)S(1)}, f32[4096]{0:T(1024)S(1)}, u32[]{:S(2)}, u32[]{:S(2)}) collective-permute-start(f32[4096]{0:T(1024)S(1)} %add.24), channel_id=1, source_target_pairs={{0,256},{64,320},{128,384},{192,448},{256,0},{320,64},{384,128},{4... | collective-permute-start | bytes 49160 | tf_op jit(solution)/shard_map/ppermute | solution.py:176

commit v2 on v0

v2 whole, which is shorter than its diff:
```python
import jax
import jax.numpy as jnp
from jax import lax
from jax.experimental import pallas as pl
from jax.experimental.pallas import tpu as pltpu
from jax.sharding import PartitionSpec as P

norm_eps = 1e-05
outer_momentum = 0.9
outer_rate = 0.7

NY, NZ, NC = 4, 8, 2
EVEN = ((0, 4, 2, 6), (0, 2, 4, 6))
ODD = ((1, 5, 3, 7), (1, 3, 5, 7))
WIDE = 1024
MIB = 1 << 20


def device_pairs(move):
    pairs = []
    for y in range(NY):
        for z in range(NZ):
            for c in range(NC):
                to_y, to_z, to_c = move(y, z, c)
                pairs.append(((y * NZ + z) * NC + c, ((to_y % NY) * NZ + to_z) * NC + to_c))
    return pairs


def to_z(*bits):
    return device_pairs(lambda y, z, c: (y, z ^ bits[c], c))


def to_y(step):
    return device_pairs(lambda y, z, c: (y + step, z, c))


to_core = device_pairs(lambda y, z, c: (y, z, 1 - c))


def send(x, pairs):
    return lax.ppermute(x, "fsdp", pairs)


def place():
    me = lax.axis_index("fsdp")
    return me // (NZ * NC), lax.rem(me // NC, NZ), lax.rem(me, NC)


def slab(y, step):
    return pl.ds(pl.multiple_of(lax.rem(y + step, NY) * WIDE, WIDE), WIDE)


def prepare_kernel(tok_ref, cot_ref, *refs):
    outs, inv_ref = refs[:NY], refs[NY]
    y, _, _ = place()
    x = tok_ref[...].astype(jnp.float32)
    inv = lax.rsqrt(jnp.mean(x * x, axis=1, keepdims=True) + norm_eps)
    inv_ref[...] = inv
    for step, out_ref in enumerate(outs):
        out_ref[:, :WIDE] = (tok_ref[:, slab(y, step)].astype(jnp.float32) * inv).astype(jnp.bfloat16)
        out_ref[:, WIDE:] = cot_ref[...]


def project_kernel(first_ref, second_ref, first_sib_ref, second_sib_ref, *refs):
    ins, (own_ref, *outs), (weight_ref, act_ref) = refs[:NY], refs[NY : 2 * NY], refs[2 * NY :]
    _, z, c = place()
    rows = ins[0].shape[0]
    for sib, pair in enumerate(((first_ref, second_ref), (first_sib_ref, second_sib_ref))):
        core = lax.rem(c + sib, NC)
        for order, ref in zip((EVEN, ODD), pair):
            for i in range(4):
                dz = jnp.where(core == 0, order[0][i], order[1][i])
                at = pl.multiple_of(jnp.bitwise_xor(z, dz) * 128 + core * 64, 64)
                weight_ref[pl.ds(at, 64)] = ref[64 * i : 64 * (i + 1)]
    for n, ref in enumerate(ins):
        act_ref[rows * n : rows * (n + 1)] = ref[...]
    for half in range(2):
        for i in range(WIDE // 256):
            cols = slice(256 * i, 256 * (i + 1))
            if half == 0:
                part = jnp.dot(act_ref[:, :WIDE], weight_ref[:, cols], preferred_element_type=jnp.float32)
            else:
                part = lax.dot_general(
                    act_ref[:, WIDE:],
                    weight_ref[cols],
                    (((1,), (1,)), ((), ())),
                    preferred_element_type=jnp.float32,
                )
            cols = slice(WIDE * half + 256 * i, WIDE * half + 256 * (i + 1))
            own_ref[:, cols] = part[:rows]
            for n, out_ref in enumerate(outs, 1):
                out_ref[:, cols] = part[rows * n : rows * (n + 1)].astype(jnp.bfloat16)


def finish_kernel(tok_ref, inv_ref, own_ref, *refs):
    gots, (kv_ref, grad_ref, full_ref) = refs[: NY - 1], refs[NY - 1 :]
    y, _, _ = place()
    inv = inv_ref[...]
    kv = own_ref[:, :WIDE]
    for ref in gots:
        kv += ref[:, :WIDE].astype(jnp.float32)
    kv_ref[...] = kv.astype(jnp.bfloat16)
    inner = 0.0
    for step, ref in enumerate((own_ref, *gots)):
        cols = slab(y, step)
        grad = ref[:, WIDE:].astype(jnp.float32)
        full_ref[:, cols] = grad
        inner += jnp.sum(grad * (tok_ref[:, cols].astype(jnp.float32) * inv), axis=1, keepdims=True)
    inner = inner / tok_ref.shape[1]
    normed = tok_ref[...].astype(jnp.float32) * inv
    grad_ref[...] = (inv * (full_ref[...] - normed * inner)).astype(jnp.bfloat16)


def local(tokens, kv_weight, kv_cotangent, fragment_index, anchor, momentum, replica_frag):
    rows, width = tokens.shape
    shard = kv_weight[0]
    tie = lax.optimization_barrier
    params = pltpu.CompilerParams(vmem_limit_bytes=40 * MIB)

    frag_pick = fragment_index[0]
    anchor_now = lax.dynamic_index_in_dim(anchor, frag_pick, 0, keepdims=False)
    moment_now = lax.dynamic_index_in_dim(momentum, frag_pick, 0, keepdims=False)
    replica_now = lax.dynamic_index_in_dim(replica_frag[0], frag_pick, 0, keepdims=False).astype(
        jnp.float32
    )
    replicas = lax.axis_size("rep")
    drift = anchor_now - replica_now

    def add_half(drift, bit):
        return drift + lax.ppermute(drift, "rep", [(r, r ^ bit) for r in range(replicas)])

    block = jax.ShapeDtypeStruct((rows, 2 * WIDE), jnp.bfloat16)
    *acts, inv = pl.pallas_call(
        prepare_kernel,
        out_shape=(block,) * NY + (jax.ShapeDtypeStruct((rows, 1), jnp.float32),),
        compiler_params=params,
        cost_estimate=pl.CostEstimate(flops=2**21, bytes_accessed=4 * MIB, transcendentals=128),
        name="prepare",
    )(tokens, kv_cotangent)

    far = send(shard, to_z(4, 2))
    act1 = send(acts[1], to_y(1))
    act3 = send(acts[3], to_y(3))
    far, drift = tie((far, drift))
    pair = jnp.concatenate([shard, far], axis=0)
    more = send(pair, to_z(2, 4))
    pair, drift = tie((pair, drift))
    drift = add_half(drift, 2)
    drift, acts[2] = tie((drift, acts[2]))
    act2 = send(acts[2], to_y(2))
    more, drift, act1 = tie((more, drift, act1))
    first = jnp.concatenate([pair, more], axis=0)
    second = send(first, to_z(1, 1))
    first_sib = send(first, to_core)
    drift = add_half(drift, 4)
    second, act2, act3, drift = tie((second, act2, act3, drift))
    acts = [acts[0], act1, act2, act3]
    second_sib = send(second, to_core)
    weights = (first, second, first_sib, second_sib)
    own, *backs = pl.pallas_call(
        project_kernel,
        out_shape=(jax.ShapeDtypeStruct((rows, 2 * WIDE), jnp.float32),) + (block,) * (NY - 1),
        scratch_shapes=[
            pltpu.VMEM((WIDE, WIDE), jnp.bfloat16),
            pltpu.VMEM((NY * rows, 2 * WIDE), jnp.bfloat16),
        ],
        compiler_params=params,
        cost_estimate=pl.CostEstimate(flops=2**31, bytes_accessed=8 * MIB, transcendentals=0),
        name="project",
    )(*weights, *acts)
    drift, *backs = tie((drift, *backs))
    gots = [send(backs[n - 1], to_y(-n)) for n in (1, 3, 2)]
    gots = [gots[0], gots[2], gots[1]]
    drift = add_half(drift, 1)
    outer_grad = drift / replicas
    momentum_new = outer_momentum * moment_now + outer_grad
    anchor_new = anchor_now - outer_rate * (outer_grad + outer_momentum * momentum_new)
    key_value, input_grad = pl.pallas_call(
        finish_kernel,
        out_shape=(
            jax.ShapeDtypeStruct((rows, WIDE), jnp.bfloat16),
            jax.ShapeDtypeStruct((rows, width), jnp.bfloat16),
        ),
        scratch_shapes=[pltpu.VMEM((rows, width), jnp.float32)],
        compiler_params=params,
        cost_estimate=pl.CostEstimate(flops=2**22, bytes_accessed=5 * MIB, transcendentals=0),
        name="finish",
    )(tokens, inv, own, *gots)
    return key_value, input_grad, anchor_new, momentum_new


def solution(mesh):
    return jax.shard_map(
        local,
        mesh=mesh,
        in_specs=(
            P(("rep", "fsdp"), None),
            P("rep", "fsdp", None),
            P(("rep", "fsdp"), None),
            P(),
            P(None, "fsdp"),
            P(None, "fsdp"),
            P("rep", None, "fsdp"),
        ),
        out_specs=(P(("rep", "fsdp"), None), P(("rep", "fsdp"), None), P("fsdp"), P("fsdp")),
        check_vma=False,
    )
```

time: 160 us -> 92.4 us (0.58)
  blocking collectives: 75.7 us -> 0 us
  starting transfers between devices: 0.04 us -> 67.4 us
  waiting for transfers between devices: 54.9 us -> 12.8 us
  between operations: 14.7 us -> 1.55 us
  matrix products: 8.5 us -> 0 us
  Pallas kernels: 0 us -> 5.27 us
  other arithmetic: 5.44 us -> 2.44 us
    psum x1 -> x0, blocking collectives: 75.7 us -> none  [local(): outer_grad = lax.psum(replica_drift, 'rep') / replicas]
    ppermute x0 -> x14, starting transfers between devices: none -> 67.4 us  [the longest x11 47.5 us: send(): return lax.ppermute(x, 'fsdp', pairs)]
    all_gather x1 -> x0, waiting for transfers between devices: 54.2 us -> none  [local(): full_rows = lax.all_gather(weight, 'fsdp', axis=0, tiled=True)]
    ppermute x0 -> x14, waiting for transfers between devices: none -> 12.8 us  [the longest x11 11 us: send(): return lax.ppermute(x, 'fsdp', pairs)]
    dot_general x2 -> x0, matrix products: 8.5 us -> none  [the longest x1 6.49 us: local(): lax.dot_general(kv_cotangent, full_rows, (((1,), (1,)), ((), ())), prefer...]
    pallas_call x0 -> x3, Pallas kernels: none -> 5.27 us  [the longest x1 2.49 us: local(): pl.pallas_call(project_kernel, out_shape=(jax.ShapeDtypeStruct((rows, 2 *...]
    unnamed x6 -> x11, local copies, waits for them, and re-layouts: 0.02 us -> 2.21 us
  transfers between devices with their start and end apart: 1 -> 14, of which waited for: 1 -> 5; matrix products, arithmetic and copies ran while one was open for 3% -> 3% of each run, Pallas kernels for 0% -> 1%
where the time goes in v2:
time: 92.4 us; the launch traced here: 91.7 us
  starting transfers between devices  67.4 us (73%)
  waiting for transfers between devices  12.8 us (14%)
  Pallas kernels  5.27 us (6%)
  other arithmetic  2.44 us (3%)
  local copies, waits for them, and re-layouts  2.24 us (2%)
  between operations  1.55 us (2%)
    ppermute x11, starting transfers between devices, send(): return lax.ppermute(x, 'fsdp', pairs)  47.5 us
    ppermute x3, starting transfers between devices, add_half(): lax.ppermute(drift, 'rep', [(r, r ^ bit) for r in range(replicas)])  19.9 us
    ppermute x11, waiting for transfers between devices, send(): return lax.ppermute(x, 'fsdp', pairs)  11 us
    pallas_call x1, Pallas kernels, local(): pl.pallas_call(project_kernel, out_shape=(jax.ShapeDtypeStruct((rows, 2 *...  2.49 us
    pallas_call x1, Pallas kernels, local(): pl.pallas_call(finish_kernel, out_shape=(jax.ShapeDtypeStruct((rows, WIDE...  2.27 us
    unnamed x11, local copies, waits for them, and re-layouts  2.21 us
  transfers between devices with their start and end apart: 14, of which 5 were waited for; matrix products, arithmetic and copies ran while one was open for 3% of the time, Pallas kernels for 1%

profile of v2, /device:TPU:1, one launch (start us, length us, event | category | flops | bytes accessed | tf_op | source)
XLA Modules:
  0.0 91.7 jit_solution(695471998387034681)
XLA Ops:
  0.6 0.0 copy-start
  0.6 5.9 %collective-permute-start = (bf16[64,1024]{1,0:T(8,128)(2,1)}, bf16[64,1024]{1,0:T(8,128)(2,1)S(1)}, u32[]{:S(2)}, u32[]{:S(2)}) collective-permute-start(bf16[64,1024]{1,0:T(8,128)(2,1)} %bitcast.10), channel_id=1, source_target_pairs={{0,8},{1,5},{2,10},{3,7},{4,12},{5,1},{6,14},{7,3},{8,0},{9,13},{1... | collective-permute-start | bytes 393224 | tf_op jit(solution)/shard_map/ppermute | solution.py:41
  6.5 0.0 copy-start.1
  6.5 1.2 %copy-done.1 = bf16[128,4096]{1,0:T(8,128)(2,1)S(1)} copy-done((bf16[128,4096]{1,0:T(8,128)(2,1)S(1)}, bf16[128,4096]{1,0:T(8,128)(2,1)}, u32[]{:S(2)}) %copy-start.1) | copy-done | bytes 1048600
  7.7 0.0 copy-start.3
  7.7 0.9 %copy-done.3 = bf16[128,1024]{1,0:T(8,128)(2,1)S(1)} copy-done((bf16[128,1024]{1,0:T(8,128)(2,1)S(1)}, bf16[128,1024]{1,0:T(8,128)(2,1)}, u32[]{:S(2)}) %copy-start.3) | copy-done | bytes 262168
  8.7 0.5 prepare.1
  9.2 0.0 copy-start.4
  9.2 3.3 %collective-permute-start.3 = (bf16[128,2048]{1,0:T(8,128)(2,1)S(1)}, bf16[128,2048]{1,0:T(8,128)(2,1)S(1)}, u32[]{:S(2)}, u32[]{:S(2)}) collective-permute-start(bf16[128,2048]{1,0:T(8,128)(2,1)S(1)} %get-tuple-element.39), channel_id=1, source_target_pairs={{0,16},{1,17},{2,18},{3,19},{4,20},{5,21},{6,22},{7,23},{8,24},{9,... | collective-permute-start | bytes 1572872 | tf_op jit(solution)/shard_map/ppermute | solution.py:41
  13.2 0.0 copy-done
  13.3 0.9 dynamic-slice_convert_fusion
  14.1 0.0 collective-permute-done
  14.1 0.0 copy-done.4
  14.2 8.8 %collective-permute-start.1 = (bf16[128,1024]{1,0:T(8,128)(2,1)S(1)}, bf16[128,1024]{1,0:T(8,128)(2,1)S(1)}, u32[]{:S(2)}, u32[]{:S(2)}) collective-permute-start(bf16[128,1024]{1,0:T(8,128)(2,1)S(1)} %pad_maximum_fusion), channel_id=1, source_target_pairs={{0,4},{1,9},{2,6},{3,11},{4,0},{5,13},{6,2},{7,15},{8,12},{9,1},{1... | collective-permute-start | bytes 786440 | tf_op jit(solution)/shard_map/ppermute | solution.py:41
  23.0 3.4 %collective-permute-start.6 = (bf16[128,2048]{1,0:T(8,128)(2,1)S(1)}, bf16[128,2048]{1,0:T(8,128)(2,1)S(1)}, u32[]{:S(2)}, u32[]{:S(2)}) collective-permute-start(bf16[128,2048]{1,0:T(8,128)(2,1)S(1)} %get-tuple-element.42), channel_id=1, source_target_pairs={{0,48},{1,49},{2,50},{3,51},{4,52},{5,53},{6,54},{7,55},{8,56},{9,... | collective-permute-start | bytes 1572872 | tf_op jit(solution)/shard_map/ppermute | solution.py:41
  26.4 3.1 %collective-permute-start.2 = (f32[4096]{0:T(1024)S(1)}, f32[4096]{0:T(1024)S(1)}, u32[]{:S(2)}, u32[]{:S(2)}) collective-permute-start(f32[4096]{0:T(1024)S(1)} %sub.6), channel_id=1, source_target_pairs={{0,128},{64,192},{128,0},{192,64},{256,384},{320,448},{384,256},{4... | collective-permute-start | bytes 49160 | tf_op jit(solution)/shard_map/ppermute | solution.py:130
  29.5 1.6 %collective-permute-done.2 = f32[4096]{0:T(1024)S(1)} collective-permute-done((f32[4096]{0:T(1024)S(1)}, f32[4096]{0:T(1024)S(1)}, u32[]{:S(2)}, u32[]{:S(2)}) %collective-permute-start.2) | collective-permute-done | bytes 16416 | tf_op jit(solution)/shard_map/ppermute | solution.py:130
  31.2 3.5 %collective-permute-start.5 = (bf16[128,2048]{1,0:T(8,128)(2,1)S(1)}, bf16[128,2048]{1,0:T(8,128)(2,1)S(1)}, u32[]{:S(2)}, u32[]{:S(2)}) collective-permute-start(bf16[128,2048]{1,0:T(8,128)(2,1)S(1)} %get-tuple-element.41), channel_id=1, source_target_pairs={{0,32},{1,33},{2,34},{3,35},{4,36},{5,37},{6,38},{7,39},{8,40},{9,... | collective-permute-start | bytes 1572872 | tf_op jit(solution)/shard_map/ppermute | solution.py:41
  34.7 0.3 collective-permute-done.1
  35.0 0.0 collective-permute-done.3.refs_1_
  35.0 3.3 %collective-permute-start.4 = (bf16[256,1024]{1,0:T(8,128)(2,1)S(1)}, bf16[256,1024]{1,0:T(8,128)(2,1)S(1)}, u32[]{:S(2)}, u32[]{:S(2)}) collective-permute-start(bf16[256,1024]{1,0:T(8,128)(2,1)S(1)} %constant_dynamic-update-slice_fusion.first_ref), channel_id=1, source_target_pairs={{0,2},{1,3},{2,0},{3,1},{4,6},{5,7},{6,4},{7,5},{8,10},{9,11},{10,... | collective-permute-start | bytes 1572872 | tf_op jit(solution)/shard_map/ppermute | solution.py:41
  38.3 4.7 %collective-permute-start.7 = (f32[4096]{0:T(1024)S(1)}, f32[4096]{0:T(1024)S(1)}, u32[]{:S(2)}, u32[]{:S(2)}) collective-permute-start(f32[4096]{0:T(1024)S(1)} %add.23), channel_id=1, source_target_pairs={{0,256},{64,320},{128,384},{192,448},{256,0},{320,64},{384,128},{4... | collective-permute-start | bytes 49160 | tf_op jit(solution)/shard_map/ppermute | solution.py:130
  43.0 5.4 %collective-permute-start.8 = (bf16[256,1024]{1,0:T(8,128)(2,1)S(1)}, bf16[256,1024]{1,0:T(8,128)(2,1)S(1)}, u32[]{:S(2)}, u32[]{:S(2)}) collective-permute-start(bf16[256,1024]{1,0:T(8,128)(2,1)S(1)} %constant_dynamic-update-slice_fusion.first_ref), channel_id=1, source_target_pairs={{0,1},{1,0},{2,3},{3,2},{4,5},{5,4},{6,7},{7,6},{8,9},{9,8},{10,11... | collective-permute-start | bytes 1572872 | tf_op jit(solution)/shard_map/ppermute | solution.py:41
  48.4 0.0 collective-permute-done.7
  48.4 0.0 collective-permute-done.6.refs_3_
  48.4 0.0 collective-permute-done.5.refs_2_
  48.4 0.0 collective-permute-done.4.second_ref
  48.4 4.7 %collective-permute-start.9 = (bf16[256,1024]{1,0:T(8,128)(2,1)S(1)}, bf16[256,1024]{1,0:T(8,128)(2,1)S(1)}, u32[]{:S(2)}, u32[]{:S(2)}) collective-permute-start(bf16[256,1024]{1,0:T(8,128)(2,1)S(1)} %collective-permute-done.4.second_ref), channel_id=1, source_target_pairs={{0,1},{1,0},{2,3},{3,2},{4,5},{5,4},{6,7},{7,6},{8,9},{9,8},{10,11... | collective-permute-start | bytes 1572872 | tf_op jit(solution)/shard_map/ppermute | solution.py:41
  53.2 0.0 collective-permute-done.8.first_sib_ref
  53.2 1.5 %collective-permute-done.9.second_sib_ref = bf16[256,1024]{1,0:T(8,128)(2,1)S(1)} collective-permute-done((bf16[256,1024]{1,0:T(8,128)(2,1)S(1)}, bf16[256,1024]{1,0:T(8,128)(2,1)S(1)}, u32[]{:S(2)}, u32[]{:S(2)}) %collective-permute-start.9) | collective-permute-done | bytes 524320 | tf_op jit(solution)/shard_map/ppermute | solution.py:41
  54.7 0.0 copy-start.2
  54.7 2.5 %project.1 = (f32[128,2048]{1,0:T(8,128)S(1)}, bf16[128,2048]{1,0:T(8,128)(2,1)S(1)}, bf16[128,2048]{1,0:T(8,128)(2,1)S(1)}, bf16[128,2048]{1,0:T(8,128)(2,1)S(1)}) custom-call(bf16[256,1024]{1,0:T(8,128)(2,1)S(1)} %constant_dynamic-update-slice_fusion.first_ref, bf16[256,1024]{1,0:T(8,128)(2,1)S(1)} %collective-permute-done.4.second_ref, ...), custom_call_target="tpu_custom_call" | custom-call | flops 2147483648 | bytes 8388608 | tf_op jit(solution)/shard_map/project/pallas_call | solution.py:160
  57.2 3.8 %collective-permute-start.10 = (bf16[128,2048]{1,0:T(8,128)(2,1)S(1)}, bf16[128,2048]{1,0:T(8,128)(2,1)S(1)}, u32[]{:S(2)}, u32[]{:S(2)}) collective-permute-start(bf16[128,2048]{1,0:T(8,128)(2,1)S(1)} %get-tuple-element.54), channel_id=1, source_target_pairs={{0,48},{1,49},{2,50},{3,51},{4,52},{5,53},{6,54},{7,55},{8,56},{9,... | collective-permute-start | bytes 1572872 | tf_op jit(solution)/shard_map/ppermute | solution.py:41
  61.0 3.1 %collective-permute-start.11 = (bf16[128,2048]{1,0:T(8,128)(2,1)S(1)}, bf16[128,2048]{1,0:T(8,128)(2,1)S(1)}, u32[]{:S(2)}, u32[]{:S(2)}) collective-permute-start(bf16[128,2048]{1,0:T(8,128)(2,1)S(1)} %get-tuple-element.55), channel_id=1, source_target_pairs={{0,32},{1,33},{2,34},{3,35},{4,36},{5,37},{6,38},{7,39},{8,40},{9,... | collective-permute-start | bytes 1572872 | tf_op jit(solution)/shard_map/ppermute | solution.py:41
  64.1 2.3 %collective-permute-start.12 = (bf16[128,2048]{1,0:T(8,128)(2,1)S(1)}, bf16[128,2048]{1,0:T(8,128)(2,1)S(1)}, u32[]{:S(2)}, u32[]{:S(2)}) collective-permute-start(bf16[128,2048]{1,0:T(8,128)(2,1)S(1)} %get-tuple-element.56), channel_id=1, source_target_pairs={{0,16},{1,17},{2,18},{3,19},{4,20},{5,21},{6,22},{7,23},{8,24},{9,... | collective-permute-start | bytes 1572872 | tf_op jit(solution)/shard_map/ppermute | solution.py:41
  66.4 12.2 %collective-permute-start.13 = (f32[4096]{0:T(1024)S(1)}, f32[4096]{0:T(1024)S(1)}, u32[]{:S(2)}, u32[]{:S(2)}) collective-permute-start(f32[4096]{0:T(1024)S(1)} %add.24), channel_id=1, source_target_pairs={{0,64},{64,0},{128,192},{192,128},{256,320},{320,256},{384,448},{4... | collective-permute-start | bytes 49160 | tf_op jit(solution)/shard_map/ppermute | solution.py:130
  78.6 0.9 %dynamic-slice_multiply_fusion = f32[1,4096]{1,0:T(1,128)S(1)} fusion(f32[8,4096]{1,0:T(8,128)} %param.12, s32[]{:T(128)S(6)} %select_n.7), kind=kLoop, calls=%fused_computation.2 | loop fusion | flops 4096 | bytes 32772 | tf_op jit(solution)/shard_map/mul | solution.py:176
  79.5 0.2 collective-permute-done.13
  79.7 0.6 multiply_subtract_fusion
  80.3 0.0 collective-permute-done.10.refs_0_
  80.3 0.0 collective-permute-done.11.refs_1_
  80.3 9.1 %collective-permute-done.12.refs_2_ = bf16[128,2048]{1,0:T(8,128)(2,1)S(1)} collective-permute-done((bf16[128,2048]{1,0:T(8,128)(2,1)S(1)}, bf16[128,2048]{1,0:T(8,128)(2,1)S(1)}, u32[]{:S(2)}, u32[]{:S(2)}) %collective-permute-start.12) | collective-permute-done | bytes 524320 | tf_op jit(solution)/shard_map/ppermute | solution.py:41
  89.5 0.0 copy-done.2
  89.5 2.3 %finish.1 = (bf16[128,1024]{1,0:T(8,128)(2,1)}, bf16[128,4096]{1,0:T(8,128)(2,1)}) custom-call(bf16[128,4096]{1,0:T(8,128)(2,1)S(1)} %copy-done.2, f32[128,1]{1,0:T(8,128)S(1)} %get-tuple-element.32.inv_ref, f32[128,2048]{1,0:T(8,128)S(1)} %get-tuple-element.49.own_ref, bf16[128,2048]{1,0:T(8,128)(2,1)S(1)} %collective-permute-done.10.refs_0_, ...), custom_call_target="tpu_custom_call" | custom-call | flops 4194304 | bytes 5242880 | tf_op jit(solution)/shard_map/finish/pallas_call | solution.py:178
  (7 shorter events, 0.1 us)
Async XLA Ops:
  0.6 12.6 %copy-start = (f32[8,4096]{1,0:T(8,128)S(1)}, f32[8,4096]{1,0:T(8,128)}, u32[]{:S(2)}) copy-start(f32[8,4096]{1,0:T(8,128)} %param.11) | copy-start | bytes 393220
  0.6 13.5 %collective-permute-start = (bf16[64,1024]{1,0:T(8,128)(2,1)}, bf16[64,1024]{1,0:T(8,128)(2,1)S(1)}, u32[]{:S(2)}, u32[]{:S(2)}) collective-permute-start(bf16[64,1024]{1,0:T(8,128)(2,1)} %bitcast.10), channel_id=1, source_target_pairs={{0,8},{1,5},{2,10},{3,7},{4,12},{5,1},{6,14},{7,3},{8,0},{9,13},{1... | collective-permute-start | bytes 393224 | tf_op jit(solution)/shard_map/ppermute | solution.py:41
  6.5 1.2 %copy-start.1 = (bf16[128,4096]{1,0:T(8,128)(2,1)S(1)}, bf16[128,4096]{1,0:T(8,128)(2,1)}, u32[]{:S(2)}) copy-start(bf16[128,4096]{1,0:T(8,128)(2,1)} %tok_ref.3) | copy-start | bytes 3145732
  7.7 0.9 %copy-start.3 = (bf16[128,1024]{1,0:T(8,128)(2,1)S(1)}, bf16[128,1024]{1,0:T(8,128)(2,1)}, u32[]{:S(2)}) copy-start(bf16[128,1024]{1,0:T(8,128)(2,1)} %cot_ref.1) | copy-start | bytes 786436
  9.2 4.9 %copy-start.4 = (bf16[1,64,1024]{2,1,0:T(8,128)(2,1)S(1)}, bf16[1,64,1024]{2,1,0:T(8,128)(2,1)}, u32[]{:S(2)}) copy-start(bf16[1,64,1024]{2,1,0:T(8,128)(2,1)} %param.8) | copy-start | bytes 393220
  9.2 25.8 %collective-permute-start.3 = (bf16[128,2048]{1,0:T(8,128)(2,1)S(1)}, bf16[128,2048]{1,0:T(8,128)(2,1)S(1)}, u32[]{:S(2)}, u32[]{:S(2)}) collective-permute-start(bf16[128,2048]{1,0:T(8,128)(2,1)S(1)} %get-tuple-element.39), channel_id=1, source_target_pairs={{0,16},{1,17},{2,18},{3,19},{4,20},{5,21},{6,22},{7,23},{8,24},{9,... | collective-permute-start | bytes 1572872 | tf_op jit(solution)/shard_map/ppermute | solution.py:41
  14.2 20.8 %collective-permute-start.1 = (bf16[128,1024]{1,0:T(8,128)(2,1)S(1)}, bf16[128,1024]{1,0:T(8,128)(2,1)S(1)}, u32[]{:S(2)}, u32[]{:S(2)}) collective-permute-start(bf16[128,1024]{1,0:T(8,128)(2,1)S(1)} %pad_maximum_fusion), channel_id=1, source_target_pairs={{0,4},{1,9},{2,6},{3,11},{4,0},{5,13},{6,2},{7,15},{8,12},{9,1},{1... | collective-permute-start | bytes 786440 | tf_op jit(solution)/shard_map/ppermute | solution.py:41
  23.0 25.4 %collective-permute-start.6 = (bf16[128,2048]{1,0:T(8,128)(2,1)S(1)}, bf16[128,2048]{1,0:T(8,128)(2,1)S(1)}, u32[]{:S(2)}, u32[]{:S(2)}) collective-permute-start(bf16[128,2048]{1,0:T(8,128)(2,1)S(1)} %get-tuple-element.42), channel_id=1, source_target_pairs={{0,48},{1,49},{2,50},{3,51},{4,52},{5,53},{6,54},{7,55},{8,56},{9,... | collective-permute-start | bytes 1572872 | tf_op jit(solution)/shard_map/ppermute | solution.py:41
  26.4 4.8 %collective-permute-start.2 = (f32[4096]{0:T(1024)S(1)}, f32[4096]{0:T(1024)S(1)}, u32[]{:S(2)}, u32[]{:S(2)}) collective-permute-start(f32[4096]{0:T(1024)S(1)} %sub.6), channel_id=1, source_target_pairs={{0,128},{64,192},{128,0},{192,64},{256,384},{320,448},{384,256},{4... | collective-permute-start | bytes 49160 | tf_op jit(solution)/shard_map/ppermute | solution.py:130
  31.2 17.2 %collective-permute-start.5 = (bf16[128,2048]{1,0:T(8,128)(2,1)S(1)}, bf16[128,2048]{1,0:T(8,128)(2,1)S(1)}, u32[]{:S(2)}, u32[]{:S(2)}) collective-permute-start(bf16[128,2048]{1,0:T(8,128)(2,1)S(1)} %get-tuple-element.41), channel_id=1, source_target_pairs={{0,32},{1,33},{2,34},{3,35},{4,36},{5,37},{6,38},{7,39},{8,40},{9,... | collective-permute-start | bytes 1572872 | tf_op jit(solution)/shard_map/ppermute | solution.py:41
  35.0 13.4 %collective-permute-start.4 = (bf16[256,1024]{1,0:T(8,128)(2,1)S(1)}, bf16[256,1024]{1,0:T(8,128)(2,1)S(1)}, u32[]{:S(2)}, u32[]{:S(2)}) collective-permute-start(bf16[256,1024]{1,0:T(8,128)(2,1)S(1)} %constant_dynamic-update-slice_fusion.first_ref), channel_id=1, source_target_pairs={{0,2},{1,3},{2,0},{3,1},{4,6},{5,7},{6,4},{7,5},{8,10},{9,11},{10,... | collective-permute-start | bytes 1572872 | tf_op jit(solution)/shard_map/ppermute | solution.py:41
  38.3 10.1 %collective-permute-start.7 = (f32[4096]{0:T(1024)S(1)}, f32[4096]{0:T(1024)S(1)}, u32[]{:S(2)}, u32[]{:S(2)}) collective-permute-start(f32[4096]{0:T(1024)S(1)} %add.23), channel_id=1, source_target_pairs={{0,256},{64,320},{128,384},{192,448},{256,0},{320,64},{384,128},{4... | collective-permute-start | bytes 49160 | tf_op jit(solution)/shard_map/ppermute | solution.py:130
  43.0 10.2 %collective-permute-start.8 = (bf16[256,1024]{1,0:T(8,128)(2,1)S(1)}, bf16[256,1024]{1,0:T(8,128)(2,1)S(1)}, u32[]{:S(2)}, u32[]{:S(2)}) collective-permute-start(bf16[256,1024]{1,0:T(8,128)(2,1)S(1)} %constant_dynamic-update-slice_fusion.first_ref), channel_id=1, source_target_pairs={{0,1},{1,0},{2,3},{3,2},{4,5},{5,4},{6,7},{7,6},{8,9},{9,8},{10,11... | collective-permute-start | bytes 1572872 | tf_op jit(solution)/shard_map/ppermute | solution.py:41
  48.4 6.3 %collective-permute-start.9 = (bf16[256,1024]{1,0:T(8,128)(2,1)S(1)}, bf16[256,1024]{1,0:T(8,128)(2,1)S(1)}, u32[]{:S(2)}, u32[]{:S(2)}) collective-permute-start(bf16[256,1024]{1,0:T(8,128)(2,1)S(1)} %collective-permute-done.4.second_ref), channel_id=1, source_target_pairs={{0,1},{1,0},{2,3},{3,2},{4,5},{5,4},{6,7},{7,6},{8,9},{9,8},{10,11... | collective-permute-start | bytes 1572872 | tf_op jit(solution)/shard_map/ppermute | solution.py:41
  54.7 34.8 %copy-start.2 = (bf16[128,4096]{1,0:T(8,128)(2,1)S(1)}, bf16[128,4096]{1,0:T(8,128)(2,1)}, u32[]{:S(2)}) copy-start(bf16[128,4096]{1,0:T(8,128)(2,1)} %tok_ref.3) | copy-start | bytes 3145732
  57.2 23.1 %collective-permute-start.10 = (bf16[128,2048]{1,0:T(8,128)(2,1)S(1)}, bf16[128,2048]{1,0:T(8,128)(2,1)S(1)}, u32[]{:S(2)}, u32[]{:S(2)}) collective-permute-start(bf16[128,2048]{1,0:T(8,128)(2,1)S(1)} %get-tuple-element.54), channel_id=1, source_target_pairs={{0,48},{1,49},{2,50},{3,51},{4,52},{5,53},{6,54},{7,55},{8,56},{9,... | collective-permute-start | bytes 1572872 | tf_op jit(solution)/shard_map/ppermute | solution.py:41
  61.0 19.3 %collective-permute-start.11 = (bf16[128,2048]{1,0:T(8,128)(2,1)S(1)}, bf16[128,2048]{1,0:T(8,128)(2,1)S(1)}, u32[]{:S(2)}, u32[]{:S(2)}) collective-permute-start(bf16[128,2048]{1,0:T(8,128)(2,1)S(1)} %get-tuple-element.55), channel_id=1, source_target_pairs={{0,32},{1,33},{2,34},{3,35},{4,36},{5,37},{6,38},{7,39},{8,40},{9,... | collective-permute-start | bytes 1572872 | tf_op jit(solution)/shard_map/ppermute | solution.py:41
  64.1 25.4 %collective-permute-start.12 = (bf16[128,2048]{1,0:T(8,128)(2,1)S(1)}, bf16[128,2048]{1,0:T(8,128)(2,1)S(1)}, u32[]{:S(2)}, u32[]{:S(2)}) collective-permute-start(bf16[128,2048]{1,0:T(8,128)(2,1)S(1)} %get-tuple-element.56), channel_id=1, source_target_pairs={{0,16},{1,17},{2,18},{3,19},{4,20},{5,21},{6,22},{7,23},{8,24},{9,... | collective-permute-start | bytes 1572872 | tf_op jit(solution)/shard_map/ppermute | solution.py:41
  66.4 13.3 %collective-permute-start.13 = (f32[4096]{0:T(1024)S(1)}, f32[4096]{0:T(1024)S(1)}, u32[]{:S(2)}, u32[]{:S(2)}) collective-permute-start(f32[4096]{0:T(1024)S(1)} %add.24), channel_id=1, source_target_pairs={{0,64},{64,0},{128,192},{192,128},{256,320},{320,256},{384,448},{4... | collective-permute-start | bytes 49160 | tf_op jit(solution)/shard_map/ppermute | solution.py:130

commit v3 on v2

--- a/solution.py
+++ b/solution.py
@@ -101,7 +101,7 @@
         kv += ref[:, :WIDE].astype(jnp.float32)
     kv_ref[...] = kv.astype(jnp.bfloat16)
     inner = 0.0
-    for step, ref in enumerate((own_ref, *gots)):
+    for step, ref in zip((0, 2, 1, 3), (own_ref, *gots)):
         cols = slab(y, step)
         grad = ref[:, WIDE:].astype(jnp.float32)
         full_ref[:, cols] = grad
@@ -169,8 +169,7 @@
         name="project",
     )(*weights, *acts)
     drift, *backs = tie((drift, *backs))
-    gots = [send(backs[n - 1], to_y(-n)) for n in (1, 3, 2)]
-    gots = [gots[0], gots[2], gots[1]]
+    gots = [send(backs[n - 1], to_y(-n)) for n in (2, 1, 3)]
     drift = add_half(drift, 1)
     outer_grad = drift / replicas
     momentum_new = outer_momentum * moment_now + outer_grad

time: 92.4 us -> 88.6 us (0.959)
  waiting for transfers between devices: 12.8 us -> 8.39 us
    ppermute x11, waiting for transfers between devices: 11 us -> 6.58 us  [send(): return lax.ppermute(x, 'fsdp', pairs)]
  transfers between devices with their start and end apart: 14 -> 14, of which waited for: 5 -> 6; matrix products, arithmetic and copies ran while one was open for 3% -> 3% of each run, Pallas kernels for 1% -> 1%
where the time goes in v3:
time: 88.6 us; the launch traced here: 87.9 us
  starting transfers between devices  68 us (77%)
  waiting for transfers between devices  8.39 us (9%)
  Pallas kernels  5.27 us (6%)
  other arithmetic  2.44 us (3%)
  local copies, waits for them, and re-layouts  2.24 us (3%)
  between operations  1.55 us (2%)
    ppermute x11, starting transfers between devices, send(): return lax.ppermute(x, 'fsdp', pairs)  48.1 us
    ppermute x3, starting transfers between devices, add_half(): lax.ppermute(drift, 'rep', [(r, r ^ bit) for r in range(replicas)])  19.9 us
    ppermute x11, waiting for transfers between devices, send(): return lax.ppermute(x, 'fsdp', pairs)  6.58 us
    pallas_call x1, Pallas kernels, local(): pl.pallas_call(project_kernel, out_shape=(jax.ShapeDtypeStruct((rows, 2 *...  2.49 us
    pallas_call x1, Pallas kernels, local(): pl.pallas_call(finish_kernel, out_shape=(jax.ShapeDtypeStruct((rows, WIDE...  2.27 us
    unnamed x11, local copies, waits for them, and re-layouts  2.21 us
    ppermute x3, waiting for transfers between devices, add_half(): lax.ppermute(drift, 'rep', [(r, r ^ bit) for r in range(replicas)])  1.81 us
  transfers between devices with their start and end apart: 14, of which 6 were waited for; matrix products, arithmetic and copies ran while one was open for 3% of the time, Pallas kernels for 1%

profile of v3, /device:TPU:1, one launch (start us, length us, event | category | flops | bytes accessed | tf_op | source)
XLA Modules:
  0.0 87.9 jit_solution(15918248615531695588)
XLA Ops:
  0.6 0.0 copy-start
  0.6 5.9 %collective-permute-start = (bf16[64,1024]{1,0:T(8,128)(2,1)}, bf16[64,1024]{1,0:T(8,128)(2,1)S(1)}, u32[]{:S(2)}, u32[]{:S(2)}) collective-permute-start(bf16[64,1024]{1,0:T(8,128)(2,1)} %bitcast.10), channel_id=1, source_target_pairs={{0,8},{1,5},{2,10},{3,7},{4,12},{5,1},{6,14},{7,3},{8,0},{9,13},{1... | collective-permute-start | bytes 393224 | tf_op jit(solution)/shard_map/ppermute | solution.py:41
  6.5 0.0 copy-start.1
  6.5 1.2 %copy-done.1 = bf16[128,4096]{1,0:T(8,128)(2,1)S(1)} copy-done((bf16[128,4096]{1,0:T(8,128)(2,1)S(1)}, bf16[128,4096]{1,0:T(8,128)(2,1)}, u32[]{:S(2)}) %copy-start.1) | copy-done | bytes 1048600
  7.7 0.0 copy-start.3
  7.7 0.9 %copy-done.3 = bf16[128,1024]{1,0:T(8,128)(2,1)S(1)} copy-done((bf16[128,1024]{1,0:T(8,128)(2,1)S(1)}, bf16[128,1024]{1,0:T(8,128)(2,1)}, u32[]{:S(2)}) %copy-start.3) | copy-done | bytes 262168
  8.7 0.5 prepare.1
  9.2 0.0 copy-start.4
  9.2 3.3 %collective-permute-start.3 = (bf16[128,2048]{1,0:T(8,128)(2,1)S(1)}, bf16[128,2048]{1,0:T(8,128)(2,1)S(1)}, u32[]{:S(2)}, u32[]{:S(2)}) collective-permute-start(bf16[128,2048]{1,0:T(8,128)(2,1)S(1)} %get-tuple-element.39), channel_id=1, source_target_pairs={{0,16},{1,17},{2,18},{3,19},{4,20},{5,21},{6,22},{7,23},{8,24},{9,... | collective-permute-start | bytes 1572872 | tf_op jit(solution)/shard_map/ppermute | solution.py:41
  13.2 0.0 copy-done
  13.3 0.9 dynamic-slice_convert_fusion
  14.1 0.0 collective-permute-done
  14.1 0.0 copy-done.4
  14.2 8.8 %collective-permute-start.1 = (bf16[128,1024]{1,0:T(8,128)(2,1)S(1)}, bf16[128,1024]{1,0:T(8,128)(2,1)S(1)}, u32[]{:S(2)}, u32[]{:S(2)}) collective-permute-start(bf16[128,1024]{1,0:T(8,128)(2,1)S(1)} %pad_maximum_fusion), channel_id=1, source_target_pairs={{0,4},{1,9},{2,6},{3,11},{4,0},{5,13},{6,2},{7,15},{8,12},{9,1},{1... | collective-permute-start | bytes 786440 | tf_op jit(solution)/shard_map/ppermute | solution.py:41
  23.0 3.4 %collective-permute-start.6 = (bf16[128,2048]{1,0:T(8,128)(2,1)S(1)}, bf16[128,2048]{1,0:T(8,128)(2,1)S(1)}, u32[]{:S(2)}, u32[]{:S(2)}) collective-permute-start(bf16[128,2048]{1,0:T(8,128)(2,1)S(1)} %get-tuple-element.42), channel_id=1, source_target_pairs={{0,48},{1,49},{2,50},{3,51},{4,52},{5,53},{6,54},{7,55},{8,56},{9,... | collective-permute-start | bytes 1572872 | tf_op jit(solution)/shard_map/ppermute | solution.py:41
  26.4 3.1 %collective-permute-start.2 = (f32[4096]{0:T(1024)S(1)}, f32[4096]{0:T(1024)S(1)}, u32[]{:S(2)}, u32[]{:S(2)}) collective-permute-start(f32[4096]{0:T(1024)S(1)} %sub.6), channel_id=1, source_target_pairs={{0,128},{64,192},{128,0},{192,64},{256,384},{320,448},{384,256},{4... | collective-permute-start | bytes 49160 | tf_op jit(solution)/shard_map/ppermute | solution.py:130
  29.5 1.6 %collective-permute-done.2 = f32[4096]{0:T(1024)S(1)} collective-permute-done((f32[4096]{0:T(1024)S(1)}, f32[4096]{0:T(1024)S(1)}, u32[]{:S(2)}, u32[]{:S(2)}) %collective-permute-start.2) | collective-permute-done | bytes 16416 | tf_op jit(solution)/shard_map/ppermute | solution.py:130
  31.2 3.5 %collective-permute-start.5 = (bf16[128,2048]{1,0:T(8,128)(2,1)S(1)}, bf16[128,2048]{1,0:T(8,128)(2,1)S(1)}, u32[]{:S(2)}, u32[]{:S(2)}) collective-permute-start(bf16[128,2048]{1,0:T(8,128)(2,1)S(1)} %get-tuple-element.41), channel_id=1, source_target_pairs={{0,32},{1,33},{2,34},{3,35},{4,36},{5,37},{6,38},{7,39},{8,40},{9,... | collective-permute-start | bytes 1572872 | tf_op jit(solution)/shard_map/ppermute | solution.py:41
  34.7 0.3 collective-permute-done.1
  35.0 0.0 collective-permute-done.3.refs_1_
  35.0 3.3 %collective-permute-start.4 = (bf16[256,1024]{1,0:T(8,128)(2,1)S(1)}, bf16[256,1024]{1,0:T(8,128)(2,1)S(1)}, u32[]{:S(2)}, u32[]{:S(2)}) collective-permute-start(bf16[256,1024]{1,0:T(8,128)(2,1)S(1)} %constant_dynamic-update-slice_fusion.first_ref), channel_id=1, source_target_pairs={{0,2},{1,3},{2,0},{3,1},{4,6},{5,7},{6,4},{7,5},{8,10},{9,11},{10,... | collective-permute-start | bytes 1572872 | tf_op jit(solution)/shard_map/ppermute | solution.py:41
  38.3 4.7 %collective-permute-start.7 = (f32[4096]{0:T(1024)S(1)}, f32[4096]{0:T(1024)S(1)}, u32[]{:S(2)}, u32[]{:S(2)}) collective-permute-start(f32[4096]{0:T(1024)S(1)} %add.23), channel_id=1, source_target_pairs={{0,256},{64,320},{128,384},{192,448},{256,0},{320,64},{384,128},{4... | collective-permute-start | bytes 49160 | tf_op jit(solution)/shard_map/ppermute | solution.py:130
  43.0 5.4 %collective-permute-start.8 = (bf16[256,1024]{1,0:T(8,128)(2,1)S(1)}, bf16[256,1024]{1,0:T(8,128)(2,1)S(1)}, u32[]{:S(2)}, u32[]{:S(2)}) collective-permute-start(bf16[256,1024]{1,0:T(8,128)(2,1)S(1)} %constant_dynamic-update-slice_fusion.first_ref), channel_id=1, source_target_pairs={{0,1},{1,0},{2,3},{3,2},{4,5},{5,4},{6,7},{7,6},{8,9},{9,8},{10,11... | collective-permute-start | bytes 1572872 | tf_op jit(solution)/shard_map/ppermute | solution.py:41
  48.4 0.0 collective-permute-done.7
  48.4 0.0 collective-permute-done.6.refs_3_
  48.4 0.0 collective-permute-done.5.refs_2_
  48.4 0.0 collective-permute-done.4.second_ref
  48.4 4.7 %collective-permute-start.9 = (bf16[256,1024]{1,0:T(8,128)(2,1)S(1)}, bf16[256,1024]{1,0:T(8,128)(2,1)S(1)}, u32[]{:S(2)}, u32[]{:S(2)}) collective-permute-start(bf16[256,1024]{1,0:T(8,128)(2,1)S(1)} %collective-permute-done.4.second_ref), channel_id=1, source_target_pairs={{0,1},{1,0},{2,3},{3,2},{4,5},{5,4},{6,7},{7,6},{8,9},{9,8},{10,11... | collective-permute-start | bytes 1572872 | tf_op jit(solution)/shard_map/ppermute | solution.py:41
  53.2 0.0 collective-permute-done.8.first_sib_ref
  53.2 1.5 %collective-permute-done.9.second_sib_ref = bf16[256,1024]{1,0:T(8,128)(2,1)S(1)} collective-permute-done((bf16[256,1024]{1,0:T(8,128)(2,1)S(1)}, bf16[256,1024]{1,0:T(8,128)(2,1)S(1)}, u32[]{:S(2)}, u32[]{:S(2)}) %collective-permute-start.9) | collective-permute-done | bytes 524320 | tf_op jit(solution)/shard_map/ppermute | solution.py:41
  54.7 0.0 copy-start.2
  54.7 2.5 %project.1 = (f32[128,2048]{1,0:T(8,128)S(1)}, bf16[128,2048]{1,0:T(8,128)(2,1)S(1)}, bf16[128,2048]{1,0:T(8,128)(2,1)S(1)}, bf16[128,2048]{1,0:T(8,128)(2,1)S(1)}) custom-call(bf16[256,1024]{1,0:T(8,128)(2,1)S(1)} %constant_dynamic-update-slice_fusion.first_ref, bf16[256,1024]{1,0:T(8,128)(2,1)S(1)} %collective-permute-done.4.second_ref, ...), custom_call_target="tpu_custom_call" | custom-call | flops 2147483648 | bytes 8388608 | tf_op jit(solution)/shard_map/project/pallas_call | solution.py:160
  57.2 4.5 %collective-permute-start.10 = (bf16[128,2048]{1,0:T(8,128)(2,1)S(1)}, bf16[128,2048]{1,0:T(8,128)(2,1)S(1)}, u32[]{:S(2)}, u32[]{:S(2)}) collective-permute-start(bf16[128,2048]{1,0:T(8,128)(2,1)S(1)} %get-tuple-element.54), channel_id=1, source_target_pairs={{0,32},{1,33},{2,34},{3,35},{4,36},{5,37},{6,38},{7,39},{8,40},{9,... | collective-permute-start | bytes 1572872 | tf_op jit(solution)/shard_map/ppermute | solution.py:41
  61.7 3.0 %collective-permute-start.11 = (bf16[128,2048]{1,0:T(8,128)(2,1)S(1)}, bf16[128,2048]{1,0:T(8,128)(2,1)S(1)}, u32[]{:S(2)}, u32[]{:S(2)}) collective-permute-start(bf16[128,2048]{1,0:T(8,128)(2,1)S(1)} %get-tuple-element.55), channel_id=1, source_target_pairs={{0,48},{1,49},{2,50},{3,51},{4,52},{5,53},{6,54},{7,55},{8,56},{9,... | collective-permute-start | bytes 1572872 | tf_op jit(solution)/shard_map/ppermute | solution.py:41
  64.7 2.3 %collective-permute-start.12 = (bf16[128,2048]{1,0:T(8,128)(2,1)S(1)}, bf16[128,2048]{1,0:T(8,128)(2,1)S(1)}, u32[]{:S(2)}, u32[]{:S(2)}) collective-permute-start(bf16[128,2048]{1,0:T(8,128)(2,1)S(1)} %get-tuple-element.56), channel_id=1, source_target_pairs={{0,16},{1,17},{2,18},{3,19},{4,20},{5,21},{6,22},{7,23},{8,24},{9,... | collective-permute-start | bytes 1572872 | tf_op jit(solution)/shard_map/ppermute | solution.py:41
  67.0 12.2 %collective-permute-start.13 = (f32[4096]{0:T(1024)S(1)}, f32[4096]{0:T(1024)S(1)}, u32[]{:S(2)}, u32[]{:S(2)}) collective-permute-start(f32[4096]{0:T(1024)S(1)} %add.24), channel_id=1, source_target_pairs={{0,64},{64,0},{128,192},{192,128},{256,320},{320,256},{384,448},{4... | collective-permute-start | bytes 49160 | tf_op jit(solution)/shard_map/ppermute | solution.py:130
  79.2 0.9 %dynamic-slice_multiply_fusion = f32[1,4096]{1,0:T(1,128)S(1)} fusion(f32[8,4096]{1,0:T(8,128)} %param.12, s32[]{:T(128)S(6)} %select_n.7), kind=kLoop, calls=%fused_computation.2 | loop fusion | flops 4096 | bytes 32772 | tf_op jit(solution)/shard_map/mul | solution.py:175
  80.1 0.2 collective-permute-done.13
  80.3 0.6 multiply_subtract_fusion
  80.9 0.0 collective-permute-done.10.refs_0_
  80.9 3.6 %collective-permute-done.11.refs_1_ = bf16[128,2048]{1,0:T(8,128)(2,1)S(1)} collective-permute-done((bf16[128,2048]{1,0:T(8,128)(2,1)S(1)}, bf16[128,2048]{1,0:T(8,128)(2,1)S(1)}, u32[]{:S(2)}, u32[]{:S(2)}) %collective-permute-start.11) | collective-permute-done | bytes 524320 | tf_op jit(solution)/shard_map/ppermute | solution.py:41
  84.5 1.2 %collective-permute-done.12.refs_2_ = bf16[128,2048]{1,0:T(8,128)(2,1)S(1)} collective-permute-done((bf16[128,2048]{1,0:T(8,128)(2,1)S(1)}, bf16[128,2048]{1,0:T(8,128)(2,1)S(1)}, u32[]{:S(2)}, u32[]{:S(2)}) %collective-permute-start.12) | collective-permute-done | bytes 524320 | tf_op jit(solution)/shard_map/ppermute | solution.py:41
  85.7 0.0 copy-done.2
  85.7 2.3 %finish.1 = (bf16[128,1024]{1,0:T(8,128)(2,1)}, bf16[128,4096]{1,0:T(8,128)(2,1)}) custom-call(bf16[128,4096]{1,0:T(8,128)(2,1)S(1)} %copy-done.2, f32[128,1]{1,0:T(8,128)S(1)} %get-tuple-element.32.inv_ref, f32[128,2048]{1,0:T(8,128)S(1)} %get-tuple-element.49.own_ref, bf16[128,2048]{1,0:T(8,128)(2,1)S(1)} %collective-permute-done.10.refs_0_, ...), custom_call_target="tpu_custom_call" | custom-call | flops 4194304 | bytes 5242880 | tf_op jit(solution)/shard_map/finish/pallas_call | solution.py:177
  (7 shorter events, 0.1 us)
Async XLA Ops:
  0.6 12.6 %copy-start = (f32[8,4096]{1,0:T(8,128)S(1)}, f32[8,4096]{1,0:T(8,128)}, u32[]{:S(2)}) copy-start(f32[8,4096]{1,0:T(8,128)} %param.11) | copy-start | bytes 393220
  0.6 13.5 %collective-permute-start = (bf16[64,1024]{1,0:T(8,128)(2,1)}, bf16[64,1024]{1,0:T(8,128)(2,1)S(1)}, u32[]{:S(2)}, u32[]{:S(2)}) collective-permute-start(bf16[64,1024]{1,0:T(8,128)(2,1)} %bitcast.10), channel_id=1, source_target_pairs={{0,8},{1,5},{2,10},{3,7},{4,12},{5,1},{6,14},{7,3},{8,0},{9,13},{1... | collective-permute-start | bytes 393224 | tf_op jit(solution)/shard_map/ppermute | solution.py:41
  6.5 1.2 %copy-start.1 = (bf16[128,4096]{1,0:T(8,128)(2,1)S(1)}, bf16[128,4096]{1,0:T(8,128)(2,1)}, u32[]{:S(2)}) copy-start(bf16[128,4096]{1,0:T(8,128)(2,1)} %tok_ref.3) | copy-start | bytes 3145732
  7.7 0.9 %copy-start.3 = (bf16[128,1024]{1,0:T(8,128)(2,1)S(1)}, bf16[128,1024]{1,0:T(8,128)(2,1)}, u32[]{:S(2)}) copy-start(bf16[128,1024]{1,0:T(8,128)(2,1)} %cot_ref.1) | copy-start | bytes 786436
  9.2 4.9 %copy-start.4 = (bf16[1,64,1024]{2,1,0:T(8,128)(2,1)S(1)}, bf16[1,64,1024]{2,1,0:T(8,128)(2,1)}, u32[]{:S(2)}) copy-start(bf16[1,64,1024]{2,1,0:T(8,128)(2,1)} %param.8) | copy-start | bytes 393220
  9.2 25.8 %collective-permute-start.3 = (bf16[128,2048]{1,0:T(8,128)(2,1)S(1)}, bf16[128,2048]{1,0:T(8,128)(2,1)S(1)}, u32[]{:S(2)}, u32[]{:S(2)}) collective-permute-start(bf16[128,2048]{1,0:T(8,128)(2,1)S(1)} %get-tuple-element.39), channel_id=1, source_target_pairs={{0,16},{1,17},{2,18},{3,19},{4,20},{5,21},{6,22},{7,23},{8,24},{9,... | collective-permute-start | bytes 1572872 | tf_op jit(solution)/shard_map/ppermute | solution.py:41
  14.2 20.8 %collective-permute-start.1 = (bf16[128,1024]{1,0:T(8,128)(2,1)S(1)}, bf16[128,1024]{1,0:T(8,128)(2,1)S(1)}, u32[]{:S(2)}, u32[]{:S(2)}) collective-permute-start(bf16[128,1024]{1,0:T(8,128)(2,1)S(1)} %pad_maximum_fusion), channel_id=1, source_target_pairs={{0,4},{1,9},{2,6},{3,11},{4,0},{5,13},{6,2},{7,15},{8,12},{9,1},{1... | collective-permute-start | bytes 786440 | tf_op jit(solution)/shard_map/ppermute | solution.py:41
  23.0 25.4 %collective-permute-start.6 = (bf16[128,2048]{1,0:T(8,128)(2,1)S(1)}, bf16[128,2048]{1,0:T(8,128)(2,1)S(1)}, u32[]{:S(2)}, u32[]{:S(2)}) collective-permute-start(bf16[128,2048]{1,0:T(8,128)(2,1)S(1)} %get-tuple-element.42), channel_id=1, source_target_pairs={{0,48},{1,49},{2,50},{3,51},{4,52},{5,53},{6,54},{7,55},{8,56},{9,... | collective-permute-start | bytes 1572872 | tf_op jit(solution)/shard_map/ppermute | solution.py:41
  26.4 4.8 %collective-permute-start.2 = (f32[4096]{0:T(1024)S(1)}, f32[4096]{0:T(1024)S(1)}, u32[]{:S(2)}, u32[]{:S(2)}) collective-permute-start(f32[4096]{0:T(1024)S(1)} %sub.6), channel_id=1, source_target_pairs={{0,128},{64,192},{128,0},{192,64},{256,384},{320,448},{384,256},{4... | collective-permute-start | bytes 49160 | tf_op jit(solution)/shard_map/ppermute | solution.py:130
  31.2 17.2 %collective-permute-start.5 = (bf16[128,2048]{1,0:T(8,128)(2,1)S(1)}, bf16[128,2048]{1,0:T(8,128)(2,1)S(1)}, u32[]{:S(2)}, u32[]{:S(2)}) collective-permute-start(bf16[128,2048]{1,0:T(8,128)(2,1)S(1)} %get-tuple-element.41), channel_id=1, source_target_pairs={{0,32},{1,33},{2,34},{3,35},{4,36},{5,37},{6,38},{7,39},{8,40},{9,... | collective-permute-start | bytes 1572872 | tf_op jit(solution)/shard_map/ppermute | solution.py:41
  35.0 13.4 %collective-permute-start.4 = (bf16[256,1024]{1,0:T(8,128)(2,1)S(1)}, bf16[256,1024]{1,0:T(8,128)(2,1)S(1)}, u32[]{:S(2)}, u32[]{:S(2)}) collective-permute-start(bf16[256,1024]{1,0:T(8,128)(2,1)S(1)} %constant_dynamic-update-slice_fusion.first_ref), channel_id=1, source_target_pairs={{0,2},{1,3},{2,0},{3,1},{4,6},{5,7},{6,4},{7,5},{8,10},{9,11},{10,... | collective-permute-start | bytes 1572872 | tf_op jit(solution)/shard_map/ppermute | solution.py:41
  38.3 10.1 %collective-permute-start.7 = (f32[4096]{0:T(1024)S(1)}, f32[4096]{0:T(1024)S(1)}, u32[]{:S(2)}, u32[]{:S(2)}) collective-permute-start(f32[4096]{0:T(1024)S(1)} %add.23), channel_id=1, source_target_pairs={{0,256},{64,320},{128,384},{192,448},{256,0},{320,64},{384,128},{4... | collective-permute-start | bytes 49160 | tf_op jit(solution)/shard_map/ppermute | solution.py:130
  43.0 10.2 %collective-permute-start.8 = (bf16[256,1024]{1,0:T(8,128)(2,1)S(1)}, bf16[256,1024]{1,0:T(8,128)(2,1)S(1)}, u32[]{:S(2)}, u32[]{:S(2)}) collective-permute-start(bf16[256,1024]{1,0:T(8,128)(2,1)S(1)} %constant_dynamic-update-slice_fusion.first_ref), channel_id=1, source_target_pairs={{0,1},{1,0},{2,3},{3,2},{4,5},{5,4},{6,7},{7,6},{8,9},{9,8},{10,11... | collective-permute-start | bytes 1572872 | tf_op jit(solution)/shard_map/ppermute | solution.py:41
  48.4 6.3 %collective-permute-start.9 = (bf16[256,1024]{1,0:T(8,128)(2,1)S(1)}, bf16[256,1024]{1,0:T(8,128)(2,1)S(1)}, u32[]{:S(2)}, u32[]{:S(2)}) collective-permute-start(bf16[256,1024]{1,0:T(8,128)(2,1)S(1)} %collective-permute-done.4.second_ref), channel_id=1, source_target_pairs={{0,1},{1,0},{2,3},{3,2},{4,5},{5,4},{6,7},{7,6},{8,9},{9,8},{10,11... | collective-permute-start | bytes 1572872 | tf_op jit(solution)/shard_map/ppermute | solution.py:41
  54.7 31.0 %copy-start.2 = (bf16[128,4096]{1,0:T(8,128)(2,1)S(1)}, bf16[128,4096]{1,0:T(8,128)(2,1)}, u32[]{:S(2)}) copy-start(bf16[128,4096]{1,0:T(8,128)(2,1)} %tok_ref.3) | copy-start | bytes 3145732
  57.2 23.7 %collective-permute-start.10 = (bf16[128,2048]{1,0:T(8,128)(2,1)S(1)}, bf16[128,2048]{1,0:T(8,128)(2,1)S(1)}, u32[]{:S(2)}, u32[]{:S(2)}) collective-permute-start(bf16[128,2048]{1,0:T(8,128)(2,1)S(1)} %get-tuple-element.54), channel_id=1, source_target_pairs={{0,32},{1,33},{2,34},{3,35},{4,36},{5,37},{6,38},{7,39},{8,40},{9,... | collective-permute-start | bytes 1572872 | tf_op jit(solution)/shard_map/ppermute | solution.py:41
  61.7 22.8 %collective-permute-start.11 = (bf16[128,2048]{1,0:T(8,128)(2,1)S(1)}, bf16[128,2048]{1,0:T(8,128)(2,1)S(1)}, u32[]{:S(2)}, u32[]{:S(2)}) collective-permute-start(bf16[128,2048]{1,0:T(8,128)(2,1)S(1)} %get-tuple-element.55), channel_id=1, source_target_pairs={{0,48},{1,49},{2,50},{3,51},{4,52},{5,53},{6,54},{7,55},{8,56},{9,... | collective-permute-start | bytes 1572872 | tf_op jit(solution)/shard_map/ppermute | solution.py:41
  64.7 21.0 %collective-permute-start.12 = (bf16[128,2048]{1,0:T(8,128)(2,1)S(1)}, bf16[128,2048]{1,0:T(8,128)(2,1)S(1)}, u32[]{:S(2)}, u32[]{:S(2)}) collective-permute-start(bf16[128,2048]{1,0:T(8,128)(2,1)S(1)} %get-tuple-element.56), channel_id=1, source_target_pairs={{0,16},{1,17},{2,18},{3,19},{4,20},{5,21},{6,22},{7,23},{8,24},{9,... | collective-permute-start | bytes 1572872 | tf_op jit(solution)/shard_map/ppermute | solution.py:41
  67.0 13.3 %collective-permute-start.13 = (f32[4096]{0:T(1024)S(1)}, f32[4096]{0:T(1024)S(1)}, u32[]{:S(2)}, u32[]{:S(2)}) collective-permute-start(f32[4096]{0:T(1024)S(1)} %add.24), channel_id=1, source_target_pairs={{0,64},{64,0},{128,192},{192,128},{256,320},{320,256},{384,448},{4... | collective-permute-start | bytes 49160 | tf_op jit(solution)/shard_map/ppermute | solution.py:130

commit v4 on v3

--- a/solution.py
+++ b/solution.py
@@ -13,6 +13,7 @@
 EVEN = ((0, 4, 2, 6), (0, 2, 4, 6))
 ODD = ((1, 5, 3, 7), (1, 3, 5, 7))
 WIDE = 1024
+HALF = WIDE // 2
 MIB = 1 << 20
 
 
@@ -61,61 +62,100 @@
         out_ref[:, WIDE:] = cot_ref[...]
 
 
-def project_kernel(first_ref, second_ref, first_sib_ref, second_sib_ref, *refs):
-    ins, (own_ref, *outs), (weight_ref, act_ref) = refs[:NY], refs[NY : 2 * NY], refs[2 * NY :]
+def half_of_features(mine_ref, sib_ref, order, acts, weight_ref, lhs_ref):
     _, z, c = place()
-    rows = ins[0].shape[0]
-    for sib, pair in enumerate(((first_ref, second_ref), (first_sib_ref, second_sib_ref))):
+    rows = acts[0].shape[0]
+    for sib, ref in enumerate((mine_ref, sib_ref)):
         core = lax.rem(c + sib, NC)
-        for order, ref in zip((EVEN, ODD), pair):
-            for i in range(4):
-                dz = jnp.where(core == 0, order[0][i], order[1][i])
-                at = pl.multiple_of(jnp.bitwise_xor(z, dz) * 128 + core * 64, 64)
-                weight_ref[pl.ds(at, 64)] = ref[64 * i : 64 * (i + 1)]
-    for n, ref in enumerate(ins):
-        act_ref[rows * n : rows * (n + 1)] = ref[...]
-    for half in range(2):
-        for i in range(WIDE // 256):
-            cols = slice(256 * i, 256 * (i + 1))
-            if half == 0:
-                part = jnp.dot(act_ref[:, :WIDE], weight_ref[:, cols], preferred_element_type=jnp.float32)
-            else:
-                part = lax.dot_general(
-                    act_ref[:, WIDE:],
-                    weight_ref[cols],
-                    (((1,), (1,)), ((), ())),
-                    preferred_element_type=jnp.float32,
-                )
-            cols = slice(WIDE * half + 256 * i, WIDE * half + 256 * (i + 1))
-            own_ref[:, cols] = part[:rows]
+        for i in range(4):
+            chip = jnp.bitwise_xor(z, jnp.where(core == 0, order[0][i], order[1][i]))
+            at = pl.multiple_of(chip // 2 * 128 + core * 64, 64)
+            weight_ref[pl.ds(at, 64)] = ref[64 * i : 64 * (i + 1)]
+    odd = lax.rem(z + order[0][0], 2)
+    for n, ref in enumerate(acts):
+        lhs_ref[rows * n : rows * (n + 1), HALF:] = ref[:, WIDE:]
+        for i in range(4):
+            cols = pl.ds(pl.multiple_of((2 * i + odd) * 128, 128), 128)
+            lhs_ref[rows * n : rows * (n + 1), 128 * i : 128 * (i + 1)] = ref[:, cols]
+
+
+def first_kernel(mine_ref, sib_ref, *refs):
+    acts, (kv_ref, own_ref, *outs), (weight_ref, lhs_ref) = refs[:NY], refs[NY:-2], refs[-2:]
+    rows = acts[0].shape[0]
+    half_of_features(mine_ref, sib_ref, EVEN, acts, weight_ref, lhs_ref)
+    for i in range(HALF // 256):
+        cols = slice(256 * i, 256 * (i + 1))
+        part = lax.dot_general(
+            lhs_ref[:, HALF:], weight_ref[cols], (((1,), (1,)), ((), ())), preferred_element_type=jnp.float32
+        )
+        own_ref[:, cols] = part[:rows]
+        for n, out_ref in enumerate(outs, 1):
+            out_ref[:, cols] = part[rows * n : rows * (n + 1)].astype(jnp.bfloat16)
+    for i in range(WIDE // 256):
+        cols = slice(256 * i, 256 * (i + 1))
+        kv_ref[:, cols] = jnp.dot(lhs_ref[:, :HALF], weight_ref[:, cols], preferred_element_type=jnp.float32)
+
+
+def second_kernel(mine_ref, sib_ref, kv_ref, *refs):
+    acts, firsts, (own_ref, *outs), (weight_ref, lhs_ref) = (
+        refs[:NY], refs[NY : 2 * NY], refs[2 * NY : -2], refs[-2:]
+    )
+    _, z, _ = place()
+    rows = acts[0].shape[0]
+    half_of_features(mine_ref, sib_ref, ODD, acts, weight_ref, lhs_ref)
+    for i in range(WIDE // 256):
+        cols = slice(256 * i, 256 * (i + 1))
+        part = kv_ref[:, cols] + jnp.dot(
+            lhs_ref[:, :HALF], weight_ref[:, cols], preferred_element_type=jnp.float32
+        )
+        own_ref[:, cols] = part[:rows]
+        for n, out_ref in enumerate(outs, 1):
+            out_ref[:, cols] = part[rows * n : rows * (n + 1)].astype(jnp.bfloat16)
+    even, odd = lax.rem(z, 2), lax.rem(z + 1, 2)
+    for i in range(HALF // 128):
+        cols = pl.ds(pl.multiple_of(WIDE + (2 * i + even) * 128, 128), 128)
+        for out_ref, first_ref in zip((own_ref, *outs), firsts):
+            out_ref[:, cols] = first_ref[:, 128 * i : 128 * (i + 1)]
+    for i in range(HALF // 256):
+        part = lax.dot_general(
+            lhs_ref[:, HALF:],
+            weight_ref[256 * i : 256 * (i + 1)],
+            (((1,), (1,)), ((), ())),
+            preferred_element_type=jnp.float32,
+        )
+        for k in range(2):
+            cols = pl.ds(pl.multiple_of(WIDE + (4 * i + 2 * k + odd) * 128, 128), 128)
+            turn = part[:, 128 * k : 128 * (k + 1)]
+            own_ref[:, cols] = turn[:rows]
             for n, out_ref in enumerate(outs, 1):
-                out_ref[:, cols] = part[rows * n : rows * (n + 1)].astype(jnp.bfloat16)
+                out_ref[:, cols] = turn[rows * n : rows * (n + 1)].astype(jnp.bfloat16)
 
 
 def finish_kernel(tok_ref, inv_ref, own_ref, *refs):
-    gots, (kv_ref, grad_ref, full_ref) = refs[: NY - 1], refs[NY - 1 :]
+    gots, (kv_ref, grad_ref) = refs[: NY - 1], refs[NY - 1 :]
     y, _, _ = place()
     inv = inv_ref[...]
     kv = own_ref[:, :WIDE]
     for ref in gots:
         kv += ref[:, :WIDE].astype(jnp.float32)
     kv_ref[...] = kv.astype(jnp.bfloat16)
+    sources = list(zip((0, 2, 1, 3), (own_ref, *gots)))
     inner = 0.0
-    for step, ref in zip((0, 2, 1, 3), (own_ref, *gots)):
-        cols = slab(y, step)
+    for step, ref in sources:
+        normed = tok_ref[:, slab(y, step)].astype(jnp.float32) * inv
+        inner += jnp.sum(ref[:, WIDE:].astype(jnp.float32) * normed, axis=1, keepdims=True)
+    inner = inner / tok_ref.shape[1]
+    for step, ref in sources:
+        normed = tok_ref[:, slab(y, step)].astype(jnp.float32) * inv
         grad = ref[:, WIDE:].astype(jnp.float32)
-        full_ref[:, cols] = grad
-        inner += jnp.sum(grad * (tok_ref[:, cols].astype(jnp.float32) * inv), axis=1, keepdims=True)
-    inner = inner / tok_ref.shape[1]
-    normed = tok_ref[...].astype(jnp.float32) * inv
-    grad_ref[...] = (inv * (full_ref[...] - normed * inner)).astype(jnp.bfloat16)
+        grad_ref[:, slab(y, step)] = (inv * (grad - normed * inner)).astype(jnp.bfloat16)
 
 
 def local(tokens, kv_weight, kv_cotangent, fragment_index, anchor, momentum, replica_frag):
     rows, width = tokens.shape
     shard = kv_weight[0]
     tie = lax.optimization_barrier
-    params = pltpu.CompilerParams(vmem_limit_bytes=40 * MIB)
+    params = pltpu.CompilerParams(vmem_limit_bytes=24 * MIB)
 
     frag_pick = fragment_index[0]
     anchor_now = lax.dynamic_index_in_dim(anchor, frag_pick, 0, keepdims=False)
@@ -153,21 +193,30 @@
     second = send(first, to_z(1, 1))
     first_sib = send(first, to_core)
     drift = add_half(drift, 4)
-    second, act2, act3, drift = tie((second, act2, act3, drift))
+    second, first_sib, act2, act3, drift = tie((second, first_sib, act2, act3, drift))
     acts = [acts[0], act1, act2, act3]
     second_sib = send(second, to_core)
-    weights = (first, second, first_sib, second_sib)
+    scratch = [pltpu.VMEM((HALF, WIDE), jnp.bfloat16), pltpu.VMEM((NY * rows, HALF + WIDE), jnp.bfloat16)]
+    kv_first, own_first, *grads_first = pl.pallas_call(
+        first_kernel,
+        out_shape=(
+            jax.ShapeDtypeStruct((NY * rows, WIDE), jnp.float32),
+            jax.ShapeDtypeStruct((rows, HALF), jnp.float32),
+        )
+        + (jax.ShapeDtypeStruct((rows, HALF), jnp.bfloat16),) * (NY - 1),
+        scratch_shapes=scratch,
+        compiler_params=params,
+        cost_estimate=pl.CostEstimate(flops=2**30, bytes_accessed=8 * MIB, transcendentals=0),
+        name="first_half",
+    )(first, first_sib, *acts)
     own, *backs = pl.pallas_call(
-        project_kernel,
+        second_kernel,
         out_shape=(jax.ShapeDtypeStruct((rows, 2 * WIDE), jnp.float32),) + (block,) * (NY - 1),
-        scratch_shapes=[
-            pltpu.VMEM((WIDE, WIDE), jnp.bfloat16),
-            pltpu.VMEM((NY * rows, 2 * WIDE), jnp.bfloat16),
-        ],
-        compiler_params=params,
-        cost_estimate=pl.CostEstimate(flops=2**31, bytes_accessed=8 * MIB, transcendentals=0),
-        name="project",
-    )(*weights, *acts)
+        scratch_shapes=scratch,
+        compiler_params=params,
+        cost_estimate=pl.CostEstimate(flops=2**30, bytes_accessed=8 * MIB, transcendentals=0),
+        name="second_half",
+    )(second, second_sib, kv_first, *acts, own_first, *grads_first)
     drift, *backs = tie((drift, *backs))
     gots = [send(backs[n - 1], to_y(-n)) for n in (2, 1, 3)]
     drift = add_half(drift, 1)
@@ -180,7 +229,6 @@
             jax.ShapeDtypeStruct((rows, WIDE), jnp.bfloat16),
             jax.ShapeDtypeStruct((rows, width), jnp.bfloat16),
         ),
-        scratch_shapes=[pltpu.VMEM((rows, width), jnp.float32)],
         compiler_params=params,
         cost_estimate=pl.CostEstimate(flops=2**22, bytes_accessed=5 * MIB, transcendentals=0),
         name="finish",

time: 88.6 us -> 88 us (level)
  starting transfers between devices: 68 us -> 66.7 us
  other arithmetic: 2.44 us -> 3.35 us
    ppermute x11, waiting for transfers between devices: 6.58 us -> 4.97 us  [send(): return lax.ppermute(x, 'fsdp', pairs)]
    ppermute x11, starting transfers between devices: 48.1 us -> 46.7 us  [send(): return lax.ppermute(x, 'fsdp', pairs)]
    ppermute x3, waiting for transfers between devices: 1.81 us -> 3.23 us  [add_half(): lax.ppermute(drift, 'rep', [(r, r ^ bit) for r in range(replicas)])]
    concatenate x1, other arithmetic: 0.02 us -> 0.92 us  [local(): pair = jnp.concatenate([shard, far], axis=0)]
    pallas_call x1 -> x2, Pallas kernels: 2.49 us -> 2.79 us  [the longest x1 1.4 us: local(): pl.pallas_call(first_kernel, out_shape=(jax.ShapeDtypeStruct((NY * rows,...]
    unnamed x11 -> x9, local copies, waits for them, and re-layouts: 2.21 us -> 2.2 us
  transfers between devices with their start and end apart: 14 -> 14, of which waited for: 6 -> 7; matrix products, arithmetic and copies ran while one was open for 3% -> 4% of each run, Pallas kernels for 1% -> 2%
where the time goes in v4:
time: 88 us; the launch traced here: 87.4 us
  starting transfers between devices  66.7 us (76%)
  waiting for transfers between devices  8.2 us (9%)
  Pallas kernels  5.36 us (6%)
  other arithmetic  3.35 us (4%)
  local copies, waits for them, and re-layouts  2.24 us (3%)
  between operations  1.52 us (2%)
    ppermute x11, starting transfers between devices, send(): return lax.ppermute(x, 'fsdp', pairs)  46.7 us
    ppermute x3, starting transfers between devices, add_half(): lax.ppermute(drift, 'rep', [(r, r ^ bit) for r in range(replicas)])  20 us
    ppermute x11, waiting for transfers between devices, send(): return lax.ppermute(x, 'fsdp', pairs)  4.97 us
    ppermute x3, waiting for transfers between devices, add_half(): lax.ppermute(drift, 'rep', [(r, r ^ bit) for r in range(replicas)])  3.23 us
    unnamed x9, local copies, waits for them, and re-layouts  2.2 us
    pallas_call x1, Pallas kernels, local(): pl.pallas_call(finish_kernel, out_shape=(jax.ShapeDtypeStruct((rows, WIDE...  2.06 us
  transfers between devices with their start and end apart: 14, of which 7 were waited for; matrix products, arithmetic and copies ran while one was open for 4% of the time, Pallas kernels for 2%

profile of v4, /device:TPU:1, one launch (start us, length us, event | category | flops | bytes accessed | tf_op | source)
XLA Modules:
  0.0 87.4 jit_solution(14342047608765428760)
XLA Ops:
  0.6 0.0 copy-start
  0.6 5.9 %collective-permute-start = (bf16[64,1024]{1,0:T(8,128)(2,1)}, bf16[64,1024]{1,0:T(8,128)(2,1)S(1)}, u32[]{:S(2)}, u32[]{:S(2)}) collective-permute-start(bf16[64,1024]{1,0:T(8,128)(2,1)} %bitcast.10), channel_id=1, source_target_pairs={{0,8},{1,5},{2,10},{3,7},{4,12},{5,1},{6,14},{7,3},{8,0},{9,13},{1... | collective-permute-start | bytes 393224 | tf_op jit(solution)/shard_map/ppermute | solution.py:42
  6.5 0.0 copy-start.1
  6.5 1.2 %copy-done.1 = bf16[128,4096]{1,0:T(8,128)(2,1)S(1)} copy-done((bf16[128,4096]{1,0:T(8,128)(2,1)S(1)}, bf16[128,4096]{1,0:T(8,128)(2,1)}, u32[]{:S(2)}) %copy-start.1) | copy-done | bytes 1048600
  7.7 0.0 copy-start.3
  7.7 0.9 %copy-done.3 = bf16[128,1024]{1,0:T(8,128)(2,1)S(1)} copy-done((bf16[128,1024]{1,0:T(8,128)(2,1)S(1)}, bf16[128,1024]{1,0:T(8,128)(2,1)}, u32[]{:S(2)}) %copy-start.3) | copy-done | bytes 262168
  8.7 0.5 prepare.1
  9.2 3.2 %collective-permute-start.3 = (bf16[128,2048]{1,0:T(8,128)(2,1)S(1)}, bf16[128,2048]{1,0:T(8,128)(2,1)S(1)}, u32[]{:S(2)}, u32[]{:S(2)}) collective-permute-start(bf16[128,2048]{1,0:T(8,128)(2,1)S(1)} %get-tuple-element.45), channel_id=1, source_target_pairs={{0,16},{1,17},{2,18},{3,19},{4,20},{5,21},{6,22},{7,23},{8,24},{9,... | collective-permute-start | bytes 1572872 | tf_op jit(solution)/shard_map/ppermute | solution.py:42
  13.1 0.0 copy-done
  13.1 0.9 dynamic-slice_convert_fusion
  14.0 0.0 collective-permute-done
  14.0 0.9 %pad_maximum_fusion = bf16[128,1024]{1,0:T(8,128)(2,1)S(1)} fusion(bf16[64,1024]{1,0:T(8,128)(2,1)S(1)} %collective-permute-done, bf16[64,1024]{1,0:T(8,128)(2,1)} %bitcast.11), kind=kLoop, calls=%fused_computation | loop fusion | flops 524288 | bytes 524288 | tf_op jit(solution)/shard_map/concatenate | solution.py:185
  14.9 8.8 %collective-permute-start.1 = (bf16[128,1024]{1,0:T(8,128)(2,1)S(1)}, bf16[128,1024]{1,0:T(8,128)(2,1)S(1)}, u32[]{:S(2)}, u32[]{:S(2)}) collective-permute-start(bf16[128,1024]{1,0:T(8,128)(2,1)S(1)} %pad_maximum_fusion), channel_id=1, source_target_pairs={{0,4},{1,9},{2,6},{3,11},{4,0},{5,13},{6,2},{7,15},{8,12},{9,1},{1... | collective-permute-start | bytes 786440 | tf_op jit(solution)/shard_map/ppermute | solution.py:42
  23.7 3.4 %collective-permute-start.7 = (bf16[128,2048]{1,0:T(8,128)(2,1)S(1)}, bf16[128,2048]{1,0:T(8,128)(2,1)S(1)}, u32[]{:S(2)}, u32[]{:S(2)}) collective-permute-start(bf16[128,2048]{1,0:T(8,128)(2,1)S(1)} %get-tuple-element.48), channel_id=1, source_target_pairs={{0,48},{1,49},{2,50},{3,51},{4,52},{5,53},{6,54},{7,55},{8,56},{9,... | collective-permute-start | bytes 1572872 | tf_op jit(solution)/shard_map/ppermute | solution.py:42
  27.2 3.1 %collective-permute-start.2 = (f32[4096]{0:T(1024)S(1)}, f32[4096]{0:T(1024)S(1)}, u32[]{:S(2)}, u32[]{:S(2)}) collective-permute-start(f32[4096]{0:T(1024)S(1)} %sub.6), channel_id=1, source_target_pairs={{0,128},{64,192},{128,0},{192,64},{256,384},{320,448},{384,256},{4... | collective-permute-start | bytes 49160 | tf_op jit(solution)/shard_map/ppermute | solution.py:170
  30.3 1.6 %collective-permute-done.2 = f32[4096]{0:T(1024)S(1)} collective-permute-done((f32[4096]{0:T(1024)S(1)}, f32[4096]{0:T(1024)S(1)}, u32[]{:S(2)}, u32[]{:S(2)}) %collective-permute-start.2) | collective-permute-done | bytes 16416 | tf_op jit(solution)/shard_map/ppermute | solution.py:170
  32.0 3.5 %collective-permute-start.6 = (bf16[128,2048]{1,0:T(8,128)(2,1)S(1)}, bf16[128,2048]{1,0:T(8,128)(2,1)S(1)}, u32[]{:S(2)}, u32[]{:S(2)}) collective-permute-start(bf16[128,2048]{1,0:T(8,128)(2,1)S(1)} %get-tuple-element.47), channel_id=1, source_target_pairs={{0,32},{1,33},{2,34},{3,35},{4,36},{5,37},{6,38},{7,39},{8,40},{9,... | collective-permute-start | bytes 1572872 | tf_op jit(solution)/shard_map/ppermute | solution.py:42
  35.4 0.3 collective-permute-done.1
  35.8 0.0 collective-permute-done.3.refs_1_
  35.8 3.3 %collective-permute-start.4 = (bf16[256,1024]{1,0:T(8,128)(2,1)S(1)}, bf16[256,1024]{1,0:T(8,128)(2,1)S(1)}, u32[]{:S(2)}, u32[]{:S(2)}) collective-permute-start(bf16[256,1024]{1,0:T(8,128)(2,1)S(1)} %constant_dynamic-update-slice_fusion.mine_ref), channel_id=1, source_target_pairs={{0,2},{1,3},{2,0},{3,1},{4,6},{5,7},{6,4},{7,5},{8,10},{9,11},{10,... | collective-permute-start | bytes 1572872 | tf_op jit(solution)/shard_map/ppermute | solution.py:42
  39.0 5.1 %collective-permute-start.5 = (bf16[256,1024]{1,0:T(8,128)(2,1)S(1)}, bf16[256,1024]{1,0:T(8,128)(2,1)S(1)}, u32[]{:S(2)}, u32[]{:S(2)}) collective-permute-start(bf16[256,1024]{1,0:T(8,128)(2,1)S(1)} %constant_dynamic-update-slice_fusion.mine_ref), channel_id=1, source_target_pairs={{0,1},{1,0},{2,3},{3,2},{4,5},{5,4},{6,7},{7,6},{8,9},{9,8},{10,11... | collective-permute-start | bytes 1572872 | tf_op jit(solution)/shard_map/ppermute | solution.py:42
  44.2 4.7 %collective-permute-start.8 = (f32[4096]{0:T(1024)S(1)}, f32[4096]{0:T(1024)S(1)}, u32[]{:S(2)}, u32[]{:S(2)}) collective-permute-start(f32[4096]{0:T(1024)S(1)} %add.23), channel_id=1, source_target_pairs={{0,256},{64,320},{128,384},{192,448},{256,0},{320,64},{384,128},{4... | collective-permute-start | bytes 49160 | tf_op jit(solution)/shard_map/ppermute | solution.py:170
  48.8 1.3 %collective-permute-done.8 = f32[4096]{0:T(1024)S(1)} collective-permute-done((f32[4096]{0:T(1024)S(1)}, f32[4096]{0:T(1024)S(1)}, u32[]{:S(2)}, u32[]{:S(2)}) %collective-permute-start.8) | collective-permute-done | bytes 16416 | tf_op jit(solution)/shard_map/ppermute | solution.py:170
  50.2 0.0 collective-permute-done.7.refs_3_
  50.2 0.0 collective-permute-done.6.refs_2_
  50.2 0.0 collective-permute-done.4.mine_ref
  50.2 0.0 collective-permute-done.5.sib_ref
  50.2 3.7 %collective-permute-start.9 = (bf16[256,1024]{1,0:T(8,128)(2,1)S(1)}, bf16[256,1024]{1,0:T(8,128)(2,1)S(1)}, u32[]{:S(2)}, u32[]{:S(2)}) collective-permute-start(bf16[256,1024]{1,0:T(8,128)(2,1)S(1)} %collective-permute-done.4.mine_ref), channel_id=1, source_target_pairs={{0,1},{1,0},{2,3},{3,2},{4,5},{5,4},{6,7},{7,6},{8,9},{9,8},{10,11... | collective-permute-start | bytes 1572872 | tf_op jit(solution)/shard_map/ppermute | solution.py:42
  53.9 1.4 %first_half.1 = (f32[512,1024]{1,0:T(8,128)S(1)}, f32[128,512]{1,0:T(8,128)S(1)}, bf16[128,512]{1,0:T(8,128)(2,1)S(1)}, bf16[128,512]{1,0:T(8,128)(2,1)S(1)}, bf16[128,512]{1,0:T(8,128)(2,1)S(1)}) custom-call(bf16[256,1024]{1,0:T(8,128)(2,1)S(1)} %constant_dynamic-update-slice_fusion.mine_ref, bf16[256,1024]{1,0:T(8,128)(2,1)S(1)} %collective-permute-done.5.sib_ref, ...), custom_call_target="tpu_custom_call" | custom-call | flops 1073741824 | bytes 8388608 | tf_op jit(solution)/shard_map/first_half/pallas_call | solution.py:200
  55.3 0.1 collective-permute-done.9.sib_ref
  55.4 0.0 copy-start.2
  55.4 1.4 %second_half.1 = (f32[128,2048]{1,0:T(8,128)S(1)}, bf16[128,2048]{1,0:T(8,128)(2,1)S(1)}, bf16[128,2048]{1,0:T(8,128)(2,1)S(1)}, bf16[128,2048]{1,0:T(8,128)(2,1)S(1)}) custom-call(bf16[256,1024]{1,0:T(8,128)(2,1)S(1)} %collective-permute-done.4.mine_ref, bf16[256,1024]{1,0:T(8,128)(2,1)S(1)} %collective-permute-done.9.sib_ref, ...), custom_call_target="tpu_custom_call" | custom-call | flops 1073741824 | bytes 8388608 | tf_op jit(solution)/shard_map/second_half/pallas_call | solution.py:212
  56.8 4.5 %collective-permute-start.10 = (bf16[128,2048]{1,0:T(8,128)(2,1)S(1)}, bf16[128,2048]{1,0:T(8,128)(2,1)S(1)}, u32[]{:S(2)}, u32[]{:S(2)}) collective-permute-start(bf16[128,2048]{1,0:T(8,128)(2,1)S(1)} %get-tuple-element.66), channel_id=1, source_target_pairs={{0,32},{1,33},{2,34},{3,35},{4,36},{5,37},{6,38},{7,39},{8,40},{9,... | collective-permute-start | bytes 1572872 | tf_op jit(solution)/shard_map/ppermute | solution.py:42
  61.4 3.0 %collective-permute-start.11 = (bf16[128,2048]{1,0:T(8,128)(2,1)S(1)}, bf16[128,2048]{1,0:T(8,128)(2,1)S(1)}, u32[]{:S(2)}, u32[]{:S(2)}) collective-permute-start(bf16[128,2048]{1,0:T(8,128)(2,1)S(1)} %get-tuple-element.67), channel_id=1, source_target_pairs={{0,48},{1,49},{2,50},{3,51},{4,52},{5,53},{6,54},{7,55},{8,56},{9,... | collective-permute-start | bytes 1572872 | tf_op jit(solution)/shard_map/ppermute | solution.py:42
  64.4 2.3 %collective-permute-start.12 = (bf16[128,2048]{1,0:T(8,128)(2,1)S(1)}, bf16[128,2048]{1,0:T(8,128)(2,1)S(1)}, u32[]{:S(2)}, u32[]{:S(2)}) collective-permute-start(bf16[128,2048]{1,0:T(8,128)(2,1)S(1)} %get-tuple-element.68), channel_id=1, source_target_pairs={{0,16},{1,17},{2,18},{3,19},{4,20},{5,21},{6,22},{7,23},{8,24},{9,... | collective-permute-start | bytes 1572872 | tf_op jit(solution)/shard_map/ppermute | solution.py:42
  66.7 12.3 %collective-permute-start.13 = (f32[4096]{0:T(1024)S(1)}, f32[4096]{0:T(1024)S(1)}, u32[]{:S(2)}, u32[]{:S(2)}) collective-permute-start(f32[4096]{0:T(1024)S(1)} %add.24), channel_id=1, source_target_pairs={{0,64},{64,0},{128,192},{192,128},{256,320},{320,256},{384,448},{4... | collective-permute-start | bytes 49160 | tf_op jit(solution)/shard_map/ppermute | solution.py:170
  78.9 0.9 %dynamic-slice_multiply_fusion = f32[1,4096]{1,0:T(1,128)S(1)} fusion(f32[8,4096]{1,0:T(8,128)} %param.12, s32[]{:T(128)S(6)} %select_n.7), kind=kLoop, calls=%fused_computation.2 | loop fusion | flops 4096 | bytes 32772 | tf_op jit(solution)/shard_map/mul | solution.py:224
  79.9 0.3 collective-permute-done.13
  80.2 0.6 multiply_subtract_fusion
  80.8 0.0 collective-permute-done.10.refs_0_
  80.8 3.4 %collective-permute-done.11.refs_1_ = bf16[128,2048]{1,0:T(8,128)(2,1)S(1)} collective-permute-done((bf16[128,2048]{1,0:T(8,128)(2,1)S(1)}, bf16[128,2048]{1,0:T(8,128)(2,1)S(1)}, u32[]{:S(2)}, u32[]{:S(2)}) %collective-permute-start.11) | collective-permute-done | bytes 524320 | tf_op jit(solution)/shard_map/ppermute | solution.py:42
  84.2 1.1 %collective-permute-done.12.refs_2_ = bf16[128,2048]{1,0:T(8,128)(2,1)S(1)} collective-permute-done((bf16[128,2048]{1,0:T(8,128)(2,1)S(1)}, bf16[128,2048]{1,0:T(8,128)(2,1)S(1)}, u32[]{:S(2)}, u32[]{:S(2)}) %collective-permute-start.12) | collective-permute-done | bytes 524320 | tf_op jit(solution)/shard_map/ppermute | solution.py:42
  85.3 0.0 copy-done.2
  85.3 2.1 %finish.1 = (bf16[128,1024]{1,0:T(8,128)(2,1)}, bf16[128,4096]{1,0:T(8,128)(2,1)}) custom-call(bf16[128,4096]{1,0:T(8,128)(2,1)S(1)} %copy-done.2, f32[128,1]{1,0:T(8,128)S(1)} %get-tuple-element.38.inv_ref, f32[128,2048]{1,0:T(8,128)S(1)} %get-tuple-element.61.own_ref, bf16[128,2048]{1,0:T(8,128)(2,1)S(1)} %collective-permute-done.10.refs_0_, ...), custom_call_target="tpu_custom_call" | custom-call | flops 4194304 | bytes 5242880 | tf_op jit(solution)/shard_map/finish/pallas_call | solution.py:226
  (6 shorter events, 0.1 us)
Async XLA Ops:
  0.6 12.4 %copy-start = (f32[8,4096]{1,0:T(8,128)S(1)}, f32[8,4096]{1,0:T(8,128)}, u32[]{:S(2)}) copy-start(f32[8,4096]{1,0:T(8,128)} %param.11) | copy-start | bytes 393220
  0.6 13.3 %collective-permute-start = (bf16[64,1024]{1,0:T(8,128)(2,1)}, bf16[64,1024]{1,0:T(8,128)(2,1)S(1)}, u32[]{:S(2)}, u32[]{:S(2)}) collective-permute-start(bf16[64,1024]{1,0:T(8,128)(2,1)} %bitcast.10), channel_id=1, source_target_pairs={{0,8},{1,5},{2,10},{3,7},{4,12},{5,1},{6,14},{7,3},{8,0},{9,13},{1... | collective-permute-start | bytes 393224 | tf_op jit(solution)/shard_map/ppermute | solution.py:42
  6.5 1.2 %copy-start.1 = (bf16[128,4096]{1,0:T(8,128)(2,1)S(1)}, bf16[128,4096]{1,0:T(8,128)(2,1)}, u32[]{:S(2)}) copy-start(bf16[128,4096]{1,0:T(8,128)(2,1)} %tok_ref.3) | copy-start | bytes 3145732
  7.7 0.9 %copy-start.3 = (bf16[128,1024]{1,0:T(8,128)(2,1)S(1)}, bf16[128,1024]{1,0:T(8,128)(2,1)}, u32[]{:S(2)}) copy-start(bf16[128,1024]{1,0:T(8,128)(2,1)} %cot_ref.1) | copy-start | bytes 786436
  9.2 26.5 %collective-permute-start.3 = (bf16[128,2048]{1,0:T(8,128)(2,1)S(1)}, bf16[128,2048]{1,0:T(8,128)(2,1)S(1)}, u32[]{:S(2)}, u32[]{:S(2)}) collective-permute-start(bf16[128,2048]{1,0:T(8,128)(2,1)S(1)} %get-tuple-element.45), channel_id=1, source_target_pairs={{0,16},{1,17},{2,18},{3,19},{4,20},{5,21},{6,22},{7,23},{8,24},{9,... | collective-permute-start | bytes 1572872 | tf_op jit(solution)/shard_map/ppermute | solution.py:42
  14.9 20.8 %collective-permute-start.1 = (bf16[128,1024]{1,0:T(8,128)(2,1)S(1)}, bf16[128,1024]{1,0:T(8,128)(2,1)S(1)}, u32[]{:S(2)}, u32[]{:S(2)}) collective-permute-start(bf16[128,1024]{1,0:T(8,128)(2,1)S(1)} %pad_maximum_fusion), channel_id=1, source_target_pairs={{0,4},{1,9},{2,6},{3,11},{4,0},{5,13},{6,2},{7,15},{8,12},{9,1},{1... | collective-permute-start | bytes 786440 | tf_op jit(solution)/shard_map/ppermute | solution.py:42
  23.7 26.4 %collective-permute-start.7 = (bf16[128,2048]{1,0:T(8,128)(2,1)S(1)}, bf16[128,2048]{1,0:T(8,128)(2,1)S(1)}, u32[]{:S(2)}, u32[]{:S(2)}) collective-permute-start(bf16[128,2048]{1,0:T(8,128)(2,1)S(1)} %get-tuple-element.48), channel_id=1, source_target_pairs={{0,48},{1,49},{2,50},{3,51},{4,52},{5,53},{6,54},{7,55},{8,56},{9,... | collective-permute-start | bytes 1572872 | tf_op jit(solution)/shard_map/ppermute | solution.py:42
  27.2 4.8 %collective-permute-start.2 = (f32[4096]{0:T(1024)S(1)}, f32[4096]{0:T(1024)S(1)}, u32[]{:S(2)}, u32[]{:S(2)}) collective-permute-start(f32[4096]{0:T(1024)S(1)} %sub.6), channel_id=1, source_target_pairs={{0,128},{64,192},{128,0},{192,64},{256,384},{320,448},{384,256},{4... | collective-permute-start | bytes 49160 | tf_op jit(solution)/shard_map/ppermute | solution.py:170
  32.0 18.2 %collective-permute-start.6 = (bf16[128,2048]{1,0:T(8,128)(2,1)S(1)}, bf16[128,2048]{1,0:T(8,128)(2,1)S(1)}, u32[]{:S(2)}, u32[]{:S(2)}) collective-permute-start(bf16[128,2048]{1,0:T(8,128)(2,1)S(1)} %get-tuple-element.47), channel_id=1, source_target_pairs={{0,32},{1,33},{2,34},{3,35},{4,36},{5,37},{6,38},{7,39},{8,40},{9,... | collective-permute-start | bytes 1572872 | tf_op jit(solution)/shard_map/ppermute | solution.py:42
  35.8 14.4 %collective-permute-start.4 = (bf16[256,1024]{1,0:T(8,128)(2,1)S(1)}, bf16[256,1024]{1,0:T(8,128)(2,1)S(1)}, u32[]{:S(2)}, u32[]{:S(2)}) collective-permute-start(bf16[256,1024]{1,0:T(8,128)(2,1)S(1)} %constant_dynamic-update-slice_fusion.mine_ref), channel_id=1, source_target_pairs={{0,2},{1,3},{2,0},{3,1},{4,6},{5,7},{6,4},{7,5},{8,10},{9,11},{10,... | collective-permute-start | bytes 1572872 | tf_op jit(solution)/shard_map/ppermute | solution.py:42
  39.0 11.1 %collective-permute-start.5 = (bf16[256,1024]{1,0:T(8,128)(2,1)S(1)}, bf16[256,1024]{1,0:T(8,128)(2,1)S(1)}, u32[]{:S(2)}, u32[]{:S(2)}) collective-permute-start(bf16[256,1024]{1,0:T(8,128)(2,1)S(1)} %constant_dynamic-update-slice_fusion.mine_ref), channel_id=1, source_target_pairs={{0,1},{1,0},{2,3},{3,2},{4,5},{5,4},{6,7},{7,6},{8,9},{9,8},{10,11... | collective-permute-start | bytes 1572872 | tf_op jit(solution)/shard_map/ppermute | solution.py:42
  44.2 6.0 %collective-permute-start.8 = (f32[4096]{0:T(1024)S(1)}, f32[4096]{0:T(1024)S(1)}, u32[]{:S(2)}, u32[]{:S(2)}) collective-permute-start(f32[4096]{0:T(1024)S(1)} %add.23), channel_id=1, source_target_pairs={{0,256},{64,320},{128,384},{192,448},{256,0},{320,64},{384,128},{4... | collective-permute-start | bytes 49160 | tf_op jit(solution)/shard_map/ppermute | solution.py:170
  50.2 5.2 %collective-permute-start.9 = (bf16[256,1024]{1,0:T(8,128)(2,1)S(1)}, bf16[256,1024]{1,0:T(8,128)(2,1)S(1)}, u32[]{:S(2)}, u32[]{:S(2)}) collective-permute-start(bf16[256,1024]{1,0:T(8,128)(2,1)S(1)} %collective-permute-done.4.mine_ref), channel_id=1, source_target_pairs={{0,1},{1,0},{2,3},{3,2},{4,5},{5,4},{6,7},{7,6},{8,9},{9,8},{10,11... | collective-permute-start | bytes 1572872 | tf_op jit(solution)/shard_map/ppermute | solution.py:42
  55.4 29.9 %copy-start.2 = (bf16[128,4096]{1,0:T(8,128)(2,1)S(1)}, bf16[128,4096]{1,0:T(8,128)(2,1)}, u32[]{:S(2)}) copy-start(bf16[128,4096]{1,0:T(8,128)(2,1)} %tok_ref.3) | copy-start | bytes 3145732
  56.8 23.9 %collective-permute-start.10 = (bf16[128,2048]{1,0:T(8,128)(2,1)S(1)}, bf16[128,2048]{1,0:T(8,128)(2,1)S(1)}, u32[]{:S(2)}, u32[]{:S(2)}) collective-permute-start(bf16[128,2048]{1,0:T(8,128)(2,1)S(1)} %get-tuple-element.66), channel_id=1, source_target_pairs={{0,32},{1,33},{2,34},{3,35},{4,36},{5,37},{6,38},{7,39},{8,40},{9,... | collective-permute-start | bytes 1572872 | tf_op jit(solution)/shard_map/ppermute | solution.py:42
  61.4 22.8 %collective-permute-start.11 = (bf16[128,2048]{1,0:T(8,128)(2,1)S(1)}, bf16[128,2048]{1,0:T(8,128)(2,1)S(1)}, u32[]{:S(2)}, u32[]{:S(2)}) collective-permute-start(bf16[128,2048]{1,0:T(8,128)(2,1)S(1)} %get-tuple-element.67), channel_id=1, source_target_pairs={{0,48},{1,49},{2,50},{3,51},{4,52},{5,53},{6,54},{7,55},{8,56},{9,... | collective-permute-start | bytes 1572872 | tf_op jit(solution)/shard_map/ppermute | solution.py:42
  64.4 21.0 %collective-permute-start.12 = (bf16[128,2048]{1,0:T(8,128)(2,1)S(1)}, bf16[128,2048]{1,0:T(8,128)(2,1)S(1)}, u32[]{:S(2)}, u32[]{:S(2)}) collective-permute-start(bf16[128,2048]{1,0:T(8,128)(2,1)S(1)} %get-tuple-element.68), channel_id=1, source_target_pairs={{0,16},{1,17},{2,18},{3,19},{4,20},{5,21},{6,22},{7,23},{8,24},{9,... | collective-permute-start | bytes 1572872 | tf_op jit(solution)/shard_map/ppermute | solution.py:42
  66.7 13.5 %collective-permute-start.13 = (f32[4096]{0:T(1024)S(1)}, f32[4096]{0:T(1024)S(1)}, u32[]{:S(2)}, u32[]{:S(2)}) collective-permute-start(f32[4096]{0:T(1024)S(1)} %add.24), channel_id=1, source_target_pairs={{0,64},{64,0},{128,192},{192,128},{256,320},{320,256},{384,448},{4... | collective-permute-start | bytes 49160 | tf_op jit(solution)/shard_map/ppermute | solution.py:170

commit v5 on v4

--- a/solution.py
+++ b/solution.py
@@ -10,8 +10,8 @@
 outer_rate = 0.7
 
 NY, NZ, NC = 4, 8, 2
-EVEN = ((0, 4, 2, 6), (0, 2, 4, 6))
-ODD = ((1, 5, 3, 7), (1, 3, 5, 7))
+EVEN = ((0, 2, 4, 6), (0, 4, 2, 6))
+ODD = ((1, 3, 5, 7), (1, 5, 3, 7))
 WIDE = 1024
 HALF = WIDE // 2
 MIB = 1 << 20
@@ -51,9 +51,10 @@
     return pl.ds(pl.multiple_of(lax.rem(y + step, NY) * WIDE, WIDE), WIDE)
 
 
-def prepare_kernel(tok_ref, cot_ref, *refs):
-    outs, inv_ref = refs[:NY], refs[NY]
+def prepare_kernel(tok_ref, cot_ref, shard_ref, *refs):
+    outs, inv_ref, kept_ref = refs[:NY], refs[NY], refs[NY + 1]
     y, _, _ = place()
+    kept_ref[...] = shard_ref[...]
     x = tok_ref[...].astype(jnp.float32)
     inv = lax.rsqrt(jnp.mean(x * x, axis=1, keepdims=True) + norm_eps)
     inv_ref[...] = inv
@@ -131,17 +132,28 @@
                 out_ref[:, cols] = turn[rows * n : rows * (n + 1)].astype(jnp.bfloat16)
 
 
-def finish_kernel(tok_ref, inv_ref, own_ref, *refs):
+def begin_kernel(tok_ref, inv_ref, own_ref, across_ref, kv_ref, inner_ref):
+    y, _, _ = place()
+    inv = inv_ref[...]
+    kv_ref[...] = own_ref[:, :WIDE] + across_ref[:, :WIDE].astype(jnp.float32)
+    inner = 0.0
+    for step, ref in ((0, own_ref), (2, across_ref)):
+        normed = tok_ref[:, slab(y, step)].astype(jnp.float32) * inv
+        inner += jnp.sum(ref[:, WIDE:].astype(jnp.float32) * normed, axis=1, keepdims=True)
+    inner_ref[...] = inner
+
+
+def finish_kernel(tok_ref, inv_ref, kv_part_ref, inner_ref, own_ref, *refs):
     gots, (kv_ref, grad_ref) = refs[: NY - 1], refs[NY - 1 :]
     y, _, _ = place()
     inv = inv_ref[...]
-    kv = own_ref[:, :WIDE]
-    for ref in gots:
+    kv = kv_part_ref[...]
+    for ref in gots[1:]:
         kv += ref[:, :WIDE].astype(jnp.float32)
     kv_ref[...] = kv.astype(jnp.bfloat16)
     sources = list(zip((0, 2, 1, 3), (own_ref, *gots)))
-    inner = 0.0
-    for step, ref in sources:
+    inner = inner_ref[...]
+    for step, ref in sources[2:]:
         normed = tok_ref[:, slab(y, step)].astype(jnp.float32) * inv
         inner += jnp.sum(ref[:, WIDE:].astype(jnp.float32) * normed, axis=1, keepdims=True)
     inner = inner / tok_ref.shape[1]
@@ -170,20 +182,21 @@
         return drift + lax.ppermute(drift, "rep", [(r, r ^ bit) for r in range(replicas)])
 
     block = jax.ShapeDtypeStruct((rows, 2 * WIDE), jnp.bfloat16)
-    *acts, inv = pl.pallas_call(
+    *acts, inv, kept = pl.pallas_call(
         prepare_kernel,
-        out_shape=(block,) * NY + (jax.ShapeDtypeStruct((rows, 1), jnp.float32),),
+        out_shape=(block,) * NY
+        + (jax.ShapeDtypeStruct((rows, 1), jnp.float32), jax.ShapeDtypeStruct(shard.shape, shard.dtype)),
         compiler_params=params,
         cost_estimate=pl.CostEstimate(flops=2**21, bytes_accessed=4 * MIB, transcendentals=128),
         name="prepare",
-    )(tokens, kv_cotangent)
-
-    far = send(shard, to_z(4, 2))
+    )(tokens, kv_cotangent, shard)
+
+    far = send(shard, to_z(2, 4))
     act1 = send(acts[1], to_y(1))
     act3 = send(acts[3], to_y(3))
     far, drift = tie((far, drift))
-    pair = jnp.concatenate([shard, far], axis=0)
-    more = send(pair, to_z(2, 4))
+    pair = jnp.concatenate([kept, far], axis=0)
+    more = send(pair, to_z(4, 2))
     pair, drift = tie((pair, drift))
     drift = add_half(drift, 2)
     drift, acts[2] = tie((drift, acts[2]))
@@ -223,6 +236,16 @@
     outer_grad = drift / replicas
     momentum_new = outer_momentum * moment_now + outer_grad
     anchor_new = anchor_now - outer_rate * (outer_grad + outer_momentum * momentum_new)
+    kv_part, inner = pl.pallas_call(
+        begin_kernel,
+        out_shape=(
+            jax.ShapeDtypeStruct((rows, WIDE), jnp.float32),
+            jax.ShapeDtypeStruct((rows, 1), jnp.float32),
+        ),
+        compiler_params=params,
+        cost_estimate=pl.CostEstimate(flops=2**21, bytes_accessed=3 * MIB, transcendentals=0),
+        name="begin",
+    )(tokens, inv, own, gots[0])
     key_value, input_grad = pl.pallas_call(
         finish_kernel,
         out_shape=(
@@ -232,7 +255,7 @@
         compiler_params=params,
         cost_estimate=pl.CostEstimate(flops=2**22, bytes_accessed=5 * MIB, transcendentals=0),
         name="finish",
-    )(tokens, inv, own, *gots)
+    )(tokens, inv, kv_part, inner, own, *gots)
     return key_value, input_grad, anchor_new, momentum_new
 
 

time: 88 us -> 87.7 us (level)
  starting transfers between devices: 66.7 us -> 64.1 us
  waiting for transfers between devices: 8.2 us -> 10.5 us
  other arithmetic: 3.35 us -> 2.42 us
  local copies, waits for them, and re-layouts: 2.24 us -> 3.16 us
    ppermute x3, starting transfers between devices: 20 us -> 17.9 us  [add_half(): lax.ppermute(drift, 'rep', [(r, r ^ bit) for r in range(replicas)])]
    ppermute x3, waiting for transfers between devices: 3.23 us -> 5.05 us  [add_half(): lax.ppermute(drift, 'rep', [(r, r ^ bit) for r in range(replicas)])]
    concatenate x1 -> x0, other arithmetic: 0.92 us -> none  [local(): pair = jnp.concatenate([shard, far], axis=0)]
    unnamed x9 -> x12, local copies, waits for them, and re-layouts: 2.2 us -> 3.12 us
  transfers between devices with their start and end apart: 14 -> 14, of which waited for: 7 -> 7; matrix products, arithmetic and copies ran while one was open for 4% -> 3% of each run, Pallas kernels for 2% -> 3%
where the time goes in v5:
time: 87.7 us; the launch traced here: 87.1 us
  starting transfers between devices  64.1 us (73%)
  waiting for transfers between devices  10.5 us (12%)
  Pallas kernels  5.35 us (6%)
  local copies, waits for them, and re-layouts  3.16 us (4%)
  other arithmetic  2.42 us (3%)
  between operations  1.54 us (2%)
    ppermute x11, starting transfers between devices, send(): return lax.ppermute(x, 'fsdp', pairs)  46.2 us
    ppermute x3, starting transfers between devices, add_half(): lax.ppermute(drift, 'rep', [(r, r ^ bit) for r in range(replicas)])  17.9 us
    ppermute x11, waiting for transfers between devices, send(): return lax.ppermute(x, 'fsdp', pairs)  5.41 us
    ppermute x3, waiting for transfers between devices, add_half(): lax.ppermute(drift, 'rep', [(r, r ^ bit) for r in range(replicas)])  5.05 us
    unnamed x12, local copies, waits for them, and re-layouts  3.12 us
  transfers between devices with their start and end apart: 14, of which 7 were waited for; matrix products, arithmetic and copies ran while one was open for 3% of the time, Pallas kernels for 3%

profile of v5, /device:TPU:1, one launch (start us, length us, event | category | flops | bytes accessed | tf_op | source)
XLA Modules:
  0.0 87.1 jit_solution(12190292575646631293)
XLA Ops:
  0.6 0.0 copy-start
  0.6 9.8 %collective-permute-start = (bf16[64,1024]{1,0:T(8,128)(2,1)}, bf16[64,1024]{1,0:T(8,128)(2,1)S(1)}, u32[]{:S(2)}, u32[]{:S(2)}) collective-permute-start(bf16[64,1024]{1,0:T(8,128)(2,1)} %bitcast.8), channel_id=1, source_target_pairs={{0,4},{1,9},{2,6},{3,11},{4,0},{5,13},{6,2},{7,15},{8,12},{9,1},{1... | collective-permute-start | bytes 393224 | tf_op jit(solution)/shard_map/ppermute | solution.py:42
  10.4 0.0 copy-start.1
  10.4 1.2 %copy-done.1 = bf16[128,4096]{1,0:T(8,128)(2,1)S(1)} copy-done((bf16[128,4096]{1,0:T(8,128)(2,1)S(1)}, bf16[128,4096]{1,0:T(8,128)(2,1)}, u32[]{:S(2)}) %copy-start.1) | copy-done | bytes 1048600
  11.7 0.0 copy-start.3
  11.7 0.9 %copy-done.3 = bf16[128,1024]{1,0:T(8,128)(2,1)S(1)} copy-done((bf16[128,1024]{1,0:T(8,128)(2,1)S(1)}, bf16[128,1024]{1,0:T(8,128)(2,1)}, u32[]{:S(2)}) %copy-start.3) | copy-done | bytes 262168
  12.6 0.0 copy-start.4
  12.6 0.9 %copy-done.4 = bf16[1,64,1024]{2,1,0:T(8,128)(2,1)S(1)} copy-done((bf16[1,64,1024]{2,1,0:T(8,128)(2,1)S(1)}, bf16[1,64,1024]{2,1,0:T(8,128)(2,1)}, u32[]{:S(2)}) %copy-start.4) | copy-done | bytes 131096
  13.5 0.5 prepare.1
  14.0 3.2 %collective-permute-start.3 = (bf16[128,2048]{1,0:T(8,128)(2,1)S(1)}, bf16[128,2048]{1,0:T(8,128)(2,1)S(1)}, u32[]{:S(2)}, u32[]{:S(2)}) collective-permute-start(bf16[128,2048]{1,0:T(8,128)(2,1)S(1)} %get-tuple-element.49), channel_id=1, source_target_pairs={{0,16},{1,17},{2,18},{3,19},{4,20},{5,21},{6,22},{7,23},{8,24},{9,... | collective-permute-start | bytes 1572872 | tf_op jit(solution)/shard_map/ppermute | solution.py:42
  17.9 0.0 copy-done
  17.9 0.9 dynamic-slice_convert_fusion
  18.8 0.0 collective-permute-done
  18.8 4.9 %collective-permute-start.1 = (bf16[128,1024]{1,0:T(8,128)(2,1)S(1)}, bf16[128,1024]{1,0:T(8,128)(2,1)S(1)}, u32[]{:S(2)}, u32[]{:S(2)}) collective-permute-start(bf16[128,1024]{1,0:T(8,128)(2,1)S(1)} %constant_dynamic-update-slice_fusion), channel_id=1, source_target_pairs={{0,8},{1,5},{2,10},{3,7},{4,12},{5,1},{6,14},{7,3},{8,0},{9,13},{1... | collective-permute-start | bytes 786440 | tf_op jit(solution)/shard_map/ppermute | solution.py:42
  23.8 3.4 %collective-permute-start.7 = (bf16[128,2048]{1,0:T(8,128)(2,1)S(1)}, bf16[128,2048]{1,0:T(8,128)(2,1)S(1)}, u32[]{:S(2)}, u32[]{:S(2)}) collective-permute-start(bf16[128,2048]{1,0:T(8,128)(2,1)S(1)} %get-tuple-element.52), channel_id=1, source_target_pairs={{0,48},{1,49},{2,50},{3,51},{4,52},{5,53},{6,54},{7,55},{8,56},{9,... | collective-permute-start | bytes 1572872 | tf_op jit(solution)/shard_map/ppermute | solution.py:42
  27.1 3.1 %collective-permute-start.2 = (f32[4096]{0:T(1024)S(1)}, f32[4096]{0:T(1024)S(1)}, u32[]{:S(2)}, u32[]{:S(2)}) collective-permute-start(f32[4096]{0:T(1024)S(1)} %sub.6), channel_id=1, source_target_pairs={{0,128},{64,192},{128,0},{192,64},{256,384},{320,448},{384,256},{4... | collective-permute-start | bytes 49160 | tf_op jit(solution)/shard_map/ppermute | solution.py:182
  30.3 1.6 %collective-permute-done.2 = f32[4096]{0:T(1024)S(1)} collective-permute-done((f32[4096]{0:T(1024)S(1)}, f32[4096]{0:T(1024)S(1)}, u32[]{:S(2)}, u32[]{:S(2)}) %collective-permute-start.2) | collective-permute-done | bytes 16416 | tf_op jit(solution)/shard_map/ppermute | solution.py:182
  31.9 3.5 %collective-permute-start.6 = (bf16[128,2048]{1,0:T(8,128)(2,1)S(1)}, bf16[128,2048]{1,0:T(8,128)(2,1)S(1)}, u32[]{:S(2)}, u32[]{:S(2)}) collective-permute-start(bf16[128,2048]{1,0:T(8,128)(2,1)S(1)} %get-tuple-element.51), channel_id=1, source_target_pairs={{0,32},{1,33},{2,34},{3,35},{4,36},{5,37},{6,38},{7,39},{8,40},{9,... | collective-permute-start | bytes 1572872 | tf_op jit(solution)/shard_map/ppermute | solution.py:42
  35.4 0.3 collective-permute-done.1
  35.8 0.0 collective-permute-done.3.refs_1_
  35.8 3.2 %collective-permute-start.4 = (bf16[256,1024]{1,0:T(8,128)(2,1)S(1)}, bf16[256,1024]{1,0:T(8,128)(2,1)S(1)}, u32[]{:S(2)}, u32[]{:S(2)}) collective-permute-start(bf16[256,1024]{1,0:T(8,128)(2,1)S(1)} %constant_dynamic-update-slice_fusion.2.mine_ref), channel_id=1, source_target_pairs={{0,2},{1,3},{2,0},{3,1},{4,6},{5,7},{6,4},{7,5},{8,10},{9,11},{10,... | collective-permute-start | bytes 1572872 | tf_op jit(solution)/shard_map/ppermute | solution.py:42
  39.0 5.1 %collective-permute-start.5 = (bf16[256,1024]{1,0:T(8,128)(2,1)S(1)}, bf16[256,1024]{1,0:T(8,128)(2,1)S(1)}, u32[]{:S(2)}, u32[]{:S(2)}) collective-permute-start(bf16[256,1024]{1,0:T(8,128)(2,1)S(1)} %constant_dynamic-update-slice_fusion.2.mine_ref), channel_id=1, source_target_pairs={{0,1},{1,0},{2,3},{3,2},{4,5},{5,4},{6,7},{7,6},{8,9},{9,8},{10,11... | collective-permute-start | bytes 1572872 | tf_op jit(solution)/shard_map/ppermute | solution.py:42
  44.2 4.7 %collective-permute-start.8 = (f32[4096]{0:T(1024)S(1)}, f32[4096]{0:T(1024)S(1)}, u32[]{:S(2)}, u32[]{:S(2)}) collective-permute-start(f32[4096]{0:T(1024)S(1)} %add.23), channel_id=1, source_target_pairs={{0,256},{64,320},{128,384},{192,448},{256,0},{320,64},{384,128},{4... | collective-permute-start | bytes 49160 | tf_op jit(solution)/shard_map/ppermute | solution.py:182
  48.8 1.3 %collective-permute-done.8 = f32[4096]{0:T(1024)S(1)} collective-permute-done((f32[4096]{0:T(1024)S(1)}, f32[4096]{0:T(1024)S(1)}, u32[]{:S(2)}, u32[]{:S(2)}) %collective-permute-start.8) | collective-permute-done | bytes 16416 | tf_op jit(solution)/shard_map/ppermute | solution.py:182
  50.2 0.0 collective-permute-done.7.refs_3_
  50.2 0.0 collective-permute-done.6.refs_2_
  50.2 0.0 collective-permute-done.4.mine_ref
  50.2 0.0 collective-permute-done.5.sib_ref
  50.2 3.7 %collective-permute-start.9 = (bf16[256,1024]{1,0:T(8,128)(2,1)S(1)}, bf16[256,1024]{1,0:T(8,128)(2,1)S(1)}, u32[]{:S(2)}, u32[]{:S(2)}) collective-permute-start(bf16[256,1024]{1,0:T(8,128)(2,1)S(1)} %collective-permute-done.4.mine_ref), channel_id=1, source_target_pairs={{0,1},{1,0},{2,3},{3,2},{4,5},{5,4},{6,7},{7,6},{8,9},{9,8},{10,11... | collective-permute-start | bytes 1572872 | tf_op jit(solution)/shard_map/ppermute | solution.py:42
  53.9 1.4 %first_half.1 = (f32[512,1024]{1,0:T(8,128)S(1)}, f32[128,512]{1,0:T(8,128)S(1)}, bf16[128,512]{1,0:T(8,128)(2,1)S(1)}, bf16[128,512]{1,0:T(8,128)(2,1)S(1)}, bf16[128,512]{1,0:T(8,128)(2,1)S(1)}) custom-call(bf16[256,1024]{1,0:T(8,128)(2,1)S(1)} %constant_dynamic-update-slice_fusion.2.mine_ref, bf16[256,1024]{1,0:T(8,128)(2,1)S(1)} %collective-permute-done.5.sib_ref, ...), custom_call_target="tpu_custom_call" | custom-call | flops 1073741824 | bytes 8388608 | tf_op jit(solution)/shard_map/first_half/pallas_call | solution.py:213
  55.3 0.1 collective-permute-done.9.sib_ref
  55.4 0.0 copy-start.2
  55.4 1.4 %second_half.1 = (f32[128,2048]{1,0:T(8,128)S(1)}, bf16[128,2048]{1,0:T(8,128)(2,1)S(1)}, bf16[128,2048]{1,0:T(8,128)(2,1)S(1)}, bf16[128,2048]{1,0:T(8,128)(2,1)S(1)}) custom-call(bf16[256,1024]{1,0:T(8,128)(2,1)S(1)} %collective-permute-done.4.mine_ref, bf16[256,1024]{1,0:T(8,128)(2,1)S(1)} %collective-permute-done.9.sib_ref, ...), custom_call_target="tpu_custom_call" | custom-call | flops 1073741824 | bytes 8388608 | tf_op jit(solution)/shard_map/second_half/pallas_call | solution.py:225
  56.8 3.9 %collective-permute-start.10 = (bf16[128,2048]{1,0:T(8,128)(2,1)S(1)}, bf16[128,2048]{1,0:T(8,128)(2,1)S(1)}, u32[]{:S(2)}, u32[]{:S(2)}) collective-permute-start(bf16[128,2048]{1,0:T(8,128)(2,1)S(1)} %get-tuple-element.70), channel_id=1, source_target_pairs={{0,32},{1,33},{2,34},{3,35},{4,36},{5,37},{6,38},{7,39},{8,40},{9,... | collective-permute-start | bytes 1572872 | tf_op jit(solution)/shard_map/ppermute | solution.py:42
  60.7 3.6 %collective-permute-start.11 = (bf16[128,2048]{1,0:T(8,128)(2,1)S(1)}, bf16[128,2048]{1,0:T(8,128)(2,1)S(1)}, u32[]{:S(2)}, u32[]{:S(2)}) collective-permute-start(bf16[128,2048]{1,0:T(8,128)(2,1)S(1)} %get-tuple-element.73), channel_id=1, source_target_pairs={{0,48},{1,49},{2,50},{3,51},{4,52},{5,53},{6,54},{7,55},{8,56},{9,... | collective-permute-start | bytes 1572872 | tf_op jit(solution)/shard_map/ppermute | solution.py:42
  64.3 1.9 %collective-permute-start.12 = (bf16[128,2048]{1,0:T(8,128)(2,1)S(1)}, bf16[128,2048]{1,0:T(8,128)(2,1)S(1)}, u32[]{:S(2)}, u32[]{:S(2)}) collective-permute-start(bf16[128,2048]{1,0:T(8,128)(2,1)S(1)} %get-tuple-element.74), channel_id=1, source_target_pairs={{0,16},{1,17},{2,18},{3,19},{4,20},{5,21},{6,22},{7,23},{8,24},{9,... | collective-permute-start | bytes 1572872 | tf_op jit(solution)/shard_map/ppermute | solution.py:42
  66.2 10.2 %collective-permute-start.13 = (f32[4096]{0:T(1024)S(1)}, f32[4096]{0:T(1024)S(1)}, u32[]{:S(2)}, u32[]{:S(2)}) collective-permute-start(f32[4096]{0:T(1024)S(1)} %add.24), channel_id=1, source_target_pairs={{0,64},{64,0},{128,192},{192,128},{256,320},{320,256},{384,448},{4... | collective-permute-start | bytes 49160 | tf_op jit(solution)/shard_map/ppermute | solution.py:182
  76.4 0.9 %dynamic-slice_multiply_fusion = f32[1,4096]{1,0:T(1,128)S(1)} fusion(f32[8,4096]{1,0:T(8,128)} %param.12, s32[]{:T(128)S(6)} %select_n.7), kind=kLoop, calls=%fused_computation.1 | loop fusion | flops 4096 | bytes 32772 | tf_op jit(solution)/shard_map/mul | solution.py:237
  77.3 2.1 %collective-permute-done.13 = f32[4096]{0:T(1024)S(1)} collective-permute-done((f32[4096]{0:T(1024)S(1)}, f32[4096]{0:T(1024)S(1)}, u32[]{:S(2)}, u32[]{:S(2)}) %collective-permute-start.13) | collective-permute-done | bytes 16416 | tf_op jit(solution)/shard_map/ppermute | solution.py:182
  79.4 0.6 multiply_subtract_fusion
  80.0 0.0 collective-permute-done.10.across_ref.refs_0_
  80.0 0.0 copy-done.2
  80.0 0.3 begin.1
  80.4 3.8 %collective-permute-done.11.refs_1_ = bf16[128,2048]{1,0:T(8,128)(2,1)S(1)} collective-permute-done((bf16[128,2048]{1,0:T(8,128)(2,1)S(1)}, bf16[128,2048]{1,0:T(8,128)(2,1)S(1)}, u32[]{:S(2)}, u32[]{:S(2)}) %collective-permute-start.11) | collective-permute-done | bytes 524320 | tf_op jit(solution)/shard_map/ppermute | solution.py:42
  84.1 1.2 %collective-permute-done.12.refs_2_ = bf16[128,2048]{1,0:T(8,128)(2,1)S(1)} collective-permute-done((bf16[128,2048]{1,0:T(8,128)(2,1)S(1)}, bf16[128,2048]{1,0:T(8,128)(2,1)S(1)}, u32[]{:S(2)}, u32[]{:S(2)}) %collective-permute-start.12) | collective-permute-done | bytes 524320 | tf_op jit(solution)/shard_map/ppermute | solution.py:42
  85.3 1.7 %finish.1 = (bf16[128,1024]{1,0:T(8,128)(2,1)}, bf16[128,4096]{1,0:T(8,128)(2,1)}) custom-call(bf16[128,4096]{1,0:T(8,128)(2,1)S(1)} %copy-done.2, f32[128,1]{1,0:T(8,128)S(1)} %get-tuple-element.41.inv_ref, f32[128,1024]{1,0:T(8,128)S(1)} %get-tuple-element.71.kv_part_ref, f32[128,1]{1,0:T(8,128)S(1)} %get-tuple-element.72.inner_ref, ...), custom_call_target="tpu_custom_call" | custom-call | flops 4194304 | bytes 5242880 | tf_op jit(solution)/shard_map/finish/pallas_call | solution.py:249
  (8 shorter events, 0.1 us)
Async XLA Ops:
  0.6 17.3 %copy-start = (f32[8,4096]{1,0:T(8,128)S(1)}, f32[8,4096]{1,0:T(8,128)}, u32[]{:S(2)}) copy-start(f32[8,4096]{1,0:T(8,128)} %param.11) | copy-start | bytes 393220
  0.6 18.2 %collective-permute-start = (bf16[64,1024]{1,0:T(8,128)(2,1)}, bf16[64,1024]{1,0:T(8,128)(2,1)S(1)}, u32[]{:S(2)}, u32[]{:S(2)}) collective-permute-start(bf16[64,1024]{1,0:T(8,128)(2,1)} %bitcast.8), channel_id=1, source_target_pairs={{0,4},{1,9},{2,6},{3,11},{4,0},{5,13},{6,2},{7,15},{8,12},{9,1},{1... | collective-permute-start | bytes 393224 | tf_op jit(solution)/shard_map/ppermute | solution.py:42
  10.4 1.2 %copy-start.1 = (bf16[128,4096]{1,0:T(8,128)(2,1)S(1)}, bf16[128,4096]{1,0:T(8,128)(2,1)}, u32[]{:S(2)}) copy-start(bf16[128,4096]{1,0:T(8,128)(2,1)} %tok_ref.5) | copy-start | bytes 3145732
  11.7 0.9 %copy-start.3 = (bf16[128,1024]{1,0:T(8,128)(2,1)S(1)}, bf16[128,1024]{1,0:T(8,128)(2,1)}, u32[]{:S(2)}) copy-start(bf16[128,1024]{1,0:T(8,128)(2,1)} %cot_ref.1) | copy-start | bytes 786436
  12.6 0.9 %copy-start.4 = (bf16[1,64,1024]{2,1,0:T(8,128)(2,1)S(1)}, bf16[1,64,1024]{2,1,0:T(8,128)(2,1)}, u32[]{:S(2)}) copy-start(bf16[1,64,1024]{2,1,0:T(8,128)(2,1)} %param.8) | copy-start | bytes 393220
  14.0 21.7 %collective-permute-start.3 = (bf16[128,2048]{1,0:T(8,128)(2,1)S(1)}, bf16[128,2048]{1,0:T(8,128)(2,1)S(1)}, u32[]{:S(2)}, u32[]{:S(2)}) collective-permute-start(bf16[128,2048]{1,0:T(8,128)(2,1)S(1)} %get-tuple-element.49), channel_id=1, source_target_pairs={{0,16},{1,17},{2,18},{3,19},{4,20},{5,21},{6,22},{7,23},{8,24},{9,... | collective-permute-start | bytes 1572872 | tf_op jit(solution)/shard_map/ppermute | solution.py:42
  18.8 16.9 %collective-permute-start.1 = (bf16[128,1024]{1,0:T(8,128)(2,1)S(1)}, bf16[128,1024]{1,0:T(8,128)(2,1)S(1)}, u32[]{:S(2)}, u32[]{:S(2)}) collective-permute-start(bf16[128,1024]{1,0:T(8,128)(2,1)S(1)} %constant_dynamic-update-slice_fusion), channel_id=1, source_target_pairs={{0,8},{1,5},{2,10},{3,7},{4,12},{5,1},{6,14},{7,3},{8,0},{9,13},{1... | collective-permute-start | bytes 786440 | tf_op jit(solution)/shard_map/ppermute | solution.py:42
  23.8 26.4 %collective-permute-start.7 = (bf16[128,2048]{1,0:T(8,128)(2,1)S(1)}, bf16[128,2048]{1,0:T(8,128)(2,1)S(1)}, u32[]{:S(2)}, u32[]{:S(2)}) collective-permute-start(bf16[128,2048]{1,0:T(8,128)(2,1)S(1)} %get-tuple-element.52), channel_id=1, source_target_pairs={{0,48},{1,49},{2,50},{3,51},{4,52},{5,53},{6,54},{7,55},{8,56},{9,... | collective-permute-start | bytes 1572872 | tf_op jit(solution)/shard_map/ppermute | solution.py:42
  27.1 4.8 %collective-permute-start.2 = (f32[4096]{0:T(1024)S(1)}, f32[4096]{0:T(1024)S(1)}, u32[]{:S(2)}, u32[]{:S(2)}) collective-permute-start(f32[4096]{0:T(1024)S(1)} %sub.6), channel_id=1, source_target_pairs={{0,128},{64,192},{128,0},{192,64},{256,384},{320,448},{384,256},{4... | collective-permute-start | bytes 49160 | tf_op jit(solution)/shard_map/ppermute | solution.py:182
  31.9 18.3 %collective-permute-start.6 = (bf16[128,2048]{1,0:T(8,128)(2,1)S(1)}, bf16[128,2048]{1,0:T(8,128)(2,1)S(1)}, u32[]{:S(2)}, u32[]{:S(2)}) collective-permute-start(bf16[128,2048]{1,0:T(8,128)(2,1)S(1)} %get-tuple-element.51), channel_id=1, source_target_pairs={{0,32},{1,33},{2,34},{3,35},{4,36},{5,37},{6,38},{7,39},{8,40},{9,... | collective-permute-start | bytes 1572872 | tf_op jit(solution)/shard_map/ppermute | solution.py:42
  35.8 14.4 %collective-permute-start.4 = (bf16[256,1024]{1,0:T(8,128)(2,1)S(1)}, bf16[256,1024]{1,0:T(8,128)(2,1)S(1)}, u32[]{:S(2)}, u32[]{:S(2)}) collective-permute-start(bf16[256,1024]{1,0:T(8,128)(2,1)S(1)} %constant_dynamic-update-slice_fusion.2.mine_ref), channel_id=1, source_target_pairs={{0,2},{1,3},{2,0},{3,1},{4,6},{5,7},{6,4},{7,5},{8,10},{9,11},{10,... | collective-permute-start | bytes 1572872 | tf_op jit(solution)/shard_map/ppermute | solution.py:42
  39.0 11.1 %collective-permute-start.5 = (bf16[256,1024]{1,0:T(8,128)(2,1)S(1)}, bf16[256,1024]{1,0:T(8,128)(2,1)S(1)}, u32[]{:S(2)}, u32[]{:S(2)}) collective-permute-start(bf16[256,1024]{1,0:T(8,128)(2,1)S(1)} %constant_dynamic-update-slice_fusion.2.mine_ref), channel_id=1, source_target_pairs={{0,1},{1,0},{2,3},{3,2},{4,5},{5,4},{6,7},{7,6},{8,9},{9,8},{10,11... | collective-permute-start | bytes 1572872 | tf_op jit(solution)/shard_map/ppermute | solution.py:42
  44.2 6.0 %collective-permute-start.8 = (f32[4096]{0:T(1024)S(1)}, f32[4096]{0:T(1024)S(1)}, u32[]{:S(2)}, u32[]{:S(2)}) collective-permute-start(f32[4096]{0:T(1024)S(1)} %add.23), channel_id=1, source_target_pairs={{0,256},{64,320},{128,384},{192,448},{256,0},{320,64},{384,128},{4... | collective-permute-start | bytes 49160 | tf_op jit(solution)/shard_map/ppermute | solution.py:182
  50.2 5.2 %collective-permute-start.9 = (bf16[256,1024]{1,0:T(8,128)(2,1)S(1)}, bf16[256,1024]{1,0:T(8,128)(2,1)S(1)}, u32[]{:S(2)}, u32[]{:S(2)}) collective-permute-start(bf16[256,1024]{1,0:T(8,128)(2,1)S(1)} %collective-permute-done.4.mine_ref), channel_id=1, source_target_pairs={{0,1},{1,0},{2,3},{3,2},{4,5},{5,4},{6,7},{7,6},{8,9},{9,8},{10,11... | collective-permute-start | bytes 1572872 | tf_op jit(solution)/shard_map/ppermute | solution.py:42
  55.4 24.6 %copy-start.2 = (bf16[128,4096]{1,0:T(8,128)(2,1)S(1)}, bf16[128,4096]{1,0:T(8,128)(2,1)}, u32[]{:S(2)}) copy-start(bf16[128,4096]{1,0:T(8,128)(2,1)} %tok_ref.5) | copy-start | bytes 3145732
  56.8 23.2 %collective-permute-start.10 = (bf16[128,2048]{1,0:T(8,128)(2,1)S(1)}, bf16[128,2048]{1,0:T(8,128)(2,1)S(1)}, u32[]{:S(2)}, u32[]{:S(2)}) collective-permute-start(bf16[128,2048]{1,0:T(8,128)(2,1)S(1)} %get-tuple-element.70), channel_id=1, source_target_pairs={{0,32},{1,33},{2,34},{3,35},{4,36},{5,37},{6,38},{7,39},{8,40},{9,... | collective-permute-start | bytes 1572872 | tf_op jit(solution)/shard_map/ppermute | solution.py:42
  60.7 23.4 %collective-permute-start.11 = (bf16[128,2048]{1,0:T(8,128)(2,1)S(1)}, bf16[128,2048]{1,0:T(8,128)(2,1)S(1)}, u32[]{:S(2)}, u32[]{:S(2)}) collective-permute-start(bf16[128,2048]{1,0:T(8,128)(2,1)S(1)} %get-tuple-element.73), channel_id=1, source_target_pairs={{0,48},{1,49},{2,50},{3,51},{4,52},{5,53},{6,54},{7,55},{8,56},{9,... | collective-permute-start | bytes 1572872 | tf_op jit(solution)/shard_map/ppermute | solution.py:42
  64.3 21.0 %collective-permute-start.12 = (bf16[128,2048]{1,0:T(8,128)(2,1)S(1)}, bf16[128,2048]{1,0:T(8,128)(2,1)S(1)}, u32[]{:S(2)}, u32[]{:S(2)}) collective-permute-start(bf16[128,2048]{1,0:T(8,128)(2,1)S(1)} %get-tuple-element.74), channel_id=1, source_target_pairs={{0,16},{1,17},{2,18},{3,19},{4,20},{5,21},{6,22},{7,23},{8,24},{9,... | collective-permute-start | bytes 1572872 | tf_op jit(solution)/shard_map/ppermute | solution.py:42
  66.2 13.2 %collective-permute-start.13 = (f32[4096]{0:T(1024)S(1)}, f32[4096]{0:T(1024)S(1)}, u32[]{:S(2)}, u32[]{:S(2)}) collective-permute-start(f32[4096]{0:T(1024)S(1)} %add.24), channel_id=1, source_target_pairs={{0,64},{64,0},{128,192},{192,128},{256,320},{320,256},{384,448},{4... | collective-permute-start | bytes 49160 | tf_op jit(solution)/shard_map/ppermute | solution.py:182

commit v6 on v5

--- a/solution.py
+++ b/solution.py
@@ -132,14 +132,13 @@
                 out_ref[:, cols] = turn[rows * n : rows * (n + 1)].astype(jnp.bfloat16)
 
 
-def begin_kernel(tok_ref, inv_ref, own_ref, across_ref, kv_ref, inner_ref):
+def begin_kernel(tok_ref, own_ref, across_ref, kv_ref, inner_ref):
     y, _, _ = place()
-    inv = inv_ref[...]
     kv_ref[...] = own_ref[:, :WIDE] + across_ref[:, :WIDE].astype(jnp.float32)
     inner = 0.0
     for step, ref in ((0, own_ref), (2, across_ref)):
-        normed = tok_ref[:, slab(y, step)].astype(jnp.float32) * inv
-        inner += jnp.sum(ref[:, WIDE:].astype(jnp.float32) * normed, axis=1, keepdims=True)
+        tok = tok_ref[:, slab(y, step)].astype(jnp.float32)
+        inner += jnp.sum(ref[:, WIDE:].astype(jnp.float32) * tok, axis=1, keepdims=True)
     inner_ref[...] = inner
 
 
@@ -154,13 +153,13 @@
     sources = list(zip((0, 2, 1, 3), (own_ref, *gots)))
     inner = inner_ref[...]
     for step, ref in sources[2:]:
-        normed = tok_ref[:, slab(y, step)].astype(jnp.float32) * inv
-        inner += jnp.sum(ref[:, WIDE:].astype(jnp.float32) * normed, axis=1, keepdims=True)
-    inner = inner / tok_ref.shape[1]
+        tok = tok_ref[:, slab(y, step)].astype(jnp.float32)
+        inner += jnp.sum(ref[:, WIDE:].astype(jnp.float32) * tok, axis=1, keepdims=True)
+    scale = inv * inv * (inv * inner / tok_ref.shape[1])
     for step, ref in sources:
-        normed = tok_ref[:, slab(y, step)].astype(jnp.float32) * inv
+        tok = tok_ref[:, slab(y, step)].astype(jnp.float32)
         grad = ref[:, WIDE:].astype(jnp.float32)
-        grad_ref[:, slab(y, step)] = (inv * (grad - normed * inner)).astype(jnp.bfloat16)
+        grad_ref[:, slab(y, step)] = (inv * grad - tok * scale).astype(jnp.bfloat16)
 
 
 def local(tokens, kv_weight, kv_cotangent, fragment_index, anchor, momentum, replica_frag):
@@ -245,7 +244,7 @@
         compiler_params=params,
         cost_estimate=pl.CostEstimate(flops=2**21, bytes_accessed=3 * MIB, transcendentals=0),
         name="begin",
-    )(tokens, inv, own, gots[0])
+    )(tokens, own, gots[0])
     key_value, input_grad = pl.pallas_call(
         finish_kernel,
         out_shape=(

time: 87.7 us -> 87.7 us (level)
  transfers between devices with their start and end apart: 14 -> 14, of which waited for: 7 -> 7; matrix products, arithmetic and copies ran while one was open for 3% -> 3% of each run, Pallas kernels for 3% -> 2%
where the time goes in v6:
time: 87.7 us; the launch traced here: 87.1 us
  starting transfers between devices  64.1 us (73%)
  waiting for transfers between devices  10.6 us (12%)
  Pallas kernels  5.25 us (6%)
  local copies, waits for them, and re-layouts  3.16 us (4%)
  other arithmetic  2.42 us (3%)
  between operations  1.53 us (2%)
    ppermute x11, starting transfers between devices, send(): return lax.ppermute(x, 'fsdp', pairs)  46.2 us
    ppermute x3, starting transfers between devices, add_half(): lax.ppermute(drift, 'rep', [(r, r ^ bit) for r in range(replicas)])  17.9 us
    ppermute x11, waiting for transfers between devices, send(): return lax.ppermute(x, 'fsdp', pairs)  5.51 us
    ppermute x3, waiting for transfers between devices, add_half(): lax.ppermute(drift, 'rep', [(r, r ^ bit) for r in range(replicas)])  5.05 us
    unnamed x12, local copies, waits for them, and re-layouts  3.12 us
  transfers between devices with their start and end apart: 14, of which 7 were waited for; matrix products, arithmetic and copies ran while one was open for 3% of the time, Pallas kernels for 2%

profile of v6, /device:TPU:1, one launch (start us, length us, event | category | flops | bytes accessed | tf_op | source)
XLA Modules:
  0.0 87.1 jit_solution(8093800432351870713)
XLA Ops:
  0.6 0.0 copy-start
  0.6 9.8 %collective-permute-start = (bf16[64,1024]{1,0:T(8,128)(2,1)}, bf16[64,1024]{1,0:T(8,128)(2,1)S(1)}, u32[]{:S(2)}, u32[]{:S(2)}) collective-permute-start(bf16[64,1024]{1,0:T(8,128)(2,1)} %bitcast.8), channel_id=1, source_target_pairs={{0,4},{1,9},{2,6},{3,11},{4,0},{5,13},{6,2},{7,15},{8,12},{9,1},{1... | collective-permute-start | bytes 393224 | tf_op jit(solution)/shard_map/ppermute | solution.py:42
  10.4 0.0 copy-start.1
  10.4 1.2 %copy-done.1 = bf16[128,4096]{1,0:T(8,128)(2,1)S(1)} copy-done((bf16[128,4096]{1,0:T(8,128)(2,1)S(1)}, bf16[128,4096]{1,0:T(8,128)(2,1)}, u32[]{:S(2)}) %copy-start.1) | copy-done | bytes 1048600
  11.7 0.0 copy-start.3
  11.7 0.9 %copy-done.3 = bf16[128,1024]{1,0:T(8,128)(2,1)S(1)} copy-done((bf16[128,1024]{1,0:T(8,128)(2,1)S(1)}, bf16[128,1024]{1,0:T(8,128)(2,1)}, u32[]{:S(2)}) %copy-start.3) | copy-done | bytes 262168
  12.6 0.0 copy-start.4
  12.6 0.9 %copy-done.4 = bf16[1,64,1024]{2,1,0:T(8,128)(2,1)S(1)} copy-done((bf16[1,64,1024]{2,1,0:T(8,128)(2,1)S(1)}, bf16[1,64,1024]{2,1,0:T(8,128)(2,1)}, u32[]{:S(2)}) %copy-start.4) | copy-done | bytes 131096
  13.5 0.5 prepare.1
  14.0 3.2 %collective-permute-start.3 = (bf16[128,2048]{1,0:T(8,128)(2,1)S(1)}, bf16[128,2048]{1,0:T(8,128)(2,1)S(1)}, u32[]{:S(2)}, u32[]{:S(2)}) collective-permute-start(bf16[128,2048]{1,0:T(8,128)(2,1)S(1)} %get-tuple-element.49), channel_id=1, source_target_pairs={{0,16},{1,17},{2,18},{3,19},{4,20},{5,21},{6,22},{7,23},{8,24},{9,... | collective-permute-start | bytes 1572872 | tf_op jit(solution)/shard_map/ppermute | solution.py:42
  17.9 0.0 copy-done
  17.9 0.9 dynamic-slice_convert_fusion
  18.8 0.0 collective-permute-done
  18.8 4.9 %collective-permute-start.1 = (bf16[128,1024]{1,0:T(8,128)(2,1)S(1)}, bf16[128,1024]{1,0:T(8,128)(2,1)S(1)}, u32[]{:S(2)}, u32[]{:S(2)}) collective-permute-start(bf16[128,1024]{1,0:T(8,128)(2,1)S(1)} %constant_dynamic-update-slice_fusion), channel_id=1, source_target_pairs={{0,8},{1,5},{2,10},{3,7},{4,12},{5,1},{6,14},{7,3},{8,0},{9,13},{1... | collective-permute-start | bytes 786440 | tf_op jit(solution)/shard_map/ppermute | solution.py:42
  23.8 3.4 %collective-permute-start.7 = (bf16[128,2048]{1,0:T(8,128)(2,1)S(1)}, bf16[128,2048]{1,0:T(8,128)(2,1)S(1)}, u32[]{:S(2)}, u32[]{:S(2)}) collective-permute-start(bf16[128,2048]{1,0:T(8,128)(2,1)S(1)} %get-tuple-element.52), channel_id=1, source_target_pairs={{0,48},{1,49},{2,50},{3,51},{4,52},{5,53},{6,54},{7,55},{8,56},{9,... | collective-permute-start | bytes 1572872 | tf_op jit(solution)/shard_map/ppermute | solution.py:42
  27.1 3.1 %collective-permute-start.2 = (f32[4096]{0:T(1024)S(1)}, f32[4096]{0:T(1024)S(1)}, u32[]{:S(2)}, u32[]{:S(2)}) collective-permute-start(f32[4096]{0:T(1024)S(1)} %sub.6), channel_id=1, source_target_pairs={{0,128},{64,192},{128,0},{192,64},{256,384},{320,448},{384,256},{4... | collective-permute-start | bytes 49160 | tf_op jit(solution)/shard_map/ppermute | solution.py:181
  30.3 1.6 %collective-permute-done.2 = f32[4096]{0:T(1024)S(1)} collective-permute-done((f32[4096]{0:T(1024)S(1)}, f32[4096]{0:T(1024)S(1)}, u32[]{:S(2)}, u32[]{:S(2)}) %collective-permute-start.2) | collective-permute-done | bytes 16416 | tf_op jit(solution)/shard_map/ppermute | solution.py:181
  31.9 3.5 %collective-permute-start.6 = (bf16[128,2048]{1,0:T(8,128)(2,1)S(1)}, bf16[128,2048]{1,0:T(8,128)(2,1)S(1)}, u32[]{:S(2)}, u32[]{:S(2)}) collective-permute-start(bf16[128,2048]{1,0:T(8,128)(2,1)S(1)} %get-tuple-element.51), channel_id=1, source_target_pairs={{0,32},{1,33},{2,34},{3,35},{4,36},{5,37},{6,38},{7,39},{8,40},{9,... | collective-permute-start | bytes 1572872 | tf_op jit(solution)/shard_map/ppermute | solution.py:42
  35.4 0.3 collective-permute-done.1
  35.8 0.0 collective-permute-done.3.refs_1_
  35.8 3.2 %collective-permute-start.4 = (bf16[256,1024]{1,0:T(8,128)(2,1)S(1)}, bf16[256,1024]{1,0:T(8,128)(2,1)S(1)}, u32[]{:S(2)}, u32[]{:S(2)}) collective-permute-start(bf16[256,1024]{1,0:T(8,128)(2,1)S(1)} %constant_dynamic-update-slice_fusion.2.mine_ref), channel_id=1, source_target_pairs={{0,2},{1,3},{2,0},{3,1},{4,6},{5,7},{6,4},{7,5},{8,10},{9,11},{10,... | collective-permute-start | bytes 1572872 | tf_op jit(solution)/shard_map/ppermute | solution.py:42
  39.0 5.1 %collective-permute-start.5 = (bf16[256,1024]{1,0:T(8,128)(2,1)S(1)}, bf16[256,1024]{1,0:T(8,128)(2,1)S(1)}, u32[]{:S(2)}, u32[]{:S(2)}) collective-permute-start(bf16[256,1024]{1,0:T(8,128)(2,1)S(1)} %constant_dynamic-update-slice_fusion.2.mine_ref), channel_id=1, source_target_pairs={{0,1},{1,0},{2,3},{3,2},{4,5},{5,4},{6,7},{7,6},{8,9},{9,8},{10,11... | collective-permute-start | bytes 1572872 | tf_op jit(solution)/shard_map/ppermute | solution.py:42
  44.2 4.7 %collective-permute-start.8 = (f32[4096]{0:T(1024)S(1)}, f32[4096]{0:T(1024)S(1)}, u32[]{:S(2)}, u32[]{:S(2)}) collective-permute-start(f32[4096]{0:T(1024)S(1)} %add.23), channel_id=1, source_target_pairs={{0,256},{64,320},{128,384},{192,448},{256,0},{320,64},{384,128},{4... | collective-permute-start | bytes 49160 | tf_op jit(solution)/shard_map/ppermute | solution.py:181
  48.8 1.3 %collective-permute-done.8 = f32[4096]{0:T(1024)S(1)} collective-permute-done((f32[4096]{0:T(1024)S(1)}, f32[4096]{0:T(1024)S(1)}, u32[]{:S(2)}, u32[]{:S(2)}) %collective-permute-start.8) | collective-permute-done | bytes 16416 | tf_op jit(solution)/shard_map/ppermute | solution.py:181
  50.2 0.0 collective-permute-done.7.refs_3_
  50.2 0.0 collective-permute-done.6.refs_2_
  50.2 0.0 collective-permute-done.4.mine_ref
  50.2 0.0 collective-permute-done.5.sib_ref
  50.2 3.7 %collective-permute-start.9 = (bf16[256,1024]{1,0:T(8,128)(2,1)S(1)}, bf16[256,1024]{1,0:T(8,128)(2,1)S(1)}, u32[]{:S(2)}, u32[]{:S(2)}) collective-permute-start(bf16[256,1024]{1,0:T(8,128)(2,1)S(1)} %collective-permute-done.4.mine_ref), channel_id=1, source_target_pairs={{0,1},{1,0},{2,3},{3,2},{4,5},{5,4},{6,7},{7,6},{8,9},{9,8},{10,11... | collective-permute-start | bytes 1572872 | tf_op jit(solution)/shard_map/ppermute | solution.py:42
  53.9 1.4 %first_half.1 = (f32[512,1024]{1,0:T(8,128)S(1)}, f32[128,512]{1,0:T(8,128)S(1)}, bf16[128,512]{1,0:T(8,128)(2,1)S(1)}, bf16[128,512]{1,0:T(8,128)(2,1)S(1)}, bf16[128,512]{1,0:T(8,128)(2,1)S(1)}) custom-call(bf16[256,1024]{1,0:T(8,128)(2,1)S(1)} %constant_dynamic-update-slice_fusion.2.mine_ref, bf16[256,1024]{1,0:T(8,128)(2,1)S(1)} %collective-permute-done.5.sib_ref, ...), custom_call_target="tpu_custom_call" | custom-call | flops 1073741824 | bytes 8388608 | tf_op jit(solution)/shard_map/first_half/pallas_call | solution.py:212
  55.3 0.1 collective-permute-done.9.sib_ref
  55.4 0.0 copy-start.2
  55.4 1.4 %second_half.1 = (f32[128,2048]{1,0:T(8,128)S(1)}, bf16[128,2048]{1,0:T(8,128)(2,1)S(1)}, bf16[128,2048]{1,0:T(8,128)(2,1)S(1)}, bf16[128,2048]{1,0:T(8,128)(2,1)S(1)}) custom-call(bf16[256,1024]{1,0:T(8,128)(2,1)S(1)} %collective-permute-done.4.mine_ref, bf16[256,1024]{1,0:T(8,128)(2,1)S(1)} %collective-permute-done.9.sib_ref, ...), custom_call_target="tpu_custom_call" | custom-call | flops 1073741824 | bytes 8388608 | tf_op jit(solution)/shard_map/second_half/pallas_call | solution.py:224
  56.8 3.9 %collective-permute-start.10 = (bf16[128,2048]{1,0:T(8,128)(2,1)S(1)}, bf16[128,2048]{1,0:T(8,128)(2,1)S(1)}, u32[]{:S(2)}, u32[]{:S(2)}) collective-permute-start(bf16[128,2048]{1,0:T(8,128)(2,1)S(1)} %get-tuple-element.70), channel_id=1, source_target_pairs={{0,32},{1,33},{2,34},{3,35},{4,36},{5,37},{6,38},{7,39},{8,40},{9,... | collective-permute-start | bytes 1572872 | tf_op jit(solution)/shard_map/ppermute | solution.py:42
  60.7 3.6 %collective-permute-start.11 = (bf16[128,2048]{1,0:T(8,128)(2,1)S(1)}, bf16[128,2048]{1,0:T(8,128)(2,1)S(1)}, u32[]{:S(2)}, u32[]{:S(2)}) collective-permute-start(bf16[128,2048]{1,0:T(8,128)(2,1)S(1)} %get-tuple-element.73), channel_id=1, source_target_pairs={{0,48},{1,49},{2,50},{3,51},{4,52},{5,53},{6,54},{7,55},{8,56},{9,... | collective-permute-start | bytes 1572872 | tf_op jit(solution)/shard_map/ppermute | solution.py:42
  64.3 1.9 %collective-permute-start.12 = (bf16[128,2048]{1,0:T(8,128)(2,1)S(1)}, bf16[128,2048]{1,0:T(8,128)(2,1)S(1)}, u32[]{:S(2)}, u32[]{:S(2)}) collective-permute-start(bf16[128,2048]{1,0:T(8,128)(2,1)S(1)} %get-tuple-element.74), channel_id=1, source_target_pairs={{0,16},{1,17},{2,18},{3,19},{4,20},{5,21},{6,22},{7,23},{8,24},{9,... | collective-permute-start | bytes 1572872 | tf_op jit(solution)/shard_map/ppermute | solution.py:42
  66.2 10.2 %collective-permute-start.13 = (f32[4096]{0:T(1024)S(1)}, f32[4096]{0:T(1024)S(1)}, u32[]{:S(2)}, u32[]{:S(2)}) collective-permute-start(f32[4096]{0:T(1024)S(1)} %add.24), channel_id=1, source_target_pairs={{0,64},{64,0},{128,192},{192,128},{256,320},{320,256},{384,448},{4... | collective-permute-start | bytes 49160 | tf_op jit(solution)/shard_map/ppermute | solution.py:181
  76.4 0.9 %dynamic-slice_multiply_fusion = f32[1,4096]{1,0:T(1,128)S(1)} fusion(f32[8,4096]{1,0:T(8,128)} %param.12, s32[]{:T(128)S(6)} %select_n.7), kind=kLoop, calls=%fused_computation.1 | loop fusion | flops 4096 | bytes 32772 | tf_op jit(solution)/shard_map/mul | solution.py:236
  77.3 2.1 %collective-permute-done.13 = f32[4096]{0:T(1024)S(1)} collective-permute-done((f32[4096]{0:T(1024)S(1)}, f32[4096]{0:T(1024)S(1)}, u32[]{:S(2)}, u32[]{:S(2)}) %collective-permute-start.13) | collective-permute-done | bytes 16416 | tf_op jit(solution)/shard_map/ppermute | solution.py:181
  79.4 0.6 multiply_subtract_fusion
  80.0 0.0 collective-permute-done.10.across_ref.refs_0_
  80.0 0.0 copy-done.2
  80.0 0.2 begin.1
  80.3 3.9 %collective-permute-done.11.refs_1_ = bf16[128,2048]{1,0:T(8,128)(2,1)S(1)} collective-permute-done((bf16[128,2048]{1,0:T(8,128)(2,1)S(1)}, bf16[128,2048]{1,0:T(8,128)(2,1)S(1)}, u32[]{:S(2)}, u32[]{:S(2)}) %collective-permute-start.11) | collective-permute-done | bytes 524320 | tf_op jit(solution)/shard_map/ppermute | solution.py:42
  84.1 1.2 %collective-permute-done.12.refs_2_ = bf16[128,2048]{1,0:T(8,128)(2,1)S(1)} collective-permute-done((bf16[128,2048]{1,0:T(8,128)(2,1)S(1)}, bf16[128,2048]{1,0:T(8,128)(2,1)S(1)}, u32[]{:S(2)}, u32[]{:S(2)}) %collective-permute-start.12) | collective-permute-done | bytes 524320 | tf_op jit(solution)/shard_map/ppermute | solution.py:42
  85.3 1.7 %finish.1 = (bf16[128,1024]{1,0:T(8,128)(2,1)}, bf16[128,4096]{1,0:T(8,128)(2,1)}) custom-call(bf16[128,4096]{1,0:T(8,128)(2,1)S(1)} %copy-done.2, f32[128,1]{1,0:T(8,128)S(1)} %get-tuple-element.41.inv_ref, f32[128,1024]{1,0:T(8,128)S(1)} %get-tuple-element.71.kv_part_ref, f32[128,1]{1,0:T(8,128)S(1)} %get-tuple-element.72.inner_ref, ...), custom_call_target="tpu_custom_call" | custom-call | flops 4194304 | bytes 5242880 | tf_op jit(solution)/shard_map/finish/pallas_call | solution.py:248
  (8 shorter events, 0.1 us)
Async XLA Ops:
  0.6 17.3 %copy-start = (f32[8,4096]{1,0:T(8,128)S(1)}, f32[8,4096]{1,0:T(8,128)}, u32[]{:S(2)}) copy-start(f32[8,4096]{1,0:T(8,128)} %param.11) | copy-start | bytes 393220
  0.6 18.2 %collective-permute-start = (bf16[64,1024]{1,0:T(8,128)(2,1)}, bf16[64,1024]{1,0:T(8,128)(2,1)S(1)}, u32[]{:S(2)}, u32[]{:S(2)}) collective-permute-start(bf16[64,1024]{1,0:T(8,128)(2,1)} %bitcast.8), channel_id=1, source_target_pairs={{0,4},{1,9},{2,6},{3,11},{4,0},{5,13},{6,2},{7,15},{8,12},{9,1},{1... | collective-permute-start | bytes 393224 | tf_op jit(solution)/shard_map/ppermute | solution.py:42
  10.4 1.2 %copy-start.1 = (bf16[128,4096]{1,0:T(8,128)(2,1)S(1)}, bf16[128,4096]{1,0:T(8,128)(2,1)}, u32[]{:S(2)}) copy-start(bf16[128,4096]{1,0:T(8,128)(2,1)} %tok_ref.5) | copy-start | bytes 3145732
  11.7 0.9 %copy-start.3 = (bf16[128,1024]{1,0:T(8,128)(2,1)S(1)}, bf16[128,1024]{1,0:T(8,128)(2,1)}, u32[]{:S(2)}) copy-start(bf16[128,1024]{1,0:T(8,128)(2,1)} %cot_ref.1) | copy-start | bytes 786436
  12.6 0.9 %copy-start.4 = (bf16[1,64,1024]{2,1,0:T(8,128)(2,1)S(1)}, bf16[1,64,1024]{2,1,0:T(8,128)(2,1)}, u32[]{:S(2)}) copy-start(bf16[1,64,1024]{2,1,0:T(8,128)(2,1)} %param.8) | copy-start | bytes 393220
  14.0 21.7 %collective-permute-start.3 = (bf16[128,2048]{1,0:T(8,128)(2,1)S(1)}, bf16[128,2048]{1,0:T(8,128)(2,1)S(1)}, u32[]{:S(2)}, u32[]{:S(2)}) collective-permute-start(bf16[128,2048]{1,0:T(8,128)(2,1)S(1)} %get-tuple-element.49), channel_id=1, source_target_pairs={{0,16},{1,17},{2,18},{3,19},{4,20},{5,21},{6,22},{7,23},{8,24},{9,... | collective-permute-start | bytes 1572872 | tf_op jit(solution)/shard_map/ppermute | solution.py:42
  18.8 16.9 %collective-permute-start.1 = (bf16[128,1024]{1,0:T(8,128)(2,1)S(1)}, bf16[128,1024]{1,0:T(8,128)(2,1)S(1)}, u32[]{:S(2)}, u32[]{:S(2)}) collective-permute-start(bf16[128,1024]{1,0:T(8,128)(2,1)S(1)} %constant_dynamic-update-slice_fusion), channel_id=1, source_target_pairs={{0,8},{1,5},{2,10},{3,7},{4,12},{5,1},{6,14},{7,3},{8,0},{9,13},{1... | collective-permute-start | bytes 786440 | tf_op jit(solution)/shard_map/ppermute | solution.py:42
  23.8 26.4 %collective-permute-start.7 = (bf16[128,2048]{1,0:T(8,128)(2,1)S(1)}, bf16[128,2048]{1,0:T(8,128)(2,1)S(1)}, u32[]{:S(2)}, u32[]{:S(2)}) collective-permute-start(bf16[128,2048]{1,0:T(8,128)(2,1)S(1)} %get-tuple-element.52), channel_id=1, source_target_pairs={{0,48},{1,49},{2,50},{3,51},{4,52},{5,53},{6,54},{7,55},{8,56},{9,... | collective-permute-start | bytes 1572872 | tf_op jit(solution)/shard_map/ppermute | solution.py:42
  27.1 4.8 %collective-permute-start.2 = (f32[4096]{0:T(1024)S(1)}, f32[4096]{0:T(1024)S(1)}, u32[]{:S(2)}, u32[]{:S(2)}) collective-permute-start(f32[4096]{0:T(1024)S(1)} %sub.6), channel_id=1, source_target_pairs={{0,128},{64,192},{128,0},{192,64},{256,384},{320,448},{384,256},{4... | collective-permute-start | bytes 49160 | tf_op jit(solution)/shard_map/ppermute | solution.py:181
  31.9 18.3 %collective-permute-start.6 = (bf16[128,2048]{1,0:T(8,128)(2,1)S(1)}, bf16[128,2048]{1,0:T(8,128)(2,1)S(1)}, u32[]{:S(2)}, u32[]{:S(2)}) collective-permute-start(bf16[128,2048]{1,0:T(8,128)(2,1)S(1)} %get-tuple-element.51), channel_id=1, source_target_pairs={{0,32},{1,33},{2,34},{3,35},{4,36},{5,37},{6,38},{7,39},{8,40},{9,... | collective-permute-start | bytes 1572872 | tf_op jit(solution)/shard_map/ppermute | solution.py:42
  35.8 14.4 %collective-permute-start.4 = (bf16[256,1024]{1,0:T(8,128)(2,1)S(1)}, bf16[256,1024]{1,0:T(8,128)(2,1)S(1)}, u32[]{:S(2)}, u32[]{:S(2)}) collective-permute-start(bf16[256,1024]{1,0:T(8,128)(2,1)S(1)} %constant_dynamic-update-slice_fusion.2.mine_ref), channel_id=1, source_target_pairs={{0,2},{1,3},{2,0},{3,1},{4,6},{5,7},{6,4},{7,5},{8,10},{9,11},{10,... | collective-permute-start | bytes 1572872 | tf_op jit(solution)/shard_map/ppermute | solution.py:42
  39.0 11.1 %collective-permute-start.5 = (bf16[256,1024]{1,0:T(8,128)(2,1)S(1)}, bf16[256,1024]{1,0:T(8,128)(2,1)S(1)}, u32[]{:S(2)}, u32[]{:S(2)}) collective-permute-start(bf16[256,1024]{1,0:T(8,128)(2,1)S(1)} %constant_dynamic-update-slice_fusion.2.mine_ref), channel_id=1, source_target_pairs={{0,1},{1,0},{2,3},{3,2},{4,5},{5,4},{6,7},{7,6},{8,9},{9,8},{10,11... | collective-permute-start | bytes 1572872 | tf_op jit(solution)/shard_map/ppermute | solution.py:42
  44.2 6.0 %collective-permute-start.8 = (f32[4096]{0:T(1024)S(1)}, f32[4096]{0:T(1024)S(1)}, u32[]{:S(2)}, u32[]{:S(2)}) collective-permute-start(f32[4096]{0:T(1024)S(1)} %add.23), channel_id=1, source_target_pairs={{0,256},{64,320},{128,384},{192,448},{256,0},{320,64},{384,128},{4... | collective-permute-start | bytes 49160 | tf_op jit(solution)/shard_map/ppermute | solution.py:181
  50.2 5.2 %collective-permute-start.9 = (bf16[256,1024]{1,0:T(8,128)(2,1)S(1)}, bf16[256,1024]{1,0:T(8,128)(2,1)S(1)}, u32[]{:S(2)}, u32[]{:S(2)}) collective-permute-start(bf16[256,1024]{1,0:T(8,128)(2,1)S(1)} %collective-permute-done.4.mine_ref), channel_id=1, source_target_pairs={{0,1},{1,0},{2,3},{3,2},{4,5},{5,4},{6,7},{7,6},{8,9},{9,8},{10,11... | collective-permute-start | bytes 1572872 | tf_op jit(solution)/shard_map/ppermute | solution.py:42
  55.4 24.6 %copy-start.2 = (bf16[128,4096]{1,0:T(8,128)(2,1)S(1)}, bf16[128,4096]{1,0:T(8,128)(2,1)}, u32[]{:S(2)}) copy-start(bf16[128,4096]{1,0:T(8,128)(2,1)} %tok_ref.5) | copy-start | bytes 3145732
  56.8 23.2 %collective-permute-start.10 = (bf16[128,2048]{1,0:T(8,128)(2,1)S(1)}, bf16[128,2048]{1,0:T(8,128)(2,1)S(1)}, u32[]{:S(2)}, u32[]{:S(2)}) collective-permute-start(bf16[128,2048]{1,0:T(8,128)(2,1)S(1)} %get-tuple-element.70), channel_id=1, source_target_pairs={{0,32},{1,33},{2,34},{3,35},{4,36},{5,37},{6,38},{7,39},{8,40},{9,... | collective-permute-start | bytes 1572872 | tf_op jit(solution)/shard_map/ppermute | solution.py:42
  60.7 23.4 %collective-permute-start.11 = (bf16[128,2048]{1,0:T(8,128)(2,1)S(1)}, bf16[128,2048]{1,0:T(8,128)(2,1)S(1)}, u32[]{:S(2)}, u32[]{:S(2)}) collective-permute-start(bf16[128,2048]{1,0:T(8,128)(2,1)S(1)} %get-tuple-element.73), channel_id=1, source_target_pairs={{0,48},{1,49},{2,50},{3,51},{4,52},{5,53},{6,54},{7,55},{8,56},{9,... | collective-permute-start | bytes 1572872 | tf_op jit(solution)/shard_map/ppermute | solution.py:42
  64.3 21.0 %collective-permute-start.12 = (bf16[128,2048]{1,0:T(8,128)(2,1)S(1)}, bf16[128,2048]{1,0:T(8,128)(2,1)S(1)}, u32[]{:S(2)}, u32[]{:S(2)}) collective-permute-start(bf16[128,2048]{1,0:T(8,128)(2,1)S(1)} %get-tuple-element.74), channel_id=1, source_target_pairs={{0,16},{1,17},{2,18},{3,19},{4,20},{5,21},{6,22},{7,23},{8,24},{9,... | collective-permute-start | bytes 1572872 | tf_op jit(solution)/shard_map/ppermute | solution.py:42
  66.2 13.2 %collective-permute-start.13 = (f32[4096]{0:T(1024)S(1)}, f32[4096]{0:T(1024)S(1)}, u32[]{:S(2)}, u32[]{:S(2)}) collective-permute-start(f32[4096]{0:T(1024)S(1)} %add.24), channel_id=1, source_target_pairs={{0,64},{64,0},{128,192},{192,128},{256,320},{320,256},{384,448},{4... | collective-permute-start | bytes 49160 | tf_op jit(solution)/shard_map/ppermute | solution.py:181
